TPU v7x, 128 devices: a whole 4x4x4 slice. The times are simulated.
128 devices in a mesh: tile: 32 (over y, z, x_lo), therm: 4 (over x_hi, core).
Axes of the slice: x: 4 (x_hi: 2, x_lo: 2; x = x_hi * 2 + x_lo), y: 4, z: 4, core: 2. Of those that a mesh axis runs over, the one named last changes fastest.
Arguments:
- sink_current: float32 [12, 1024, 1024], P('therm', 'tile'), may hold values from 0 to 60, as said below
- metal_category: int32 [12, 1024, 1024], P('therm', 'tile'), may hold values from 0 to 7
- upward_link_flag: int32 [12, 1024, 1024], P('therm', 'tile'), may hold values 0 or 1
- supply_contact_flag: int32 [12, 1024, 1024], P('therm', 'tile'), may hold values 0 or 1
- baseline_admittance: float32 [8], replicated, may hold values from 0.3 to 3
- beginning_warmth: float32 [64, 1024, 1024], P('therm', 'tile'), may hold values from 0.5 to 4
- cell_diffusivity: float32 [64, 1024, 1024], P('therm', 'tile'), may hold values from 0.5 to 2
- dissipation_split: float32 [64, 12], replicated, may hold values from 0.1 to 1
- probe_weighting: float32 [12, 64], replicated, may hold values from 0.005 to 0.05
Outputs:
- voltage_loss: float32 [12, 1024, 1024], P('therm', 'tile')
- final_warmth: float32 [64, 1024, 1024], P('therm', 'tile')
- updated_admittance: float32 [12, 1024, 1024], P('therm', 'tile')
Inputs may be any that keep to these rules, and one draw needn't show every extreme that they name: `sink_current`: positive load currents.
All inputs are finite; a program needn't handle non-finite values. No bound on the sum of `upward_link_flag` or of `supply_contact_flag` on one device may be relied on, other than what follows from the above.
Results may differ from a plain program's by a relative error of at most 0.0003.
Values sent between devices are 32-bit elements; how exact they have to be, the bound alone decides.
No kernel may reach another device: no remote copies, remote signals or barrier semaphores. Data moves between devices by JAX's collectives and lax.ppermute only.
A program may use at most 192 MiB of HBM per device.

v0:
```python
import jax
import jax.numpy as jnp
from jax import lax
from jax.sharding import PartitionSpec as P

ITERS = 3
SWEEPS = 4


shunt_level = 0.05
pad_conductance = 4.0
via_conductance = 2.0
thermal_slope = 0.2
sink_level = 0.1


def extended(value, sides, width):
    for axis, dim in sides:
        devices, length = (lax.axis_size(axis), value.shape[dim])
        up = [(i, (i + 1) % devices) for i in range(devices - 1)]
        down = [(j, i) for i, j in up]
        last = lax.slice_in_dim(value, length - width, length, axis=dim)
        initial = lax.slice_in_dim(value, 0, width, axis=dim)
        before = lax.ppermute(last, axis, up)
        after = lax.ppermute(initial, axis, down)
        value = jnp.concatenate([before, value, after], axis=dim)
    return value


def harmonic(first, second):
    return first * second / (first + second)


def layer_rim(stacked):
    return extended(stacked, (("tile", 2), ("therm", 1)), 1)


def block_fringe(stacked):
    return extended(stacked, (("tile", 2), ("therm", 1)), 1)


def class_table(baseline_admittance, metal_category):
    table = jnp.zeros(metal_category.shape, jnp.float32)
    for number in range(baseline_admittance.shape[0]):
        table = table + jnp.where(metal_category == number, baseline_admittance[number], 0.0)
    return table


def ohmic_warming(probe_weighting, field, owned_strata, stratum_shift):
    present_stratum = field.shape[0]
    weights = lax.dynamic_slice(
        probe_weighting,
        (0, stratum_shift),
        (owned_strata * lax.axis_size("therm"), present_stratum),
    )
    return lax.psum_scatter(
        jnp.einsum("lz,zxy->lxy", weights, field, precision=lax.Precision.HIGHEST),
        "therm",
        scatter_dimension=0,
        tiled=True,
    )


def contact_stripes(field):
    return jnp.pad(field, ((0, 0), (0, 0), (1, 1)))


def squares(residual):
    return lax.psum(jnp.sum(residual * residual), ("tile", "therm"))


def per_device(
    sink_current,
    metal_category,
    upward_link_flag,
    supply_contact_flag,
    baseline_admittance,
    beginning_warmth,
    cell_diffusivity,
    dissipation_split,
    probe_weighting,
):
    owned_strata = sink_current.shape[0]
    present_stratum = beginning_warmth.shape[0]
    stratum_shift = lax.axis_index("therm") * present_stratum
    table = class_table(baseline_admittance, metal_category)
    power_density = ohmic_warming(probe_weighting, beginning_warmth, owned_strata, stratum_shift)
    lateral = table / (1.0 + thermal_slope * power_density)
    vertical = (
        upward_link_flag.astype(jnp.float32)
        * via_conductance
        / (1.0 + thermal_slope * power_density)
    )
    grounded = shunt_level + supply_contact_flag.astype(jnp.float32) * pad_conductance
    rimmed = layer_rim(jnp.stack([lateral, vertical]))
    lateral_rim = rimmed[0]
    below = rimmed[1][:-2, 1:-1, :]
    row_edges = harmonic(lateral_rim[1:-1, :-1, :], lateral_rim[1:-1, 1:, :])
    lateral_cols = contact_stripes(lateral)
    col_edges = harmonic(lateral_cols[..., :-1], lateral_cols[..., 1:])
    diagonal = (
        grounded
        + vertical
        + below
        + row_edges[:, :-1]
        + row_edges[:, 1:]
        + col_edges[..., :-1]
        + col_edges[..., 1:]
    )

    def surround(field):
        return contact_stripes(layer_rim(field[None])[0])

    voltage_loss = jnp.zeros_like(sink_current)
    residual = sink_current
    direction = sink_current
    norm_now = squares(residual)
    for step in range(ITERS):
        operate_beside_all = surround(direction)
        result = (
            diagonal * direction
            - row_edges[:, :-1] * operate_beside_all[1:-1, :-2, 1:-1]
            - row_edges[:, 1:] * operate_beside_all[1:-1, 2:, 1:-1]
        )
        result = (
            result
            - col_edges[..., :-1] * operate_beside_all[1:-1, 1:-1, :-2]
            - col_edges[..., 1:] * operate_beside_all[1:-1, 1:-1, 2:]
        )
        image = (
            result
            - vertical * operate_beside_all[2:, 1:-1, 1:-1]
            - below * operate_beside_all[:-2, 1:-1, 1:-1]
        )
        alpha = norm_now / lax.psum(jnp.sum(direction * image), ("tile", "therm"))
        voltage_loss = voltage_loss + alpha * direction
        residual = residual - alpha * image
        norm_next = squares(residual)
        direction = residual + norm_next / norm_now * direction
        norm_now = norm_next
    beside_all = surround(voltage_loss)
    pairs = [
        (row_edges[:, :-1], beside_all[1:-1, :-2, 1:-1]),
        (row_edges[:, 1:], beside_all[1:-1, 2:, 1:-1]),
        (col_edges[..., :-1], beside_all[1:-1, 1:-1, :-2]),
        (col_edges[..., 1:], beside_all[1:-1, 1:-1, 2:]),
        (vertical, beside_all[2:, 1:-1, 1:-1]),
        (below, beside_all[:-2, 1:-1, 1:-1]),
    ]
    edge_power = jnp.zeros_like(voltage_loss)
    for edge, other in pairs:
        edge_power = edge_power + edge * (voltage_loss - other) * (voltage_loss - other)
    power = grounded * voltage_loss * voltage_loss + 0.5 * edge_power
    piece = lax.all_gather(power, "therm", axis=0, tiled=True)
    weights = lax.dynamic_slice(
        dissipation_split, (stratum_shift, 0), (present_stratum, piece.shape[0])
    )
    source = jnp.einsum("zl,lxy->zxy", weights, piece, precision=lax.Precision.HIGHEST)
    krim = block_fringe(cell_diffusivity[None])[0]
    depth_edges = harmonic(krim[:-1, 1:-1, :], krim[1:, 1:-1, :])
    row_heat = harmonic(krim[1:-1, :-1, :], krim[1:-1, 1:, :])
    kcols = contact_stripes(cell_diffusivity)
    col_heat = harmonic(kcols[..., :-1], kcols[..., 1:])
    overall_total = (
        sink_level
        + depth_edges[:-1]
        + depth_edges[1:]
        + row_heat[:, :-1]
        + row_heat[:, 1:]
        + col_heat[..., :-1]
        + col_heat[..., 1:]
    )
    final_warmth = beginning_warmth
    for sweep in range(SWEEPS):
        warmth_fringe = contact_stripes(block_fringe(final_warmth[None])[0])
        inward_current_flow = (
            source
            + depth_edges[:-1] * warmth_fringe[:-2, 1:-1, 1:-1]
            + depth_edges[1:] * warmth_fringe[2:, 1:-1, 1:-1]
        )
        inward_current_flow = (
            inward_current_flow
            + row_heat[:, :-1] * warmth_fringe[1:-1, :-2, 1:-1]
            + row_heat[:, 1:] * warmth_fringe[1:-1, 2:, 1:-1]
        )
        inward_current_flow = (
            inward_current_flow
            + col_heat[..., :-1] * warmth_fringe[1:-1, 1:-1, :-2]
            + col_heat[..., 1:] * warmth_fringe[1:-1, 1:-1, 2:]
        )
        final_warmth = inward_current_flow / overall_total
    leftover_energy = ohmic_warming(probe_weighting, final_warmth, owned_strata, stratum_shift)
    updated_admittance = table / (1.0 + thermal_slope * leftover_energy)
    return (voltage_loss, final_warmth, updated_admittance)


def solution(mesh):
    return jax.shard_map(
        per_device,
        mesh=mesh,
        in_specs=(
            P("therm", "tile", None),
            P("therm", "tile", None),
            P("therm", "tile", None),
            P("therm", "tile", None),
            P(),
            P("therm", "tile", None),
            P("therm", "tile", None),
            P(),
            P(),
        ),
        out_specs=(P("therm", "tile", None), P("therm", "tile", None), P("therm", "tile", None)),
        check_vma=False,
    )
```

profile of v0, /device:TPU:25, one launch (start us, length us, event | category | flops | bytes accessed | tf_op | source)
XLA Modules:
  0.0 685.9 jit_solution(1718712626072286952)
XLA Ops:
  7.9 4.4 fusion.41
  14.5 3.1 collective-permute-start.4
  17.6 5.6 collective-permute-start.5
  23.9 27.8 %reduce-scatter.3.cloned.1.call-done = f32[3,32,1024]{2,1,0:T(8,128)} async-done(((f32[12,32,1024]{2,1,0:T(8,128)}), f32[3,32,1024]{2,1,0:T(8,128)}) %reduce-scatter.3.cloned.1.call-update) | async-done | bytes 393232 | tf_op jit(solution)/shard_map/reduce_scatter | solution.py:56
  51.7 6.6 fusion.78
  60.5 6.1 collective-permute-start.1
  66.7 3.3 collective-permute-start.6
  72.0 5.1 collective-permute-start.2
  81.2 5.9 collective-permute-done.3
  89.7 62.1 %all-reduce.10 = (f32[]{:T(128)}, f32[]{:T(128)}) all-reduce(f32[]{:T(128)} %get-tuple-element.10, f32[]{:T(128)} %get-tuple-element.9), channel_id=1, replica_groups=mesh['tile'=32,'therm'=4] {'tile','therm'}, use_global_device_ids=true, to_apply=%region_1.2 | all-reduce | flops 2 | bytes 16 | tf_op jit(solution)/shard_map/psum | solution.py:69
  154.5 64.1 %psum.44 = f32[]{:T(128)} all-reduce(f32[]{:T(128)} %get-tuple-element.15), channel_id=1, replica_groups=mesh['tile'=32,'therm'=4] {'tile','therm'}, use_global_device_ids=true, to_apply=%region_6.7 | all-reduce | flops 1 | bytes 8 | tf_op jit(solution)/shard_map/psum | solution.py:69
  222.9 6.4 collective-permute-start.9
  230.2 4.8 collective-permute-start.10
  237.2 5.9 collective-permute-done.11
  245.2 65.1 %psum.45 = f32[]{:T(128)} all-reduce(f32[]{:T(128)} %get-tuple-element.13), channel_id=1, replica_groups=mesh['tile'=32,'therm'=4] {'tile','therm'}, use_global_device_ids=true, to_apply=%region_8.9 | all-reduce | flops 1 | bytes 8 | tf_op jit(solution)/shard_map/psum | solution.py:135
  313.5 63.0 %psum.46 = f32[]{:T(128)} all-reduce(f32[]{:T(128)} %multiply_reduce_fusion), channel_id=1, replica_groups=mesh['tile'=32,'therm'=4] {'tile','therm'}, use_global_device_ids=true, to_apply=%region_10.11 | all-reduce | flops 1 | bytes 8 | tf_op jit(solution)/shard_map/psum | solution.py:69
  378.9 2.7 collective-permute-start.12
  381.6 5.6 collective-permute-start.13
  388.1 4.4 collective-permute-start.14
  394.7 5.9 collective-permute-done.15
  403.0 63.9 %psum.47 = f32[]{:T(128)} all-reduce(f32[]{:T(128)} %fusion.77), channel_id=1, replica_groups=mesh['tile'=32,'therm'=4] {'tile','therm'}, use_global_device_ids=true, to_apply=%region_12.13 | all-reduce | flops 1 | bytes 8 | tf_op jit(solution)/shard_map/psum | solution.py:135
  468.3 3.7 collective-permute-start.16
  472.0 4.7 collective-permute-start.17
  477.6 5.4 collective-permute-start.18
  486.3 5.0 collective-permute-done.19
  495.9 6.4 collective-permute-start.21
  502.3 2.9 copy.53
  507.1 6.4 collective-permute-start.25
  513.8 3.0 collective-permute-start.22
  521.2 5.1 collective-permute-start.26
  529.0 5.2 collective-permute-done.27
  539.4 4.2 fusion.39
  543.6 12.2 %fusion.4 = f32[1,16,32,1024]{3,1,2,0:T(8,128)S(1)} fusion(f32[18,34,1024]{2,0,1:T(8,128)} %maximum_bitcast_fusion.1, f32[16,32,1024]{2,0,1:T(8,128)S(1)} %fusion.39, f32[16,32,1025]{2,0,1:T(8,128)S(1)} %copy-done.1, f32[16,33,1024]{2,0,1:T(8,128)S(1)} %add_divide_fusion.2, f32[17,32,1024]{2,0,1:T(8,128)} %add_divide_fusion), kind=kLoop, calls=%fused_computation.20 | loop fusion | flops 9961472 | bytes 28508160 | tf_op jit(solution)/shard_map/broadcast_in_dim | solution.py:175
  557.8 6.4 collective-permute-start.29
  565.7 2.9 collective-permute-start.30
  570.9 5.9 collective-permute-done.31
  577.5 4.0 fusion.10
  583.5 6.4 collective-permute-start.33
  591.4 3.2 collective-permute-start.34
  596.8 5.7 collective-permute-done.35
  603.2 4.0 fusion.16
  609.2 6.4 collective-permute-start.37
  617.1 3.2 collective-permute-start.38
  622.4 5.9 collective-permute-done.39
  629.0 4.0 fusion.21
  637.0 4.2 copy.44
  641.2 30.7 %reduce-scatter.5.cloned.1.call-done = f32[3,32,1024]{2,1,0:T(8,128)} async-done(((f32[12,32,1024]{2,1,0:T(8,128)}), f32[3,32,1024]{2,1,0:T(8,128)}) %reduce-scatter.5.cloned.1.call-update) | async-done | bytes 393232 | tf_op jit(solution)/shard_map/reduce_scatter | solution.py:56
  671.9 7.3 %add_divide_fusion.5 = f32[3,32,1024]{2,1,0:T(8,128)} fusion(f32[3,32,1024]{2,1,0:T(8,128)} %reduce-scatter.5.cloned.1.call-done, f32[]{:T(128)} %bitcast.8, s32[3,32,1024]{2,1,0:T(8,128)S(1)} %copy-done.11, f32[]{:T(128)} %bitcast.7, f32[]{:T(128)} %bitcast.6, f32[]{:T(128)} %bitcast.5, f32[]{:T(128)} %bitcast.4, f32[]{:T(128)} %bitcast.3, f32[]{:T(128)} %bitcast.2, ...), kind=kLoop, calls=%fused_computation.151 | loop fusion | flops 2555904 | bytes 1179680 | tf_op jit(solution)/shard_map/div | solution.py:193
  (136 shorter events, 78.4 us)
Async XLA Ops:
  7.2 44.5 %reduce-scatter.3.cloned.1.call-start = ((), (), s32[]{:S(2)}) async-start(), calls=%async_computation.2 | async-start | bytes 1966080 | tf_op jit(solution)/shard_map/reduce_scatter | solution.py:56
  12.3 39.4 %copy-start.10 = (s32[3,32,1024]{2,1,0:T(8,128)S(1)}, s32[3,32,1024]{2,1,0:T(8,128)}, u32[]{:S(2)}) copy-start(s32[3,32,1024]{2,1,0:T(8,128)} %param.10) | copy-start | bytes 1179652
  12.3 39.4 %copy-start.12 = (s32[3,32,1024]{2,1,0:T(8,128)S(1)}, s32[3,32,1024]{2,1,0:T(8,128)}, u32[]{:S(2)}) copy-start(s32[3,32,1024]{2,1,0:T(8,128)} %param.11) | copy-start | bytes 1179652
  14.4 525.0 %all-gather.2.cloned.1.call-start = ((), (), s32[]{:S(2)}) async-start(), calls=%async_computation.3 | async-start | bytes 1966080 | tf_op jit(solution)/shard_map/all_gather | solution.py:154
  14.5 52.1 %collective-permute-start.4 = (f32[1,3,1,1024]{3,2,1,0:T(1,128)S(1)}, f32[1,3,1,1024]{3,2,1,0:T(1,128)S(1)}, u32[]{:S(2)}, u32[]{:S(2)}) collective-permute-start(f32[1,3,1,1024]{3,2,1,0:T(1,128)S(1)} %get-tuple-element.62), channel_id=1, source_target_pairs={{0,4},{4,8},{8,12},{12,16},{16,20},{20,24},{24,28},{28,32},{32,36}... | collective-permute-start | bytes 36872 | tf_op jit(solution)/shard_map/ppermute | solution.py:24
  17.6 49.0 %collective-permute-start.5 = (f32[1,3,1,1024]{3,2,1,0:T(1,128)S(1)}, f32[1,3,1,1024]{3,2,1,0:T(1,128)S(1)}, u32[]{:S(2)}, u32[]{:S(2)}) collective-permute-start(f32[1,3,1,1024]{3,2,1,0:T(1,128)S(1)} %get-tuple-element.63), channel_id=1, source_target_pairs={{4,0},{8,4},{12,8},{16,12},{20,16},{24,20},{28,24},{32,28},{36,32}... | collective-permute-start | bytes 36872 | tf_op jit(solution)/shard_map/ppermute | solution.py:25
  58.3 13.6 %collective-permute-start = (f32[2,3,1,1024]{3,2,1,0:T(1,128)S(1)}, f32[2,3,1,1024]{3,2,1,0:T(1,128)S(1)}, u32[]{:S(2)}, u32[]{:S(2)}) collective-permute-start(f32[2,3,1,1024]{3,2,1,0:T(1,128)S(1)} %get-tuple-element.44), channel_id=1, source_target_pairs={{0,4},{4,8},{8,12},{12,16},{16,20},{20,24},{24,28},{28,32},{32,36}... | collective-permute-start | bytes 73736 | tf_op jit(solution)/shard_map/ppermute | solution.py:24
  60.5 11.4 %collective-permute-start.1 = (f32[2,3,1,1024]{3,2,1,0:T(1,128)S(1)}, f32[2,3,1,1024]{3,2,1,0:T(1,128)S(1)}, u32[]{:S(2)}, u32[]{:S(2)}) collective-permute-start(f32[2,3,1,1024]{3,2,1,0:T(1,128)S(1)} %get-tuple-element.45), channel_id=1, source_target_pairs={{4,0},{8,4},{12,8},{16,12},{20,16},{24,20},{28,24},{32,28},{36,32}... | collective-permute-start | bytes 73736 | tf_op jit(solution)/shard_map/ppermute | solution.py:25
  66.7 12.4 %collective-permute-start.6 = (f32[1,1,34,1024]{3,2,1,0:T(8,128)S(1)}, f32[1,1,34,1024]{3,2,1,0:T(8,128)S(1)}, u32[]{:S(2)}, u32[]{:S(2)}) collective-permute-start(f32[1,1,34,1024]{3,2,1,0:T(8,128)S(1)} %get-tuple-element.52), channel_id=1, source_target_pairs={{0,1},{1,2},{2,3},{4,5},{5,6},{6,7},{8,9},{9,10},{10,11},{12,13},{... | collective-permute-start | bytes 417800 | tf_op jit(solution)/shard_map/ppermute | solution.py:24
  70.0 9.1 %collective-permute-start.7 = (f32[1,1,34,1024]{3,2,1,0:T(8,128)S(1)}, f32[1,1,34,1024]{3,2,1,0:T(8,128)S(1)}, u32[]{:S(2)}, u32[]{:S(2)}) collective-permute-start(f32[1,1,34,1024]{3,2,1,0:T(8,128)S(1)} %get-tuple-element.53), channel_id=1, source_target_pairs={{1,0},{2,1},{3,2},{5,4},{6,5},{7,6},{9,8},{10,9},{11,10},{13,12},{... | collective-permute-start | bytes 417800 | tf_op jit(solution)/shard_map/ppermute | solution.py:25
  72.0 9.2 %collective-permute-start.2 = (f32[2,1,34,1024]{3,2,1,0:T(8,128)S(1)}, f32[2,1,34,1024]{3,2,1,0:T(8,128)S(1)}, u32[]{:S(2)}, u32[]{:S(2)}) collective-permute-start(f32[2,1,34,1024]{3,2,1,0:T(8,128)S(1)} %get-tuple-element.42), channel_id=1, source_target_pairs={{0,1},{1,2},{2,3},{4,5},{5,6},{6,7},{8,9},{9,10},{10,11},{12,13},{... | collective-permute-start | bytes 835592 | tf_op jit(solution)/shard_map/ppermute | solution.py:24
  77.2 9.9 %collective-permute-start.3 = (f32[2,1,34,1024]{3,2,1,0:T(8,128)S(1)}, f32[2,1,34,1024]{3,2,1,0:T(8,128)S(1)}, u32[]{:S(2)}, u32[]{:S(2)}) collective-permute-start(f32[2,1,34,1024]{3,2,1,0:T(8,128)S(1)} %get-tuple-element.43), channel_id=1, source_target_pairs={{1,0},{2,1},{3,2},{5,4},{6,5},{7,6},{9,8},{10,9},{11,10},{13,12},{... | collective-permute-start | bytes 835592 | tf_op jit(solution)/shard_map/ppermute | solution.py:25
  87.5 313.2 %copy-start.5 = (f32[5,34,1024]{2,1,0:T(8,128)}, f32[5,34,1024]{2,1,0:T(8,128)S(1)}, u32[]{:S(2)}) copy-start(f32[5,34,1024]{2,1,0:T(8,128)S(1)} %get-tuple-element.40) | copy-start | bytes 2088964
  221.0 8.3 %collective-permute-start.8 = (f32[1,3,1,1024]{3,2,1,0:T(1,128)S(1)}, f32[1,3,1,1024]{3,2,1,0:T(1,128)S(1)}, u32[]{:S(2)}, u32[]{:S(2)}) collective-permute-start(f32[1,3,1,1024]{3,2,1,0:T(1,128)S(1)} %get-tuple-element.58), channel_id=1, source_target_pairs={{0,4},{4,8},{8,12},{12,16},{16,20},{20,24},{24,28},{28,32},{32,36}... | collective-permute-start | bytes 36872 | tf_op jit(solution)/shard_map/ppermute | solution.py:24
  222.9 7.2 %collective-permute-start.9 = (f32[1,3,1,1024]{3,2,1,0:T(1,128)S(1)}, f32[1,3,1,1024]{3,2,1,0:T(1,128)S(1)}, u32[]{:S(2)}, u32[]{:S(2)}) collective-permute-start(f32[1,3,1,1024]{3,2,1,0:T(1,128)S(1)} %get-tuple-element.59), channel_id=1, source_target_pairs={{4,0},{8,4},{12,8},{16,12},{20,16},{24,20},{28,24},{32,28},{36,32}... | collective-permute-start | bytes 36872 | tf_op jit(solution)/shard_map/ppermute | solution.py:25
  230.2 7.0 %collective-permute-start.10 = (f32[1,1,34,1024]{3,2,1,0:T(8,128)S(1)}, f32[1,1,34,1024]{3,2,1,0:T(8,128)S(1)}, u32[]{:S(2)}, u32[]{:S(2)}) collective-permute-start(f32[1,1,34,1024]{3,2,1,0:T(8,128)S(1)} %get-tuple-element.50), channel_id=1, source_target_pairs={{0,1},{1,2},{2,3},{4,5},{5,6},{6,7},{8,9},{9,10},{10,11},{12,13},{... | collective-permute-start | bytes 417800 | tf_op jit(solution)/shard_map/ppermute | solution.py:24
  235.0 8.1 %collective-permute-start.11 = (f32[1,1,34,1024]{3,2,1,0:T(8,128)S(1)}, f32[1,1,34,1024]{3,2,1,0:T(8,128)S(1)}, u32[]{:S(2)}, u32[]{:S(2)}) collective-permute-start(f32[1,1,34,1024]{3,2,1,0:T(8,128)S(1)} %get-tuple-element.51), channel_id=1, source_target_pairs={{1,0},{2,1},{3,2},{5,4},{6,5},{7,6},{9,8},{10,9},{11,10},{13,12},{... | collective-permute-start | bytes 417800 | tf_op jit(solution)/shard_map/ppermute | solution.py:25
  378.9 8.3 %collective-permute-start.12 = (f32[1,3,1,1024]{3,2,1,0:T(1,128)S(1)}, f32[1,3,1,1024]{3,2,1,0:T(1,128)S(1)}, u32[]{:S(2)}, u32[]{:S(2)}) collective-permute-start(f32[1,3,1,1024]{3,2,1,0:T(1,128)S(1)} %get-tuple-element.56), channel_id=1, source_target_pairs={{0,4},{4,8},{8,12},{12,16},{16,20},{20,24},{24,28},{28,32},{32,36}... | collective-permute-start | bytes 36872 | tf_op jit(solution)/shard_map/ppermute | solution.py:24
  381.6 6.4 collective-permute-start.13
  388.1 6.6 collective-permute-start.14
  392.4 8.1 %collective-permute-start.15 = (f32[1,1,34,1024]{3,2,1,0:T(8,128)S(1)}, f32[1,1,34,1024]{3,2,1,0:T(8,128)S(1)}, u32[]{:S(2)}, u32[]{:S(2)}) collective-permute-start(f32[1,1,34,1024]{3,2,1,0:T(8,128)S(1)} %get-tuple-element.49), channel_id=1, source_target_pairs={{1,0},{2,1},{3,2},{5,4},{6,5},{7,6},{9,8},{10,9},{11,10},{13,12},{... | collective-permute-start | bytes 417800 | tf_op jit(solution)/shard_map/ppermute | solution.py:25
  468.3 23.1 %copy-start.6 = (f32[3,32,1024]{2,1,0:T(8,128)}, f32[3,32,1024]{2,1,0:T(8,128)S(1)}, u32[]{:S(2)}) copy-start(f32[3,32,1024]{2,1,0:T(8,128)S(1)} %multiply_add_fusion) | copy-start | bytes 1179652
  468.3 8.4 %collective-permute-start.16 = (f32[1,3,1,1024]{3,2,1,0:T(1,128)S(1)}, f32[1,3,1,1024]{3,2,1,0:T(1,128)S(1)}, u32[]{:S(2)}, u32[]{:S(2)}) collective-permute-start(f32[1,3,1,1024]{3,2,1,0:T(1,128)S(1)} %get-tuple-element.54), channel_id=1, source_target_pairs={{0,4},{4,8},{8,12},{12,16},{16,20},{20,24},{24,28},{28,32},{32,36}... | collective-permute-start | bytes 36872 | tf_op jit(solution)/shard_map/ppermute | solution.py:24
  472.0 5.5 collective-permute-start.17
  477.6 8.7 %collective-permute-start.18 = (f32[1,1,34,1024]{3,2,1,0:T(8,128)S(1)}, f32[1,1,34,1024]{3,2,1,0:T(8,128)S(1)}, u32[]{:S(2)}, u32[]{:S(2)}) collective-permute-start(f32[1,1,34,1024]{3,2,1,0:T(8,128)S(1)} %get-tuple-element.46), channel_id=1, source_target_pairs={{0,1},{1,2},{2,3},{4,5},{5,6},{6,7},{8,9},{9,10},{10,11},{12,13},{... | collective-permute-start | bytes 417800 | tf_op jit(solution)/shard_map/ppermute | solution.py:24
  483.0 8.3 %collective-permute-start.19 = (f32[1,1,34,1024]{3,2,1,0:T(8,128)S(1)}, f32[1,1,34,1024]{3,2,1,0:T(8,128)S(1)}, u32[]{:S(2)}, u32[]{:S(2)}) collective-permute-start(f32[1,1,34,1024]{3,2,1,0:T(8,128)S(1)} %get-tuple-element.47), channel_id=1, source_target_pairs={{1,0},{2,1},{3,2},{5,4},{6,5},{7,6},{9,8},{10,9},{11,10},{13,12},{... | collective-permute-start | bytes 417800 | tf_op jit(solution)/shard_map/ppermute | solution.py:25
  493.9 178.0 %reduce-scatter.5.cloned.1.call-start = ((), (), s32[]{:S(2)}) async-start(), calls=%async_computation.4 | async-start | bytes 1966080 | tf_op jit(solution)/shard_map/reduce_scatter | solution.py:56
  494.0 19.6 %collective-permute-start.20 = (f32[1,16,1,1024]{3,1,2,0:T(8,128)S(1)}, f32[1,16,1,1024]{3,1,2,0:T(8,128)S(1)}, u32[]{:S(2)}, u32[]{:S(2)}) collective-permute-start(f32[1,16,1,1024]{3,1,2,0:T(8,128)S(1)} %get-tuple-element.34), channel_id=1, source_target_pairs={{0,4},{4,8},{8,12},{12,16},{16,20},{20,24},{24,28},{28,32},{32,36}... | collective-permute-start | bytes 196616 | tf_op jit(solution)/shard_map/ppermute | solution.py:24
  495.9 17.6 %collective-permute-start.21 = (f32[1,16,1,1024]{3,1,2,0:T(8,128)S(1)}, f32[1,16,1,1024]{3,1,2,0:T(8,128)S(1)}, u32[]{:S(2)}, u32[]{:S(2)}) collective-permute-start(f32[1,16,1,1024]{3,1,2,0:T(8,128)S(1)} %get-tuple-element.35), channel_id=1, source_target_pairs={{4,0},{8,4},{12,8},{16,12},{20,16},{24,20},{28,24},{32,28},{36,32}... | collective-permute-start | bytes 196616 | tf_op jit(solution)/shard_map/ppermute | solution.py:25
  505.2 15.7 %collective-permute-start.24 = (f32[1,16,1,1024]{3,1,2,0:T(8,128)S(1)}, f32[1,16,1,1024]{3,1,2,0:T(8,128)S(1)}, u32[]{:S(2)}, u32[]{:S(2)}) collective-permute-start(f32[1,16,1,1024]{3,1,2,0:T(8,128)S(1)} %get-tuple-element.38), channel_id=1, source_target_pairs={{0,4},{4,8},{8,12},{12,16},{16,20},{20,24},{24,28},{28,32},{32,36}... | collective-permute-start | bytes 196616 | tf_op jit(solution)/shard_map/ppermute | solution.py:24
  507.1 13.8 %collective-permute-start.25 = (f32[1,16,1,1024]{3,1,2,0:T(8,128)S(1)}, f32[1,16,1,1024]{3,1,2,0:T(8,128)S(1)}, u32[]{:S(2)}, u32[]{:S(2)}) collective-permute-start(f32[1,16,1,1024]{3,1,2,0:T(8,128)S(1)} %get-tuple-element.39), channel_id=1, source_target_pairs={{4,0},{8,4},{12,8},{16,12},{20,16},{24,20},{28,24},{32,28},{36,32}... | collective-permute-start | bytes 196616 | tf_op jit(solution)/shard_map/ppermute | solution.py:25
  513.8 14.7 %collective-permute-start.22 = (f32[1,1,34,1024]{3,1,2,0:T(1,128)S(1)}, f32[1,1,34,1024]{3,1,2,0:T(1,128)S(1)}, u32[]{:S(2)}, u32[]{:S(2)}) collective-permute-start(f32[1,1,34,1024]{3,1,2,0:T(1,128)S(1)} %get-tuple-element.24), channel_id=1, source_target_pairs={{0,1},{1,2},{2,3},{4,5},{5,6},{6,7},{8,9},{9,10},{10,11},{12,13},{... | collective-permute-start | bytes 417800 | tf_op jit(solution)/shard_map/ppermute | solution.py:24
  516.8 11.7 %collective-permute-start.23 = (f32[1,1,34,1024]{3,1,2,0:T(1,128)S(1)}, f32[1,1,34,1024]{3,1,2,0:T(1,128)S(1)}, u32[]{:S(2)}, u32[]{:S(2)}) collective-permute-start(f32[1,1,34,1024]{3,1,2,0:T(1,128)S(1)} %get-tuple-element.25), channel_id=1, source_target_pairs={{1,0},{2,1},{3,2},{5,4},{6,5},{7,6},{9,8},{10,9},{11,10},{13,12},{... | collective-permute-start | bytes 417800 | tf_op jit(solution)/shard_map/ppermute | solution.py:25
  521.2 7.8 %collective-permute-start.26 = (f32[1,1,34,1024]{3,1,2,0:T(1,128)S(1)}, f32[1,1,34,1024]{3,1,2,0:T(1,128)S(1)}, u32[]{:S(2)}, u32[]{:S(2)}) collective-permute-start(f32[1,1,34,1024]{3,1,2,0:T(1,128)S(1)} %get-tuple-element.26), channel_id=1, source_target_pairs={{0,1},{1,2},{2,3},{4,5},{5,6},{6,7},{8,9},{9,10},{10,11},{12,13},{... | collective-permute-start | bytes 417800 | tf_op jit(solution)/shard_map/ppermute | solution.py:24
  526.4 7.9 %collective-permute-start.27 = (f32[1,1,34,1024]{3,1,2,0:T(1,128)S(1)}, f32[1,1,34,1024]{3,1,2,0:T(1,128)S(1)}, u32[]{:S(2)}, u32[]{:S(2)}) collective-permute-start(f32[1,1,34,1024]{3,1,2,0:T(1,128)S(1)} %get-tuple-element.27), channel_id=1, source_target_pairs={{1,0},{2,1},{3,2},{5,4},{6,5},{7,6},{9,8},{10,9},{11,10},{13,12},{... | collective-permute-start | bytes 417800 | tf_op jit(solution)/shard_map/ppermute | solution.py:25
  555.9 8.3 %collective-permute-start.28 = (f32[1,16,1,1024]{3,1,2,0:T(8,128)S(1)}, f32[1,16,1,1024]{3,1,2,0:T(8,128)S(1)}, u32[]{:S(2)}, u32[]{:S(2)}) collective-permute-start(f32[1,16,1,1024]{3,1,2,0:T(8,128)S(1)} %get-tuple-element.32), channel_id=1, source_target_pairs={{0,4},{4,8},{8,12},{12,16},{16,20},{20,24},{24,28},{28,32},{32,36}... | collective-permute-start | bytes 196616 | tf_op jit(solution)/shard_map/ppermute | solution.py:24
  557.8 7.7 %collective-permute-start.29 = (f32[1,16,1,1024]{3,1,2,0:T(8,128)S(1)}, f32[1,16,1,1024]{3,1,2,0:T(8,128)S(1)}, u32[]{:S(2)}, u32[]{:S(2)}) collective-permute-start(f32[1,16,1,1024]{3,1,2,0:T(8,128)S(1)} %get-tuple-element.33), channel_id=1, source_target_pairs={{4,0},{8,4},{12,8},{16,12},{20,16},{24,20},{28,24},{32,28},{36,32}... | collective-permute-start | bytes 196616 | tf_op jit(solution)/shard_map/ppermute | solution.py:25
  565.7 5.1 collective-permute-start.30
  568.7 8.1 %collective-permute-start.31 = (f32[1,1,34,1024]{3,1,2,0:T(1,128)S(1)}, f32[1,1,34,1024]{3,1,2,0:T(1,128)S(1)}, u32[]{:S(2)}, u32[]{:S(2)}) collective-permute-start(f32[1,1,34,1024]{3,1,2,0:T(1,128)S(1)} %get-tuple-element.23), channel_id=1, source_target_pairs={{1,0},{2,1},{3,2},{5,4},{6,5},{7,6},{9,8},{10,9},{11,10},{13,12},{... | collective-permute-start | bytes 417800 | tf_op jit(solution)/shard_map/ppermute | solution.py:25
  581.5 8.3 %collective-permute-start.32 = (f32[1,16,1,1024]{3,1,2,0:T(8,128)S(1)}, f32[1,16,1,1024]{3,1,2,0:T(8,128)S(1)}, u32[]{:S(2)}, u32[]{:S(2)}) collective-permute-start(f32[1,16,1,1024]{3,1,2,0:T(8,128)S(1)} %get-tuple-element.30), channel_id=1, source_target_pairs={{0,4},{4,8},{8,12},{12,16},{16,20},{20,24},{24,28},{28,32},{32,36}... | collective-permute-start | bytes 196616 | tf_op jit(solution)/shard_map/ppermute | solution.py:24
  583.5 7.7 %collective-permute-start.33 = (f32[1,16,1,1024]{3,1,2,0:T(8,128)S(1)}, f32[1,16,1,1024]{3,1,2,0:T(8,128)S(1)}, u32[]{:S(2)}, u32[]{:S(2)}) collective-permute-start(f32[1,16,1,1024]{3,1,2,0:T(8,128)S(1)} %get-tuple-element.31), channel_id=1, source_target_pairs={{4,0},{8,4},{12,8},{16,12},{20,16},{24,20},{28,24},{32,28},{36,32}... | collective-permute-start | bytes 196616 | tf_op jit(solution)/shard_map/ppermute | solution.py:25
  591.4 5.4 collective-permute-start.34
  594.6 7.9 %collective-permute-start.35 = (f32[1,1,34,1024]{3,1,2,0:T(1,128)S(1)}, f32[1,1,34,1024]{3,1,2,0:T(1,128)S(1)}, u32[]{:S(2)}, u32[]{:S(2)}) collective-permute-start(f32[1,1,34,1024]{3,1,2,0:T(1,128)S(1)} %get-tuple-element.21), channel_id=1, source_target_pairs={{1,0},{2,1},{3,2},{5,4},{6,5},{7,6},{9,8},{10,9},{11,10},{13,12},{... | collective-permute-start | bytes 417800 | tf_op jit(solution)/shard_map/ppermute | solution.py:25
  607.2 8.3 %collective-permute-start.36 = (f32[1,16,1,1024]{3,1,2,0:T(8,128)S(1)}, f32[1,16,1,1024]{3,1,2,0:T(8,128)S(1)}, u32[]{:S(2)}, u32[]{:S(2)}) collective-permute-start(f32[1,16,1,1024]{3,1,2,0:T(8,128)S(1)} %get-tuple-element.28), channel_id=1, source_target_pairs={{0,4},{4,8},{8,12},{12,16},{16,20},{20,24},{24,28},{28,32},{32,36}... | collective-permute-start | bytes 196616 | tf_op jit(solution)/shard_map/ppermute | solution.py:24
  609.2 7.7 %collective-permute-start.37 = (f32[1,16,1,1024]{3,1,2,0:T(8,128)S(1)}, f32[1,16,1,1024]{3,1,2,0:T(8,128)S(1)}, u32[]{:S(2)}, u32[]{:S(2)}) collective-permute-start(f32[1,16,1,1024]{3,1,2,0:T(8,128)S(1)} %get-tuple-element.29), channel_id=1, source_target_pairs={{4,0},{8,4},{12,8},{16,12},{20,16},{24,20},{28,24},{32,28},{36,32}... | collective-permute-start | bytes 196616 | tf_op jit(solution)/shard_map/ppermute | solution.py:25
  617.1 5.2 collective-permute-start.38
  620.4 7.9 %collective-permute-start.39 = (f32[1,1,34,1024]{3,1,2,0:T(1,128)S(1)}, f32[1,1,34,1024]{3,1,2,0:T(1,128)S(1)}, u32[]{:S(2)}, u32[]{:S(2)}) collective-permute-start(f32[1,1,34,1024]{3,1,2,0:T(1,128)S(1)} %get-tuple-element.19), channel_id=1, source_target_pairs={{1,0},{2,1},{3,2},{5,4},{6,5},{7,6},{9,8},{10,9},{11,10},{13,12},{... | collective-permute-start | bytes 417800 | tf_op jit(solution)/shard_map/ppermute | solution.py:25
  637.0 34.9 %copy-start.11 = (s32[3,32,1024]{2,1,0:T(8,128)S(1)}, s32[3,32,1024]{2,1,0:T(8,128)}, u32[]{:S(2)}) copy-start(s32[3,32,1024]{2,1,0:T(8,128)} %param.10) | copy-start | bytes 1179652
  (10 other events, 57.6 us)
Sparse Core Ops, SparseCore 0:
  14.5 37.1 reduce-scatter.2
  494.0 25.7 all-gather.1
  637.1 34.7 reduce-scatter.4
where the time goes:
time: 697 us; the launch traced here: 686 us
  blocking collectives  318 us (46%)
  starting transfers between devices  144 us (21%)
  waiting for transfers between devices  113 us (16%)
  other arithmetic  64 us (9%)
  between operations  21.4 us (3%)
  local copies, waits for them, and re-layouts  14.8 us (2%)
  matrix products  10.5 us (2%)
    psum x3, blocking collectives, squares(): return lax.psum(jnp.sum(residual * residual), ('tile', 'therm'))  189 us
    psum x2, blocking collectives, per_device(): alpha = norm_now / lax.psum(jnp.sum(direction * image), ('tile', 'therm'))  129 us
    ppermute x20, starting transfers between devices, extended(): after = lax.ppermute(initial, axis, down)  80.2 us
    ppermute x20, starting transfers between devices, extended(): before = lax.ppermute(last, axis, up)  63.8 us
    reduce_scatter x2, waiting for transfers between devices, ohmic_warming(): lax.psum_scatter(jnp.einsum('lz,zxy->lxy', weights, field, precision=lax....  58.5 us
    ppermute x20, waiting for transfers between devices, extended(): after = lax.ppermute(initial, axis, down)  51.8 us
    broadcast_in_dim x3, other arithmetic, per_device(): warmth_fringe = contact_stripes(block_fringe(final_warmth[None])[0])  20.2 us
  transfers between devices with their start and end apart: 43, of which 20 were waited for; matrix products, arithmetic and copies ran while one was open for 4% of the time, Pallas kernels for 0%

commit v1 on v0

v1 whole, which is shorter than its diff:
```python
import functools

import jax
import jax.numpy as jnp
from jax import lax
from jax.experimental import pallas as pl
from jax.experimental.pallas import tpu as pltpu
from jax.sharding import PartitionSpec as P


LAYERS = 12
HALF = LAYERS // 2
OWN = 3
DEPTHS = 64
SLAB = DEPTHS // 2
DEEP = 16
ROWS = 16
RIM = 3
EXT = ROWS + 2 * RIM
HEATED = 7
SWEEPS = 4
WIDE = ROWS + 2 * SWEEPS
THICK = SLAB + SWEEPS
SCALE = 1.0 / 16.0
TINY = 1e-30

shunt_level = 0.05
pad_conductance = 4.0
via_conductance = 2.0
thermal_slope = 0.2
sink_level = 0.1

F32 = jnp.float32


def place():
    therm = lax.axis_index("therm")
    return therm // 2, therm % 2


def tile_spec(n):
    return [pl.BlockSpec(memory_space=pltpu.VMEM)] * n


def shaped(*dims):
    return jax.ShapeDtypeStruct(dims + (8, 128), F32)


def call(kernel, outs, scratch=(), scalars=0, cost=0):
    def run(*args):
        smem = [pl.BlockSpec(memory_space=pltpu.SMEM)] * scalars
        return pl.pallas_call(
            kernel,
            out_shape=outs,
            in_specs=smem + tile_spec(len(args) - scalars),
            out_specs=jax.tree.map(lambda _: pl.BlockSpec(memory_space=pltpu.VMEM), outs),
            scratch_shapes=[pltpu.VMEM(dims + (8, 128), F32) for dims in scratch],
            compiler_params=pltpu.CompilerParams(vmem_limit_bytes=56 * 1024 * 1024),
            cost_estimate=pl.CostEstimate(flops=cost * 2000, bytes_accessed=cost * 3000, transcendentals=0),
        )(*args)

    return run


def raw_view(value):
    n, rows, width = value.shape
    split = value.reshape(n, rows // 8, 8, width // 128, 128).transpose(0, 1, 3, 2, 4)
    return split.reshape(n, rows // 8, 8 * (width // 128), 128)


def raw_back(value):
    n, blocks, high, lanes = value.shape
    split = value.reshape(n, blocks, high // 8, 8, lanes).transpose(0, 1, 3, 2, 4)
    return split.reshape(n, blocks * 8, (high // 8) * lanes)


def at_row(ref, n, chunk, row):
    return ref[n, chunk * 2 + row // 8, pl.ds(row % 8, 8, stride=8), :]


def loop(count, body):
    def step(i, carry):
        body(i)
        return carry

    lax.fori_loop(0, count, step, 0)


def iotas():
    return lax.broadcasted_iota(jnp.int32, (8, 128), 0), lax.broadcasted_iota(jnp.int32, (8, 128), 1)


def after(v, lane):
    r = pltpu.roll(v, 127, 1)
    return jnp.where(lane == 127, pltpu.roll(r, 7, 0), r)


def before(v, lane):
    r = pltpu.roll(v, 1, 1)
    return jnp.where(lane == 0, pltpu.roll(r, 1, 0), r)


def inverse(v):
    r = pl.reciprocal(v, approx=True)
    r = r * (2.0 - v * r)
    return r * (2.0 - v * r)


def harmonic(a, b):
    return a * b * inverse(jnp.maximum(a + b, TINY))


def pack_kernel(value, own, send):
    _, core = place()

    def body(n):
        for row in range(ROWS):
            own[n, row] = at_row(value, n, core, row)
            send[n, row] = at_row(value, n, 1 - core, row)

    loop(value.shape[0], body)


def pack_args_kernel(classes, sink, category, link, contact, own, send):
    _, core = place()

    def body(n):
        for row in range(ROWS):
            for chunk, out in ((core, own), (1 - core, send)):
                kind = at_row(category, n, chunk, row)
                table = jnp.full((8, 128), classes[0], F32)
                for number in range(1, 8):
                    table = jnp.where(kind == number, classes[number], table)
                out[n, row] = at_row(sink, n, chunk, row)
                out[OWN + n, row] = table * SCALE
                out[2 * OWN + n, row] = at_row(link, n, chunk, row).astype(F32) * (via_conductance * SCALE)
                out[3 * OWN + n, row] = at_row(contact, n, chunk, row).astype(F32) * (
                    pad_conductance * SCALE
                ) + (shunt_level * SCALE)

    loop(OWN, body)


def weigh(weights, stride, parts, acc):
    def rows(block):
        total = [jnp.zeros((8, 128), F32)] * (4 * LAYERS)
        for ref, first, base in parts:

            def step(z, total):
                field = [ref[first + z, block * 4 + k] for k in range(4)]
                out = []
                for layer in range(LAYERS):
                    w = weights[layer * stride + base + z]
                    out += [total[layer * 4 + k] + w * field[k] for k in range(4)]
                return tuple(out)

            total = lax.fori_loop(0, DEEP, step, tuple(total), unroll=4)
        for layer in range(LAYERS):
            for k in range(4):
                acc[layer, block * 4 + k] = total[layer * 4 + k]

    loop(ROWS // 4, rows)


def heat_kernel(weights, t_own, t_got, a_own, a_got, part, a6, s_far, s_core_far, s_tile_far, s_core, s_tile):
    far, core = place()
    weigh(
        weights,
        DEPTHS,
        ((t_own, 0, SLAB * far + DEEP * core), (t_got, 0, SLAB * far + DEEP * (1 - core))),
        part,
    )

    def merge(n):
        for row in range(ROWS):
            for ch in range(4):
                a6[ch, OWN * core + n, row] = a_own[ch * OWN + n, row]
                a6[ch, OWN * (1 - core) + n, row] = a_got[ch * OWN + n, row]

    loop(OWN, merge)
    to_core, to_tile = (ROWS - RIM) * (1 - core), (ROWS - RIM) * core

    def heats(n):
        for row in range(ROWS):
            s_far[n, row] = part[5 * (1 - far) + n, row]
        for k in range(RIM):
            s_core_far[n, k] = part[5 * (1 - far) + n, to_core + k]
            s_tile_far[n, k] = part[5 * (1 - far) + n, to_tile + k]
            s_core[n, k] = part[5 * far + n, to_core + k]
            s_tile[n, k] = part[5 * far + n, to_tile + k]

    loop(HEATED, heats)
    edge = 5 * (1 - far)
    for n, ch in ((HEATED, 0), (HEATED + 1, 2)):
        for row in range(ROWS):
            s_far[n, row] = a6[ch, edge, row]
        for k in range(RIM):
            s_core_far[n, k] = a6[ch, edge, to_core + k]
            s_tile_far[n, k] = a6[ch, edge, to_tile + k]

    def args(o):
        for ch in range(4):
            for k in range(RIM):
                s_core[HEATED + ch * HALF + o, k] = a6[ch, o, to_core + k]
                s_tile[HEATED + ch * HALF + o, k] = a6[ch, o, to_tile + k]

    loop(HALF, args)


def apply(v, o, row, diag, row_edge, col_edge, vert, lane):
    here = v[o + 1, row]
    ce = col_edge[o, row]
    return (
        diag[o, row] * here
        - row_edge[o, row - 1] * v[o + 1, row - 1]
        - row_edge[o, row] * v[o + 1, row + 1]
        - ce * after(here, lane)
        - before(ce * here, lane)
        - vert[o + 1, row] * v[o + 2, row]
        - vert[o, row] * v[o, row]
    )


def basis_kernel(
    part, a6, g_far, g_core_far, g_tile_far, g_core, g_tile,
    v0, v1, v2, diag, row_edge, col_edge, vert, ground, s_basis, inv, lat,
):
    far, core = place()
    sub, lane = iotas()
    from_core, from_tile = (EXT - RIM) * (1 - core), (EXT - RIM) * core
    zero = jnp.zeros((8, 128), F32)

    def heats(n):
        def one(row, heat):
            inv[n, row] = inverse(1.0 + thermal_slope * heat)

        for k in range(ROWS):
            one(RIM + k, part[5 * far + n, k] + g_far[n, k])
        for k in range(RIM):
            one(from_core + k, g_core[n, k] + g_core_far[n, k])
            one(from_tile + k, g_tile[n, k] + g_tile_far[n, k])

    loop(HEATED, heats)
    lower = far.astype(F32)
    halo, none = 7 * (1 - far), 7 * far

    def rim(row, b, up):
        v0[halo, row] = b
        v0[none, row] = zero
        vert[0, row] = up * inv[0, row] * lower

    for k in range(ROWS):
        rim(RIM + k, g_far[HEATED, k], g_far[HEATED + 1, k])
    for k in range(RIM):
        rim(from_core + k, g_core_far[HEATED, k], g_core_far[HEATED + 1, k])
        rim(from_tile + k, g_tile_far[HEATED, k], g_tile_far[HEATED + 1, k])
    for row in range(EXT):
        for edge in (0, 7):
            v1[edge, row] = zero
            v2[edge, row] = zero

    def fields(o):
        def one(row, b, g, up, gr):
            warm = inv[o + far, row]
            v0[o + 1, row] = b
            lat[o, row] = g * warm
            vert[o + 1, row] = up * warm
            ground[o, row] = gr

        for k in range(ROWS):
            one(RIM + k, *[a6[ch, o, k] for ch in range(4)])
        for k in range(RIM):
            one(from_core + k, *[g_core[HEATED + ch * HALF + o, k] for ch in range(4)])
            one(from_tile + k, *[g_tile[HEATED + ch * HALF + o, k] for ch in range(4)])

    loop(HALF, fields)
    last = (sub == 7) & (lane == 127)

    def edges(o):
        for row in range(EXT - 1):
            row_edge[o, row] = harmonic(lat[o, row], lat[o, row + 1])
        for row in range(1, EXT - 1):
            here = lat[o, row]
            ce = jnp.where(last, 0.0, harmonic(here, after(here, lane)))
            col_edge[o, row] = ce
            diag[o, row] = (
                ground[o, row] + vert[o + 1, row] + vert[o, row]
                + row_edge[o, row - 1] + row_edge[o, row] + ce + before(ce, lane)
            )

    loop(HALF, edges)

    def first(o):
        for row in range(1, EXT - 1):
            v1[o + 1, row] = apply(v0, o, row, diag, row_edge, col_edge, vert, lane)

    loop(HALF, first)

    def second(o):
        for row in range(2, EXT - 2):
            v2[o + 1, row] = apply(v1, o, row, diag, row_edge, col_edge, vert, lane)

    loop(HALF, second)
    edge = 5 * (1 - far) + 1
    for k in range(EXT - 4):
        s_basis[0, k] = v1[edge, 2 + k]
        s_basis[1, k] = v2[edge, 2 + k]


def moments_kernel(v0, v1, v2, diag, row_edge, col_edge, vert, got, w2, out):
    far, _ = place()
    _, lane = iotas()

    def copy(n):
        for row in range(2, EXT - 2):
            w2[n, row] = v2[n, row]

    loop(HALF + 2, copy)
    edge, halo = 5 * (1 - far) + 1, 7 * (1 - far)
    for k in range(EXT - 4):
        row = 2 + k
        link = vert[6 * (1 - far), row]
        w2[edge, row] = v2[edge, row] - link * got[0, k]
        w2[halo, row] = got[1, k] - link * v1[edge, row]

    def body(o, sums):
        sums = list(sums)
        for row in range(RIM, RIM + ROWS):
            a, b, c = v0[o + 1, row], v1[o + 1, row], w2[o + 1, row]
            d = apply(w2, o, row, diag, row_edge, col_edge, vert, lane)
            for n, term in enumerate((a * a, a * b, b * b, b * c, c * c, c * d)):
                sums[n] = sums[n] + term
        return tuple(sums)

    sums = lax.fori_loop(0, HALF, body, (jnp.zeros((8, 128), F32),) * 6)
    for n in range(6):
        out[0, pl.ds(n, 1), :] = jnp.full((1, 128), jnp.sum(sums[n]), F32)
    out[0, pl.ds(6, 2), :] = jnp.zeros((2, 128), F32)
    out[1] = jnp.zeros((8, 128), F32)


def two_sum(a, b):
    s = a + b
    t = s - a
    return s, (a - (s - t)) + (b - t)


def two_prod(a, b):
    def split(v):
        t = v * 4097.0
        high = t - (t - v)
        return high, v - high

    p = a * b
    (ah, al), (bh, bl) = split(a), split(b)
    return p, ((ah * bh - p) + ah * bl + al * bh) + al * bl


def pair_add(a, b):
    s, e = two_sum(a[0], b[0])
    e = e + (a[1] + b[1])
    high = s + e
    return high, e - (high - s)


def pair_mul(a, b):
    p, e = two_prod(a[0], b[0])
    e = e + (a[0] * b[1] + a[1] * b[0])
    high = p + e
    return high, e - (high - p)


def pair_neg(a):
    return -a[0], -a[1]


def pair_div(a, b):
    q = a[0] / b[0]
    r = pair_add(a, pair_neg(pair_mul(b, (q, jnp.zeros_like(q)))))
    q2 = (r[0] + r[1]) / b[0]
    high = q + q2
    return high, q2 - (high - q)


def coefficients(m):
    mean, m2, m3, m4, m5 = [pair_div(v, m[0]) for v in m[1:]]
    low = pair_neg(mean)

    def lowered(seq):
        return [pair_add(b, pair_mul(low, a)) for a, b in zip(seq, seq[1:])]

    one = (jnp.ones_like(mean[0]), jnp.zeros_like(mean[0]))
    seq = [one, mean, m2, m3, m4, m5]
    seq = lowered(seq)
    central = []
    for power in range(2, 6):
        seq = lowered(seq)
        central.append(seq[0])
    c2, c3, c4, c5 = [v[0] + v[1] for v in central]
    s = mean[0] + mean[1]
    ok1 = c2 > 3e-8 * s * s
    c2 = jnp.where(ok1, c2, 1.0)
    skew = c3 / c2
    n2 = c4 - skew * c3 - c2 * c2
    ok2 = ok1 & (n2 > 1e-6 * c2 * c2) & (n2 > 3e-8 * (s * s) * (s * s))
    n2 = jnp.where(ok2, n2, 1.0)
    tq = c5 - 2.0 * skew * c4 + (skew * skew - 2.0 * c2) * c3 + 2.0 * skew * c2 * c2
    a2 = s + tq / n2
    a1 = s + skew
    b1, b2 = c2, n2 / c2
    d0 = s
    d1 = a1 - b1 / d0
    d2 = a2 - b2 / d1
    y0 = 1.0 / d0
    y1 = jnp.where(ok1, -y0 / d1, 0.0)
    y2 = jnp.where(ok2, -y1 / d2, 0.0)
    z2 = y2
    z1 = y1 - jnp.where(ok2, b2 * z2 / d1, 0.0)
    z0 = y0 - jnp.where(ok1, b1 * z1 / d0, 0.0)
    k2 = z2
    k1 = z1 - z2 * (skew + 2.0 * s)
    k0 = z0 - z1 * s + z2 * (s * s + skew * s - c2)
    return k0 * SCALE, k1 * SCALE, k2 * SCALE


def power_kernel(
    total, v0, v1, w2, diag, row_edge, col_edge, vert, ground, got,
    power, s_core, s_tile, loss, s_loss, volts,
):
    far, core = place()
    _, lane = iotas()
    spread = [
        (
            jnp.broadcast_to(total[0, pl.ds(n, 1), :], (8, 128)),
            jnp.broadcast_to(total[1, pl.ds(n, 1), :], (8, 128)),
        )
        for n in range(6)
    ]
    c0, c1, c2 = coefficients(spread)
    halo = 7 * (1 - far)

    def combine(n):
        for row in range(2, EXT - 2):
            volts[n, row] = c0 * v0[n, row] + c1 * v1[n, row] + c2 * w2[n, row]

    loop(HALF + 2, combine)
    for k in range(EXT - 4):
        row = 2 + k
        volts[halo, row] = c0 * v0[halo, row] + c1 * got[0, k] + c2 * w2[halo, row]

    def body(o):
        for k in range(ROWS):
            row = RIM + k
            x = volts[o + 1, row]
            near = after(x, lane) - x
            q = col_edge[o, row] * near * near
            q = q + before(q, lane)
            for edge, other in (
                (row_edge[o, row - 1], volts[o + 1, row - 1]),
                (row_edge[o, row], volts[o + 1, row + 1]),
                (vert[o + 1, row], volts[o + 2, row]),
                (vert[o, row], volts[o, row]),
            ):
                d = x - other
                q = q + edge * d * d
            power[o, k] = 16.0 * ground[o, row] * x * x + 8.0 * q

    loop(HALF, body)
    to_core, to_tile = (ROWS - RIM) * (1 - core), (ROWS - RIM) * core

    def sides(o):
        for k in range(RIM):
            s_core[o, k] = power[o, to_core + k]
            s_tile[o, k] = power[o, to_tile + k]

    loop(HALF, sides)

    def outs(n):
        for k in range(ROWS):
            loss[n, k] = volts[1 + OWN * core + n, RIM + k]
            s_loss[n, k] = volts[1 + OWN * (1 - core) + n, RIM + k]

    loop(OWN, outs)


def slab_rim_kernel(t_own, t_got, k_own, k_got, s_core, s_tile):
    _, core = place()
    to_core, to_tile = (ROWS - SWEEPS) * (1 - core), (ROWS - SWEEPS) * core

    def body(n):
        for f, (own, got) in enumerate(((t_own, t_got), (k_own, k_got))):
            for ref, z in ((own, DEEP * core + n), (got, DEEP * (1 - core) + n)):
                for k in range(SWEEPS):
                    s_core[f, z, k] = ref[n, to_core + k]
                    s_tile[f, z, k] = ref[n, to_tile + k]

    loop(DEEP, body)


def slab_wide_kernel(t_own, t_got, k_own, k_got, g_core, g_tile, wide, s_far):
    far, core = place()
    from_core, from_tile = (WIDE - SWEEPS) * (1 - core), (WIDE - SWEEPS) * core

    def body(n):
        for f, (own, got) in enumerate(((t_own, t_got), (k_own, k_got))):
            for ref, z in ((own, DEEP * core + n), (got, DEEP * (1 - core) + n)):
                for k in range(ROWS):
                    wide[f, z, SWEEPS + k] = ref[n, k]
                for k in range(SWEEPS):
                    wide[f, z, from_core + k] = g_core[f, z, k]
                    wide[f, z, from_tile + k] = g_tile[f, z, k]

    loop(DEEP, body)
    first = (SLAB - SWEEPS) * (1 - far)

    def send(n):
        for f in range(2):
            for row in range(WIDE):
                s_far[f, n, row] = wide[f, first + n, row]

    loop(SWEEPS, send)


def slab_edges_kernel(wide, g_far, warm, deep_edge, row_edge, col_edge, turn, cond):
    far, _ = place()
    sub, lane = iotas()
    zero = jnp.zeros((8, 128), F32)

    def body(n):
        for row in range(WIDE):
            warm[1 + SWEEPS * far + n, row] = wide[0, n, row]
            cond[SWEEPS * far + n, row] = wide[1, n, row]

    loop(SLAB, body)

    def rim(n):
        for row in range(WIDE):
            warm[1 + SLAB * (1 - far) + n, row] = g_far[0, n, row]
            cond[SLAB * (1 - far) + n, row] = g_far[1, n, row]

    loop(SWEEPS, rim)
    for row in range(WIDE):
        for n in (0, THICK + 1):
            warm[n, row] = zero
        for n in (0, THICK):
            deep_edge[n, row] = zero

    def deep(n):
        for row in range(WIDE):
            deep_edge[n + 1, row] = harmonic(cond[n, row], cond[n + 1, row])

    loop(THICK - 1, deep)
    last = (sub == 7) & (lane == 127)

    def edges(n):
        for row in range(WIDE - 1):
            row_edge[n, row] = harmonic(cond[n, row], cond[n, row + 1])
        for row in range(1, WIDE - 1):
            here = cond[n, row]
            ce = jnp.where(last, 0.0, harmonic(here, after(here, lane)))
            col_edge[n, row] = ce
            turn[n, row] = inverse(
                sink_level + deep_edge[n, row] + deep_edge[n + 1, row]
                + row_edge[n, row - 1] + row_edge[n, row] + ce + before(ce, lane)
            )

    loop(THICK, edges)


def sweeps_kernel(
    split, weights, power, p_far, p_core, p_core_far, p_tile, p_tile_far,
    warm, deep_edge, row_edge, col_edge, turn,
    out, s_out, final, s_final,
    joule, source, one, two,
):
    far, core = place()
    _, lane = iotas()
    zero = jnp.zeros((8, 128), F32)
    from_core = 1 + (EXT - RIM) * (1 - core)
    from_tile = 1 + (EXT - RIM) * core

    def gather(o):
        for layer, mid, by_core, by_tile in (
            (HALF * far + o, power, p_core, p_tile),
            (HALF * (1 - far) + o, p_far, p_core_far, p_tile_far),
        ):
            for k in range(ROWS):
                joule[layer, SWEEPS + k] = mid[o, k]
            for k in range(RIM):
                joule[layer, from_core + k] = by_core[o, k]
                joule[layer, from_tile + k] = by_tile[o, k]
            joule[layer, 0] = zero
            joule[layer, WIDE - 1] = zero

    loop(HALF, gather)
    base = (SLAB - SWEEPS) * far

    def sources(block):
        field = [[joule[layer, block * 4 + k] for k in range(4)] for layer in range(LAYERS)]

        def depth(n, carry):
            total = [zero] * 4
            for layer in range(LAYERS):
                w = split[(base + n) * LAYERS + layer]
                total = [total[k] + w * field[layer][k] for k in range(4)]
            for k in range(4):
                source[n, block * 4 + k] = total[k]
            return carry

        lax.fori_loop(0, THICK, depth, 0)

    loop(WIDE // 4, sources)
    for ref in (one, two):
        for row in range(WIDE):
            ref[0, row] = zero
            ref[THICK + 1, row] = zero

    before_ref = warm
    for sweep in range(1, SWEEPS + 1):
        after_ref = one if sweep % 2 else two
        start = sweep * far

        def step(i, src=before_ref, dst=after_ref, sweep=sweep, start=start):
            n = start + i
            for row in range(sweep, WIDE - sweep):
                here = src[n + 1, row]
                ce = col_edge[n, row]
                flow = source[n, row] + ce * after(here, lane) + before(ce * here, lane)
                flow = flow + row_edge[n, row - 1] * src[n + 1, row - 1] + row_edge[n, row] * src[n + 1, row + 1]
                flow = flow + deep_edge[n, row] * src[n, row] + deep_edge[n + 1, row] * src[n + 2, row]
                dst[n + 1, row] = flow * turn[n, row]

        loop(THICK - sweep, step)
        before_ref = after_ref

    def outs(n):
        for k in range(ROWS):
            out[n, k] = before_ref[1 + SWEEPS * far + DEEP * core + n, SWEEPS + k]
            s_out[n, k] = before_ref[1 + SWEEPS * far + DEEP * (1 - core) + n, SWEEPS + k]

    loop(DEEP, outs)
    weigh(
        weights,
        DEPTHS,
        ((out, 0, SLAB * far + DEEP * core), (s_out, 0, SLAB * far + DEEP * (1 - core))),
        final,
    )

    def sends(o):
        for k in range(ROWS):
            s_final[o, k] = final[HALF * (1 - far) + o, k]

    loop(HALF, sends)


def update_kernel(final, got, a6, mine, send):
    far, core = place()

    def body(n):
        for half, out in ((core, mine), (1 - core, send)):
            o = OWN * half + n
            for k in range(ROWS):
                heat = final[HALF * far + o, k] + got[o, k]
                out[n, k] = (16.0 * a6[1, o, k]) * inverse(1.0 + thermal_slope * heat)

    loop(OWN, body)


def unpack_kernel(own, got, out):
    _, core = place()

    def body(n):
        for k in range(ROWS):
            out[n, core * 2 + k // 8, pl.ds(k % 8, 8, stride=8), :] = own[n, k]
            out[n, (1 - core) * 2 + k // 8, pl.ds(k % 8, 8, stride=8), :] = got[n, k]

    loop(own.shape[0], body)


def unpack(own, got):
    n = own.shape[0]
    out = jax.ShapeDtypeStruct((n, 4, 64, 128), F32)
    return raw_back(call(unpack_kernel, out, cost=n)(own, got))


def pack(value):
    n = value.shape[0]
    return call(pack_kernel, [shaped(n, ROWS)] * 2, cost=n)(raw_view(value))


def to_core(value):
    return lax.ppermute(value, "therm", [(i, i ^ 1) for i in range(4)])


def to_far(value):
    return lax.ppermute(value, "therm", [(i, i ^ 2) for i in range(4)])


def to_core_far(value):
    return lax.ppermute(value, "therm", [(i, i ^ 3) for i in range(4)])


def to_tile(value, cross=0):
    pairs = []
    for t in range(lax.axis_size("tile") - 1):
        for half in range(2):
            low = 4 * t + 2 * half + 1
            high = 4 * (t + 1) + 2 * (half ^ cross)
            pairs += [(low, high), (high, low)]
    return lax.ppermute(value, ("tile", "therm"), pairs)


def total_of(values):
    def add(a, b):
        high, low = pair_add((a[0], a[1]), (b[0], b[1]))
        return jnp.stack([high, low])

    values = add(values, to_core(values))
    x_peers = []
    for bits in (1, 2, 3):
        pairs = []
        for t in range(lax.axis_size("tile")):
            for h in range(4):
                pairs.append((4 * t + h, 4 * (t ^ (bits & 1)) + (h ^ (bits & 2))))
        x_peers.append(lax.ppermute(values, ("tile", "therm"), pairs))
    for peer in x_peers:
        values = add(values, peer)
    for unit in (2, 8):
        peers = [
            lax.ppermute(values, "tile", [(t, t ^ (unit * k)) for t in range(lax.axis_size("tile"))])
            for k in (1, 2, 3)
        ]
        for peer in peers:
            values = add(values, peer)
    return values


def per_device(
    sink_current,
    metal_category,
    upward_link_flag,
    supply_contact_flag,
    baseline_admittance,
    beginning_warmth,
    cell_diffusivity,
    dissipation_split,
    probe_weighting,
):
    weights = probe_weighting.reshape(-1)
    split = dissipation_split.reshape(-1)
    t_own, t_send = pack(beginning_warmth)
    t_got = to_core(t_send)
    a_own, a_send = call(pack_args_kernel, [shaped(4 * OWN, ROWS)] * 2, scalars=1, cost=12)(
        baseline_admittance,
        *[raw_view(v) for v in (sink_current, metal_category, upward_link_flag, supply_contact_flag)],
    )
    a_got = to_core(a_send)
    k_own, k_send = pack(cell_diffusivity)
    k_got = to_core(k_send)

    part, a6, s_far, s_core_far, s_tile_far, s_core, s_tile = call(
        heat_kernel,
        [
            shaped(LAYERS, ROWS),
            shaped(4, HALF, ROWS),
            shaped(HEATED + 2, ROWS),
            shaped(HEATED + 2, RIM),
            shaped(HEATED + 2, RIM),
            shaped(HEATED + 4 * HALF, RIM),
            shaped(HEATED + 4 * HALF, RIM),
        ],
        scalars=1,
        cost=24,
    )(weights, t_own, t_got, a_own, a_got)
    g_far = to_far(s_far)
    g_tile = to_tile(s_tile)
    g_tile_far = to_tile(s_tile_far, 1)
    g_core_far = to_core_far(s_core_far)
    g_core = to_core(s_core)

    field = shaped(HALF + 2, EXT)
    coef = shaped(HALF, EXT)
    v0, v1, v2, diag, row_edge, col_edge, vert, ground, s_basis = call(
        basis_kernel,
        [field, field, field, coef, coef, coef, shaped(HALF + 1, EXT), coef, shaped(2, EXT - 4)],
        scratch=((HEATED, EXT), (HALF, EXT)),
        cost=16,
    )(part, a6, g_far, g_core_far, g_tile_far, g_core, g_tile)
    g_basis = to_far(s_basis)
    w2, sums = call(moments_kernel, [field, shaped(2)], cost=10)(
        v0, v1, v2, diag, row_edge, col_edge, vert, g_basis
    )
    total = total_of(sums)

    rim = shaped(2, SLAB, SWEEPS)
    k_core, k_tile = call(slab_rim_kernel, [rim, rim], cost=8)(t_own, t_got, k_own, k_got)
    wide, s_deep = call(slab_wide_kernel, [shaped(2, SLAB, WIDE), shaped(2, SWEEPS, WIDE)], cost=24)(
        t_own, t_got, k_own, k_got, to_core(k_core), to_tile(k_tile)
    )
    thick = shaped(THICK, WIDE)
    warm, deep_edge, row_heat, col_heat, turn = call(
        slab_edges_kernel,
        [shaped(THICK + 2, WIDE), shaped(THICK + 1, WIDE), thick, thick, thick],
        scratch=((THICK, WIDE),),
        cost=64,
    )(wide, to_far(s_deep))

    power, p_core, p_tile, loss, s_loss = call(
        power_kernel,
        [shaped(HALF, ROWS), shaped(HALF, RIM), shaped(HALF, RIM), shaped(OWN, ROWS), shaped(OWN, ROWS)],
        scratch=((HALF + 2, EXT),),
        cost=10,
    )(total, v0, v1, w2, diag, row_edge, col_edge, vert, ground, g_basis)
    p_far = to_far(power)
    q_tile = to_tile(p_tile)
    q_tile_far = to_tile(p_tile, 1)
    q_core_far = to_core_far(p_core)
    q_core = to_core(p_core)
    voltage_loss = unpack(loss, to_core(s_loss))

    out, s_out, final, s_final = call(
        sweeps_kernel,
        [shaped(DEEP, ROWS), shaped(DEEP, ROWS), shaped(LAYERS, ROWS), shaped(HALF, ROWS)],
        scratch=((LAYERS, WIDE), (THICK, WIDE), (THICK + 2, WIDE), (THICK + 2, WIDE)),
        scalars=2,
        cost=128,
    )(split, weights, power, p_far, q_core, q_core_far, q_tile, q_tile_far, warm, deep_edge, row_heat, col_heat, turn)
    g_final = to_far(s_final)
    final_warmth = unpack(out, to_core(s_out))
    mine, s_mine = call(update_kernel, [shaped(OWN, ROWS)] * 2, cost=4)(final, g_final, a6)
    updated_admittance = unpack(mine, to_core(s_mine))
    return voltage_loss, final_warmth, updated_admittance


def solution(mesh):
    spread = P("therm", "tile", None)
    return jax.shard_map(
        per_device,
        mesh=mesh,
        in_specs=(spread, spread, spread, spread, P(), spread, spread, P(), P()),
        out_specs=(spread, spread, spread),
        check_vma=False,
    )
```

time: 697 us -> 227 us (0.33); the launches traced: 686 us -> 226 us
  blocking collectives: 318 us -> 0 us
  Pallas kernels: 0 us -> 102 us
  starting transfers between devices: 144 us -> 59.9 us
  other arithmetic: 64 us -> 1.42 us
  waiting for transfers between devices: 113 us -> 51.4 us
  between operations: 21.4 us -> 0.86 us
  matrix products: 10.5 us -> 0 us
    psum x5 -> x0, blocking collectives: 318 us -> none  [the longest x3 189 us: squares(): return lax.psum(jnp.sum(residual * residual), ('tile', 'therm'))]
    pallas_call x0 -> x15, Pallas kernels: none -> 102 us  [run(): pl.pallas_call(kernel, out_shape=outs, in_specs=smem + tile_spec(len(args...]
    ppermute x40 -> x31, starting transfers between devices: 144 us -> 59.9 us  [the longest x5 18.9 us: to_tile(): return lax.ppermute(value, ('tile', 'therm'), pairs)]
    reduce_scatter x2 -> x0, waiting for transfers between devices: 58.5 us -> none  [ohmic_warming(): lax.psum_scatter(jnp.einsum('lz,zxy->lxy', weights, field, precision=lax....]
    div x8 -> x0, other arithmetic: 23.2 us -> none  [the longest x1 7.27 us: per_device(): updated_admittance = table / (1.0 + thermal_slope * leftover_energy)]
    broadcast_in_dim x3 -> x0, other arithmetic: 20.2 us -> none  [per_device(): warmth_fringe = contact_stripes(block_fringe(final_warmth[None])[0])]
    dot_general x3 -> x0, matrix products: 10.5 us -> none  [the longest x2 6.31 us: ohmic_warming(): jnp.einsum('lz,zxy->lxy', weights, field, precision=lax.Precision.HIGHEST)]
    reduce_sum x5 -> x0, other arithmetic: 8.8 us -> none  [the longest x3 5.6 us: per_device(): alpha = norm_now / lax.psum(jnp.sum(direction * image), ('tile', 'therm'))]
  transfers between devices with their start and end apart: 43 -> 31, of which waited for: 20 -> 11; matrix products, arithmetic and copies ran while one was open for 4% -> 1% of each run, Pallas kernels for 0% -> 25%
where the time goes in v1:
time: 227 us; the launch traced here: 226 us
  Pallas kernels  102 us (45%)
  starting transfers between devices  59.9 us (26%)
  waiting for transfers between devices  51.4 us (23%)
  local copies, waits for them, and re-layouts  10.4 us (5%)
    pallas_call x15, Pallas kernels, run(): pl.pallas_call(kernel, out_shape=outs, in_specs=smem + tile_spec(len(args...  102 us
    ppermute x5, starting transfers between devices, to_tile(): return lax.ppermute(value, ('tile', 'therm'), pairs)  18.9 us
    ppermute x5, waiting for transfers between devices, to_far(): return lax.ppermute(value, 'therm', [(i, i ^ 2) for i in range(4)])  18.6 us
    ppermute x10, starting transfers between devices, to_core(): return lax.ppermute(value, 'therm', [(i, i ^ 1) for i in range(4)])  13.6 us
    ppermute x2, waiting for transfers between devices, to_core_far(): return lax.ppermute(value, 'therm', [(i, i ^ 3) for i in range(4)])  13 us
    ppermute x5, waiting for transfers between devices, to_tile(): return lax.ppermute(value, ('tile', 'therm'), pairs)  11 us
    unnamed x49, local copies, waits for them, and re-layouts  9.04 us
    ppermute x5, starting transfers between devices, to_far(): return lax.ppermute(value, 'therm', [(i, i ^ 2) for i in range(4)])  8.6 us
  transfers between devices with their start and end apart: 31, of which 11 were waited for; matrix products, arithmetic and copies ran while one was open for 1% of the time, Pallas kernels for 25%

profile of v1, /device:TPU:25, one launch (start us, length us, event | category | flops | bytes accessed | tf_op | source)
XLA Modules:
  0.0 226.2 jit_solution(8386998742898298)
XLA Ops:
  0.6 3.4 %shard_map.112 = (f32[16,16,8,128]{3,2,1,0:T(8,128)}, f32[16,16,8,128]{3,2,1,0:T(8,128)}) custom-call(f32[16,4,64,128]{3,2,1,0:T(8,128)} %bitcast.45), custom_call_target="tpu_custom_call" | custom-call | flops 32000 | bytes 48000 | tf_op jit(solution)/shard_map/pallas_call | solution.py:52
  4.7 3.0 %shard_map.113 = (f32[12,16,8,128]{3,2,1,0:T(8,128)}, f32[12,16,8,128]{3,2,1,0:T(8,128)}) custom-call(f32[8]{0:T(128)} %classes.1, f32[3,4,64,128]{3,2,1,0:T(8,128)} %bitcast.50, s32[3,4,64,128]{3,2,1,0:T(8,128)} %bitcast.51, s32[3,4,64,128]{3,2,1,0:T(8,128)} %bitcast.52, s32[3,4,64,128]{3,2,1,0:T(8,128)} %bitcast.53), custom_call_target="tpu_custom_call" | custom-call | flops 24000 | bytes 36000 | tf_op jit(solution)/shard_map/pallas_call | solution.py:52
  8.3 1.8 collective-permute-done.1.a_got
  10.1 0.9 copy-done.6
  11.5 6.6 %shard_map.114 = (f32[12,16,8,128]{3,2,1,0:T(8,128)}, f32[4,6,16,8,128]{4,3,2,1,0:T(8,128)}, f32[9,16,8,128]{3,2,1,0:T(8,128)}, f32[9,3,8,128]{3,2,1,0:T(8,128)}...) custom-call(f32[768]{0:T(1024)} %reshape.66.weights, ...), custom_call_target="tpu_custom_call" | custom-call | flops 48000 | bytes 72000 | tf_op jit(solution)/shard_map/pallas_call | solution.py:52
  18.1 2.7 %collective-permute-start.2 = (f32[9,16,8,128]{3,2,1,0:T(8,128)}, f32[9,16,8,128]{3,2,1,0:T(8,128)S(1)}, u32[]{:S(2)}, u32[]{:S(2)}) collective-permute-start(f32[9,16,8,128]{3,2,1,0:T(8,128)} %get-tuple-element.53), channel_id=1, source_target_pairs={{0,2},{1,3},{2,0},{3,1},{4,6},{5,7},{6,4},{7,5},{8,10},{9,11},{10,... | collective-permute-start | bytes 1769480 | tf_op jit(solution)/shard_map/ppermute | solution.py:696
  20.8 3.4 %shard_map.119 = (f32[16,16,8,128]{3,2,1,0:T(8,128)}, f32[16,16,8,128]{3,2,1,0:T(8,128)}) custom-call(f32[16,4,64,128]{3,2,1,0:T(8,128)} %bitcast.46), custom_call_target="tpu_custom_call" | custom-call | flops 32000 | bytes 48000 | tf_op jit(solution)/shard_map/pallas_call | solution.py:52
  24.7 2.5 %collective-permute-start.6 = (f32[31,3,8,128]{3,2,1,0:T(8,128)}, f32[31,3,8,128]{3,2,1,0:T(8,128)S(1)}, u32[]{:S(2)}, u32[]{:S(2)}) collective-permute-start(f32[31,3,8,128]{3,2,1,0:T(8,128)} %get-tuple-element.57), channel_id=1, source_target_pairs={{1,4},{4,1},{3,6},{6,3},{5,8},{8,5},{7,10},{10,7},{9,12},{12,9},{1... | collective-permute-start | bytes 1142792 | tf_op jit(solution)/shard_map/ppermute | solution.py:710
  27.2 5.4 %collective-permute-start.3 = (f32[9,3,8,128]{3,2,1,0:T(8,128)}, f32[9,3,8,128]{3,2,1,0:T(8,128)S(1)}, u32[]{:S(2)}, u32[]{:S(2)}) collective-permute-start(f32[9,3,8,128]{3,2,1,0:T(8,128)} %get-tuple-element.54), channel_id=1, source_target_pairs={{0,3},{1,2},{2,1},{3,0},{4,7},{5,6},{6,5},{7,4},{8,11},{9,10},{10,... | collective-permute-start | bytes 331784 | tf_op jit(solution)/shard_map/ppermute | solution.py:700
  32.7 13.0 %collective-permute-done.3.g_core_far = f32[9,3,8,128]{3,2,1,0:T(8,128)S(1)} collective-permute-done((f32[9,3,8,128]{3,2,1,0:T(8,128)}, f32[9,3,8,128]{3,2,1,0:T(8,128)S(1)}, u32[]{:S(2)}, u32[]{:S(2)}) %collective-permute-start.3) | collective-permute-done | bytes 110624 | tf_op jit(solution)/shard_map/ppermute | solution.py:700
  45.7 4.1 %collective-permute-start.4 = (f32[9,3,8,128]{3,2,1,0:T(8,128)}, f32[9,3,8,128]{3,2,1,0:T(8,128)S(1)}, u32[]{:S(2)}, u32[]{:S(2)}) collective-permute-start(f32[9,3,8,128]{3,2,1,0:T(8,128)} %get-tuple-element.55), channel_id=1, source_target_pairs={{1,6},{6,1},{3,4},{4,3},{5,10},{10,5},{7,8},{8,7},{9,14},{14,9},{1... | collective-permute-start | bytes 331784 | tf_op jit(solution)/shard_map/ppermute | solution.py:710
  49.8 4.1 %collective-permute-done.4.g_tile_far = f32[9,3,8,128]{3,2,1,0:T(8,128)S(1)} collective-permute-done((f32[9,3,8,128]{3,2,1,0:T(8,128)}, f32[9,3,8,128]{3,2,1,0:T(8,128)S(1)}, u32[]{:S(2)}, u32[]{:S(2)}) %collective-permute-start.4) | collective-permute-done | bytes 110624 | tf_op jit(solution)/shard_map/ppermute | solution.py:710
  55.0 7.3 %shard_map.115 = (f32[8,22,8,128]{3,2,1,0:T(8,128)}, f32[8,22,8,128]{3,2,1,0:T(8,128)}, f32[8,22,8,128]{3,2,1,0:T(8,128)}, f32[6,22,8,128]{3,2,1,0:T(8,128)}, f3...) custom-call(f32[12,16,8,128]{3,2,1,0:T(8,128)} %get-tuple-element.51, ...), custom_call_target="tpu_custom_call" | custom-call | flops 32000 | bytes 48000 | tf_op jit(solution)/shard_map/pallas_call | solution.py:52
  62.3 1.1 collective-permute-start.7
  63.4 4.6 %collective-permute-done.7.got = f32[2,18,8,128]{3,2,1,0:T(8,128)S(1)} collective-permute-done((f32[2,18,8,128]{3,2,1,0:T(8,128)}, f32[2,18,8,128]{3,2,1,0:T(8,128)S(1)}, u32[]{:S(2)}, u32[]{:S(2)}) %collective-permute-start.7) | collective-permute-done | bytes 147488 | tf_op jit(solution)/shard_map/ppermute | solution.py:696
  68.7 3.8 %shard_map.116 = (f32[8,22,8,128]{3,2,1,0:T(8,128)}, f32[2,8,128]{2,1,0:T(8,128)}) custom-call(f32[8,22,8,128]{3,2,1,0:T(8,128)} %get-tuple-element.58.v0, f32[8,22,8,128]{3,2,1,0:T(8,128)} %get-tuple-element.59.v1, f32[8,22,8,128]{3,2,1,0:T(8,128)} %get-tuple-element.60.v2, f32[6,22,8,128]{3,2,1,0:T(8,128)} %get-tuple-element.61.diag, ...), custom_call_target="tpu_custom_call" | custom-call | flops 20000 | bytes 30000 | tf_op jit(solution)/shard_map/pallas_call | solution.py:52
  72.5 4.2 %collective-permute-start.8 = (f32[2,8,128]{2,1,0:T(8,128)}, f32[2,8,128]{2,1,0:T(8,128)S(1)}, u32[]{:S(2)}, u32[]{:S(2)}) collective-permute-start(f32[2,8,128]{2,1,0:T(8,128)} %get-tuple-element.66), channel_id=1, source_target_pairs={{0,1},{1,0},{2,3},{3,2},{4,5},{5,4},{6,7},{7,6},{8,9},{9,8},{10,11... | collective-permute-start | bytes 24584 | tf_op jit(solution)/shard_map/ppermute | solution.py:692
  76.6 1.0 collective-permute-done.8
  79.1 1.0 copy-done.1
  80.1 3.7 %shard_map.120 = (f32[2,32,4,8,128]{4,3,2,1,0:T(8,128)}, f32[2,32,4,8,128]{4,3,2,1,0:T(8,128)}) custom-call(f32[16,16,8,128]{3,2,1,0:T(8,128)} %get-tuple-element.47.t_own, f32[16,16,8,128]{3,2,1,0:T(8,128)} %copy-done, f32[16,16,8,128]{3,2,1,0:T(8,128)} %get-tuple-element.74.k_own, f32[16,16,8,128]{3,2,1,0:T(8,128)} %copy-done.1), custom_call_target="tpu_custom_call" | custom-call | flops 16000 | bytes 24000 | tf_op jit(solution)/shard_map/pallas_call | solution.py:52
  84.4 3.5 %collective-permute-start.26 = (f32[2,32,4,8,128]{4,3,2,1,0:T(8,128)}, f32[2,32,4,8,128]{4,3,2,1,0:T(8,128)S(1)}, u32[]{:S(2)}, u32[]{:S(2)}) collective-permute-start(f32[2,32,4,8,128]{4,3,2,1,0:T(8,128)} %get-tuple-element.77), channel_id=1, source_target_pairs={{1,4},{4,1},{3,6},{6,3},{5,8},{8,5},{7,10},{10,7},{9,12},{12,9},{1... | collective-permute-start | bytes 3145736 | tf_op jit(solution)/shard_map/ppermute | solution.py:710
  88.0 1.6 collective-permute-start.11
  89.6 2.1 collective-permute-done.11
  91.8 1.4 collective-permute-start.12
  93.2 2.4 %collective-permute-start.13 = (f32[2,8,128]{2,1,0:T(8,128)S(1)}, f32[2,8,128]{2,1,0:T(8,128)S(1)}, u32[]{:S(2)}, u32[]{:S(2)}) collective-permute-start(f32[2,8,128]{2,1,0:T(8,128)S(1)} %pad_maximum_fusion.1), channel_id=1, source_target_pairs={{0,16},{4,20},{8,24},{12,28},{16,0},{20,4},{24,8},{28,12},{32,48},... | collective-permute-start | bytes 24584 | tf_op jit(solution)/shard_map/ppermute | solution.py:730
  95.7 1.8 collective-permute-done.13
  97.6 2.0 collective-permute-done.14
  99.6 1.1 collective-permute-start.15
  101.3 2.3 %collective-permute-start.17 = (f32[2,8,128]{2,1,0:T(8,128)S(1)}, f32[2,8,128]{2,1,0:T(8,128)S(1)}, u32[]{:S(2)}, u32[]{:S(2)}) collective-permute-start(f32[2,8,128]{2,1,0:T(8,128)S(1)} %pad_maximum_fusion.2), channel_id=1, source_target_pairs={{0,96},{4,100},{8,104},{12,108},{16,112},{20,116},{24,120},{28,124... | collective-permute-start | bytes 24584 | tf_op jit(solution)/shard_map/ppermute | solution.py:730
  103.6 6.8 %collective-permute-done.26.g_tile = f32[2,32,4,8,128]{4,3,2,1,0:T(8,128)S(1)} collective-permute-done((f32[2,32,4,8,128]{4,3,2,1,0:T(8,128)}, f32[2,32,4,8,128]{4,3,2,1,0:T(8,128)S(1)}, u32[]{:S(2)}, u32[]{:S(2)}) %collective-permute-start.26) | collective-permute-done | bytes 1048608 | tf_op jit(solution)/shard_map/ppermute | solution.py:710
  110.4 1.0 copy-done.3
  111.4 6.3 %shard_map.121 = (f32[2,32,24,8,128]{4,3,2,1,0:T(8,128)}, f32[2,4,24,8,128]{4,3,2,1,0:T(8,128)}) custom-call(f32[16,16,8,128]{3,2,1,0:T(8,128)} %get-tuple-element.47.t_own, f32[16,16,8,128]{3,2,1,0:T(8,128)} %copy-done, f32[16,16,8,128]{3,2,1,0:T(8,128)} %get-tuple-element.74.k_own, f32[16,16,8,128]{3,2,1,0:T(8,128)} %copy-done.1, ...), custom_call_target="tpu_custom_call" | custom-call | flops 48000 | bytes 72000 | tf_op jit(solution)/shard_map/pallas_call | solution.py:52
  117.8 4.2 %collective-permute-start.27 = (f32[2,4,24,8,128]{4,3,2,1,0:T(8,128)}, f32[2,4,24,8,128]{4,3,2,1,0:T(8,128)S(1)}, u32[]{:S(2)}, u32[]{:S(2)}) collective-permute-start(f32[2,4,24,8,128]{4,3,2,1,0:T(8,128)} %get-tuple-element.79), channel_id=1, source_target_pairs={{0,2},{1,3},{2,0},{3,1},{4,6},{5,7},{6,4},{7,5},{8,10},{9,11},{10,... | collective-permute-start | bytes 2359304 | tf_op jit(solution)/shard_map/ppermute | solution.py:696
  122.6 4.7 %shard_map.117 = (f32[6,16,8,128]{3,2,1,0:T(8,128)}, f32[6,3,8,128]{3,2,1,0:T(8,128)}, f32[6,3,8,128]{3,2,1,0:T(8,128)}, f32[3,16,8,128]{3,2,1,0:T(8,128)}, f32[3,16,8,128]{3,2,1,0:T(8,128)}) custom-call(f32[2,8,128]{2,1,0:T(8,128)} %pad_maximum_fusion.3.total, f32[8,22,8,128]{3,2,1,0:T(8,128)} %get-tuple-element.58.v0, ...), custom_call_target="tpu_custom_call" | custom-call | flops 20000 | bytes 30000 | tf_op jit(solution)/shard_map/pallas_call | solution.py:52
  127.4 2.8 %collective-permute-start.20 = (f32[6,3,8,128]{3,2,1,0:T(8,128)}, f32[6,3,8,128]{3,2,1,0:T(8,128)S(1)}, u32[]{:S(2)}, u32[]{:S(2)}) collective-permute-start(f32[6,3,8,128]{3,2,1,0:T(8,128)} %get-tuple-element.72), channel_id=1, source_target_pairs={{0,1},{1,0},{2,3},{3,2},{4,5},{5,4},{6,7},{7,6},{8,9},{9,8},{10,11... | collective-permute-start | bytes 221192 | tf_op jit(solution)/shard_map/ppermute | solution.py:692
  130.2 3.1 %collective-permute-start.21 = (f32[6,3,8,128]{3,2,1,0:T(8,128)}, f32[6,3,8,128]{3,2,1,0:T(8,128)S(1)}, u32[]{:S(2)}, u32[]{:S(2)}) collective-permute-start(f32[6,3,8,128]{3,2,1,0:T(8,128)} %get-tuple-element.72), channel_id=1, source_target_pairs={{0,3},{1,2},{2,1},{3,0},{4,7},{5,6},{6,5},{7,4},{8,11},{9,10},{10,... | collective-permute-start | bytes 221192 | tf_op jit(solution)/shard_map/ppermute | solution.py:700
  133.2 1.9 collective-permute-start.22
  135.2 2.4 %collective-permute-done.27.g_far = f32[2,4,24,8,128]{4,3,2,1,0:T(8,128)S(1)} collective-permute-done((f32[2,4,24,8,128]{4,3,2,1,0:T(8,128)}, f32[2,4,24,8,128]{4,3,2,1,0:T(8,128)S(1)}, u32[]{:S(2)}, u32[]{:S(2)}) %collective-permute-start.27) | collective-permute-done | bytes 786464 | tf_op jit(solution)/shard_map/ppermute | solution.py:696
  137.6 6.9 %collective-permute-start.23 = (f32[6,3,8,128]{3,2,1,0:T(8,128)}, f32[6,3,8,128]{3,2,1,0:T(8,128)S(1)}, u32[]{:S(2)}, u32[]{:S(2)}) collective-permute-start(f32[6,3,8,128]{3,2,1,0:T(8,128)} %get-tuple-element.73), channel_id=1, source_target_pairs={{1,6},{6,1},{3,4},{4,3},{5,10},{10,5},{7,8},{8,7},{9,14},{14,9},{1... | collective-permute-start | bytes 221192 | tf_op jit(solution)/shard_map/ppermute | solution.py:710
  145.3 18.4 %shard_map.122 = (f32[38,24,8,128]{3,2,1,0:T(8,128)}, f32[37,24,8,128]{3,2,1,0:T(8,128)}, f32[36,24,8,128]{3,2,1,0:T(8,128)}, f32[36,24,8,128]{3,2,1,0:T(8,128)}, f32[36,24,8,128]{3,2,1,0:T(8,128)}) custom-call(f32[2,32,24,8,128]{4,3,2,1,0:T(8,128)} %get-tuple-element.78.wide, f32[2,4,24,8,128]{4,3,2,1,0:T(8,128)} %copy-done.5), custom_call_target="tpu_custom_call" | custom-call | flops 128000 | bytes 192000 | tf_op jit(solution)/shard_map/pallas_call | solution.py:52
  164.6 31.9 %shard_map.123 = (f32[16,16,8,128]{3,2,1,0:T(8,128)}, f32[16,16,8,128]{3,2,1,0:T(8,128)}, f32[12,16,8,128]{3,2,1,0:T(8,128)}, f32[6,16,8,128]{3,2,1,0:T(8,128)}) custom-call(f32[768]{0:T(1024)} %reshape.79.split, f32[768]{0:T(1024)} %reshape.66.weights, f32[6,16,8,128]{3,2,1,0:T(8,128)} %get-tuple-element.71.power, f32[6,16,8,128]{3,2,1,0:T(8,128)} %copy-done.10, ...), custom_call_target="tpu_custom_call" | custom-call | flops 256000 | bytes 384000 | tf_op jit(solution)/shard_map/pallas_call | solution.py:52
  196.5 3.7 %collective-permute-start.28 = (f32[16,16,8,128]{3,2,1,0:T(8,128)}, f32[16,16,8,128]{3,2,1,0:T(8,128)S(1)}, u32[]{:S(2)}, u32[]{:S(2)}) collective-permute-start(f32[16,16,8,128]{3,2,1,0:T(8,128)} %get-tuple-element.86), channel_id=1, source_target_pairs={{0,1},{1,0},{2,3},{3,2},{4,5},{5,4},{6,7},{7,6},{8,9},{9,8},{10,11... | collective-permute-start | bytes 3145736 | tf_op jit(solution)/shard_map/ppermute | solution.py:692
  201.1 11.5 %collective-permute-done.29.got = f32[6,16,8,128]{3,2,1,0:T(8,128)S(1)} collective-permute-done((f32[6,16,8,128]{3,2,1,0:T(8,128)}, f32[6,16,8,128]{3,2,1,0:T(8,128)S(1)}, u32[]{:S(2)}, u32[]{:S(2)}) %collective-permute-start.29) | collective-permute-done | bytes 393248 | tf_op jit(solution)/shard_map/ppermute | solution.py:696
  213.3 2.7 %shard_map.125 = (f32[3,16,8,128]{3,2,1,0:T(8,128)}, f32[3,16,8,128]{3,2,1,0:T(8,128)}) custom-call(f32[12,16,8,128]{3,2,1,0:T(8,128)} %get-tuple-element.87.final, f32[6,16,8,128]{3,2,1,0:T(8,128)} %copy-done.9, f32[4,6,16,8,128]{4,3,2,1,0:T(8,128)} %get-tuple-element.52.a6), custom_call_target="tpu_custom_call" | custom-call | flops 8000 | bytes 12000 | tf_op jit(solution)/shard_map/pallas_call | solution.py:52
  217.6 1.8 shard_map.118
  220.1 1.8 shard_map.126
  221.9 1.0 copy-done.4
  222.9 3.3 %shard_map.124 = f32[16,4,64,128]{3,2,1,0:T(8,128)} custom-call(f32[16,16,8,128]{3,2,1,0:T(8,128)} %get-tuple-element.85.own, f32[16,16,8,128]{3,2,1,0:T(8,128)} %copy-done.4), custom_call_target="tpu_custom_call" | custom-call | flops 32000 | bytes 48000 | tf_op jit(solution)/shard_map/pallas_call | solution.py:52
  (91 shorter events, 13.1 us)
Async XLA Ops:
  0.6 7.0 %copy-start.22 = (f32[12,64]{1,0:T(8,128)S(1)}, f32[12,64]{1,0:T(8,128)}, u32[]{:S(2)}) copy-start(f32[12,64]{1,0:T(8,128)} %param.17) | copy-start | bytes 9220
  4.0 6.1 %collective-permute-start = (f32[16,16,8,128]{3,2,1,0:T(8,128)}, f32[16,16,8,128]{3,2,1,0:T(8,128)S(1)}, u32[]{:S(2)}, u32[]{:S(2)}) collective-permute-start(f32[16,16,8,128]{3,2,1,0:T(8,128)} %get-tuple-element.48), channel_id=1, source_target_pairs={{0,1},{1,0},{2,3},{3,2},{4,5},{5,4},{6,7},{7,6},{8,9},{9,8},{10,11... | collective-permute-start | bytes 3145736 | tf_op jit(solution)/shard_map/ppermute | solution.py:692
  7.6 2.5 %collective-permute-start.1 = (f32[12,16,8,128]{3,2,1,0:T(8,128)}, f32[12,16,8,128]{3,2,1,0:T(8,128)S(1)}, u32[]{:S(2)}, u32[]{:S(2)}) collective-permute-start(f32[12,16,8,128]{3,2,1,0:T(8,128)} %get-tuple-element.50), channel_id=1, source_target_pairs={{0,1},{1,0},{2,3},{3,2},{4,5},{5,4},{6,7},{7,6},{8,9},{9,8},{10,11... | collective-permute-start | bytes 2359304 | tf_op jit(solution)/shard_map/ppermute | solution.py:692
  10.1 0.9 copy-start.6
  10.1 1.3 copy-start
  18.1 35.9 %collective-permute-start.2 = (f32[9,16,8,128]{3,2,1,0:T(8,128)}, f32[9,16,8,128]{3,2,1,0:T(8,128)S(1)}, u32[]{:S(2)}, u32[]{:S(2)}) collective-permute-start(f32[9,16,8,128]{3,2,1,0:T(8,128)} %get-tuple-element.53), channel_id=1, source_target_pairs={{0,2},{1,3},{2,0},{3,1},{4,6},{5,7},{6,4},{7,5},{8,10},{9,11},{10,... | collective-permute-start | bytes 1769480 | tf_op jit(solution)/shard_map/ppermute | solution.py:696
  24.2 54.9 %collective-permute-start.24 = (f32[16,16,8,128]{3,2,1,0:T(8,128)}, f32[16,16,8,128]{3,2,1,0:T(8,128)S(1)}, u32[]{:S(2)}, u32[]{:S(2)}) collective-permute-start(f32[16,16,8,128]{3,2,1,0:T(8,128)} %get-tuple-element.75), channel_id=1, source_target_pairs={{0,1},{1,0},{2,3},{3,2},{4,5},{5,4},{6,7},{7,6},{8,9},{9,8},{10,11... | collective-permute-start | bytes 3145736 | tf_op jit(solution)/shard_map/ppermute | solution.py:692
  24.6 29.3 %collective-permute-start.5 = (f32[31,3,8,128]{3,2,1,0:T(8,128)}, f32[31,3,8,128]{3,2,1,0:T(8,128)S(1)}, u32[]{:S(2)}, u32[]{:S(2)}) collective-permute-start(f32[31,3,8,128]{3,2,1,0:T(8,128)} %get-tuple-element.56), channel_id=1, source_target_pairs={{0,1},{1,0},{2,3},{3,2},{4,5},{5,4},{6,7},{7,6},{8,9},{9,8},{10,11... | collective-permute-start | bytes 1142792 | tf_op jit(solution)/shard_map/ppermute | solution.py:692
  24.7 29.2 %collective-permute-start.6 = (f32[31,3,8,128]{3,2,1,0:T(8,128)}, f32[31,3,8,128]{3,2,1,0:T(8,128)S(1)}, u32[]{:S(2)}, u32[]{:S(2)}) collective-permute-start(f32[31,3,8,128]{3,2,1,0:T(8,128)} %get-tuple-element.57), channel_id=1, source_target_pairs={{1,4},{4,1},{3,6},{6,3},{5,8},{8,5},{7,10},{10,7},{9,12},{12,9},{1... | collective-permute-start | bytes 1142792 | tf_op jit(solution)/shard_map/ppermute | solution.py:710
  27.2 18.4 %collective-permute-start.3 = (f32[9,3,8,128]{3,2,1,0:T(8,128)}, f32[9,3,8,128]{3,2,1,0:T(8,128)S(1)}, u32[]{:S(2)}, u32[]{:S(2)}) collective-permute-start(f32[9,3,8,128]{3,2,1,0:T(8,128)} %get-tuple-element.54), channel_id=1, source_target_pairs={{0,3},{1,2},{2,1},{3,0},{4,7},{5,6},{6,5},{7,4},{8,11},{9,10},{10,... | collective-permute-start | bytes 331784 | tf_op jit(solution)/shard_map/ppermute | solution.py:700
  45.7 8.3 %copy-start.15 = (f32[9,3,8,128]{3,2,1,0:T(8,128)}, f32[9,3,8,128]{3,2,1,0:T(8,128)S(1)}, u32[]{:S(2)}) copy-start(f32[9,3,8,128]{3,2,1,0:T(8,128)S(1)} %collective-permute-done.3.g_core_far) | copy-start | bytes 331780
  45.7 8.2 %collective-permute-start.4 = (f32[9,3,8,128]{3,2,1,0:T(8,128)}, f32[9,3,8,128]{3,2,1,0:T(8,128)S(1)}, u32[]{:S(2)}, u32[]{:S(2)}) collective-permute-start(f32[9,3,8,128]{3,2,1,0:T(8,128)} %get-tuple-element.55), channel_id=1, source_target_pairs={{1,6},{6,1},{3,4},{4,3},{5,10},{10,5},{7,8},{8,7},{9,14},{14,9},{1... | collective-permute-start | bytes 331784 | tf_op jit(solution)/shard_map/ppermute | solution.py:710
  53.9 0.8 copy-start.11
  53.9 0.9 copy-start.12
  53.9 1.1 copy-start.8
  62.3 5.7 %collective-permute-start.7 = (f32[2,18,8,128]{3,2,1,0:T(8,128)}, f32[2,18,8,128]{3,2,1,0:T(8,128)S(1)}, u32[]{:S(2)}, u32[]{:S(2)}) collective-permute-start(f32[2,18,8,128]{3,2,1,0:T(8,128)} %get-tuple-element.65), channel_id=1, source_target_pairs={{0,2},{1,3},{2,0},{3,1},{4,6},{5,7},{6,4},{7,5},{8,10},{9,11},{10,... | collective-permute-start | bytes 442376 | tf_op jit(solution)/shard_map/ppermute | solution.py:696
  72.5 5.2 %collective-permute-start.8 = (f32[2,8,128]{2,1,0:T(8,128)}, f32[2,8,128]{2,1,0:T(8,128)S(1)}, u32[]{:S(2)}, u32[]{:S(2)}) collective-permute-start(f32[2,8,128]{2,1,0:T(8,128)} %get-tuple-element.66), channel_id=1, source_target_pairs={{0,1},{1,0},{2,3},{3,2},{4,5},{5,4},{6,7},{7,6},{8,9},{9,8},{10,11... | collective-permute-start | bytes 24584 | tf_op jit(solution)/shard_map/ppermute | solution.py:692
  78.4 11.2 %collective-permute-start.10 = (f32[2,8,128]{2,1,0:T(8,128)S(1)}, f32[2,8,128]{2,1,0:T(8,128)S(1)}, u32[]{:S(2)}, u32[]{:S(2)}) collective-permute-start(f32[2,8,128]{2,1,0:T(8,128)S(1)} %pad_maximum_fusion), channel_id=1, source_target_pairs={{0,2},{1,3},{2,0},{3,1},{4,6},{5,7},{6,4},{7,5},{8,10},{9,11},{10,... | collective-permute-start | bytes 24584 | tf_op jit(solution)/shard_map/ppermute | solution.py:725
  79.1 10.5 %collective-permute-start.9 = (f32[2,8,128]{2,1,0:T(8,128)S(1)}, f32[2,8,128]{2,1,0:T(8,128)S(1)}, u32[]{:S(2)}, u32[]{:S(2)}) collective-permute-start(f32[2,8,128]{2,1,0:T(8,128)S(1)} %pad_maximum_fusion), channel_id=1, source_target_pairs={{0,4},{1,5},{2,6},{3,7},{4,0},{5,1},{6,2},{7,3},{8,12},{9,13},{10,... | collective-permute-start | bytes 24584 | tf_op jit(solution)/shard_map/ppermute | solution.py:725
  79.1 1.0 copy-start.1
  83.8 19.8 %collective-permute-start.25 = (f32[2,32,4,8,128]{4,3,2,1,0:T(8,128)}, f32[2,32,4,8,128]{4,3,2,1,0:T(8,128)S(1)}, u32[]{:S(2)}, u32[]{:S(2)}) collective-permute-start(f32[2,32,4,8,128]{4,3,2,1,0:T(8,128)} %get-tuple-element.76), channel_id=1, source_target_pairs={{0,1},{1,0},{2,3},{3,2},{4,5},{5,4},{6,7},{7,6},{8,9},{9,8},{10,11... | collective-permute-start | bytes 3145736 | tf_op jit(solution)/shard_map/ppermute | solution.py:692
  84.4 26.0 %collective-permute-start.26 = (f32[2,32,4,8,128]{4,3,2,1,0:T(8,128)}, f32[2,32,4,8,128]{4,3,2,1,0:T(8,128)S(1)}, u32[]{:S(2)}, u32[]{:S(2)}) collective-permute-start(f32[2,32,4,8,128]{4,3,2,1,0:T(8,128)} %get-tuple-element.77), channel_id=1, source_target_pairs={{1,4},{4,1},{3,6},{6,3},{5,8},{8,5},{7,10},{10,7},{9,12},{12,9},{1... | collective-permute-start | bytes 3145736 | tf_op jit(solution)/shard_map/ppermute | solution.py:710
  88.0 3.8 %collective-permute-start.11 = (f32[2,8,128]{2,1,0:T(8,128)S(1)}, f32[2,8,128]{2,1,0:T(8,128)S(1)}, u32[]{:S(2)}, u32[]{:S(2)}) collective-permute-start(f32[2,8,128]{2,1,0:T(8,128)S(1)} %pad_maximum_fusion), channel_id=1, source_target_pairs={{0,6},{1,7},{2,4},{3,5},{4,2},{5,3},{6,0},{7,1},{8,14},{9,15},{10,... | collective-permute-start | bytes 24584 | tf_op jit(solution)/shard_map/ppermute | solution.py:725
  91.8 3.9 %collective-permute-start.12 = (f32[2,8,128]{2,1,0:T(8,128)S(1)}, f32[2,8,128]{2,1,0:T(8,128)S(1)}, u32[]{:S(2)}, u32[]{:S(2)}) collective-permute-start(f32[2,8,128]{2,1,0:T(8,128)S(1)} %pad_maximum_fusion.1), channel_id=1, source_target_pairs={{0,8},{4,12},{8,0},{12,4},{16,24},{20,28},{24,16},{28,20},{32,40},... | collective-permute-start | bytes 24584 | tf_op jit(solution)/shard_map/ppermute | solution.py:730
  93.2 4.4 %collective-permute-start.13 = (f32[2,8,128]{2,1,0:T(8,128)S(1)}, f32[2,8,128]{2,1,0:T(8,128)S(1)}, u32[]{:S(2)}, u32[]{:S(2)}) collective-permute-start(f32[2,8,128]{2,1,0:T(8,128)S(1)} %pad_maximum_fusion.1), channel_id=1, source_target_pairs={{0,16},{4,20},{8,24},{12,28},{16,0},{20,4},{24,8},{28,12},{32,48},... | collective-permute-start | bytes 24584 | tf_op jit(solution)/shard_map/ppermute | solution.py:730
  95.5 4.1 %collective-permute-start.14 = (f32[2,8,128]{2,1,0:T(8,128)S(1)}, f32[2,8,128]{2,1,0:T(8,128)S(1)}, u32[]{:S(2)}, u32[]{:S(2)}) collective-permute-start(f32[2,8,128]{2,1,0:T(8,128)S(1)} %pad_maximum_fusion.1), channel_id=1, source_target_pairs={{0,24},{4,28},{8,16},{12,20},{16,8},{20,12},{24,0},{28,4},{32,56},... | collective-permute-start | bytes 24584 | tf_op jit(solution)/shard_map/ppermute | solution.py:730
  99.6 22.3 %collective-permute-start.15 = (f32[2,8,128]{2,1,0:T(8,128)S(1)}, f32[2,8,128]{2,1,0:T(8,128)S(1)}, u32[]{:S(2)}, u32[]{:S(2)}) collective-permute-start(f32[2,8,128]{2,1,0:T(8,128)S(1)} %pad_maximum_fusion.2), channel_id=1, source_target_pairs={{0,32},{4,36},{8,40},{12,44},{16,48},{20,52},{24,56},{28,60},{32,0... | collective-permute-start | bytes 24584 | tf_op jit(solution)/shard_map/ppermute | solution.py:730
  100.7 21.3 %collective-permute-start.16 = (f32[2,8,128]{2,1,0:T(8,128)S(1)}, f32[2,8,128]{2,1,0:T(8,128)S(1)}, u32[]{:S(2)}, u32[]{:S(2)}) collective-permute-start(f32[2,8,128]{2,1,0:T(8,128)S(1)} %pad_maximum_fusion.2), channel_id=1, source_target_pairs={{0,64},{4,68},{8,72},{12,76},{16,80},{20,84},{24,88},{28,92},{32,9... | collective-permute-start | bytes 24584 | tf_op jit(solution)/shard_map/ppermute | solution.py:730
  101.3 20.7 %collective-permute-start.17 = (f32[2,8,128]{2,1,0:T(8,128)S(1)}, f32[2,8,128]{2,1,0:T(8,128)S(1)}, u32[]{:S(2)}, u32[]{:S(2)}) collective-permute-start(f32[2,8,128]{2,1,0:T(8,128)S(1)} %pad_maximum_fusion.2), channel_id=1, source_target_pairs={{0,96},{4,100},{8,104},{12,108},{16,112},{20,116},{24,120},{28,124... | collective-permute-start | bytes 24584 | tf_op jit(solution)/shard_map/ppermute | solution.py:730
  103.6 6.8 %copy-start.2 = (f32[2,32,4,8,128]{4,3,2,1,0:T(8,128)}, f32[2,32,4,8,128]{4,3,2,1,0:T(8,128)S(1)}, u32[]{:S(2)}) copy-start(f32[2,32,4,8,128]{4,3,2,1,0:T(8,128)S(1)} %collective-permute-done.25.g_core) | copy-start | bytes 3145732
  110.4 1.0 copy-start.3
  117.8 26.7 %copy-start.21 = (f32[64,12]{0,1:T(8,128)S(1)}, f32[64,12]{0,1:T(8,128)}, u32[]{:S(2)}) copy-start(f32[64,12]{0,1:T(8,128)} %param.16) | copy-start | bytes 9220
  117.8 19.8 %collective-permute-start.27 = (f32[2,4,24,8,128]{4,3,2,1,0:T(8,128)}, f32[2,4,24,8,128]{4,3,2,1,0:T(8,128)S(1)}, u32[]{:S(2)}, u32[]{:S(2)}) collective-permute-start(f32[2,4,24,8,128]{4,3,2,1,0:T(8,128)} %get-tuple-element.79), channel_id=1, source_target_pairs={{0,2},{1,3},{2,0},{3,1},{4,6},{5,7},{6,4},{7,5},{8,10},{9,11},{10,... | collective-permute-start | bytes 2359304 | tf_op jit(solution)/shard_map/ppermute | solution.py:696
  127.4 36.4 %collective-permute-start.19 = (f32[6,16,8,128]{3,2,1,0:T(8,128)}, f32[6,16,8,128]{3,2,1,0:T(8,128)S(1)}, u32[]{:S(2)}, u32[]{:S(2)}) collective-permute-start(f32[6,16,8,128]{3,2,1,0:T(8,128)} %get-tuple-element.71.power), channel_id=1, source_target_pairs={{0,2},{1,3},{2,0},{3,1},{4,6},{5,7},{6,4},{7,5},{8,10},{9,11},{10,... | collective-permute-start | bytes 1179656 | tf_op jit(solution)/shard_map/ppermute | solution.py:696
  127.4 36.3 %collective-permute-start.20 = (f32[6,3,8,128]{3,2,1,0:T(8,128)}, f32[6,3,8,128]{3,2,1,0:T(8,128)S(1)}, u32[]{:S(2)}, u32[]{:S(2)}) collective-permute-start(f32[6,3,8,128]{3,2,1,0:T(8,128)} %get-tuple-element.72), channel_id=1, source_target_pairs={{0,1},{1,0},{2,3},{3,2},{4,5},{5,4},{6,7},{7,6},{8,9},{9,8},{10,11... | collective-permute-start | bytes 221192 | tf_op jit(solution)/shard_map/ppermute | solution.py:692
  130.2 33.5 %collective-permute-start.21 = (f32[6,3,8,128]{3,2,1,0:T(8,128)}, f32[6,3,8,128]{3,2,1,0:T(8,128)S(1)}, u32[]{:S(2)}, u32[]{:S(2)}) collective-permute-start(f32[6,3,8,128]{3,2,1,0:T(8,128)} %get-tuple-element.72), channel_id=1, source_target_pairs={{0,3},{1,2},{2,1},{3,0},{4,7},{5,6},{6,5},{7,4},{8,11},{9,10},{10,... | collective-permute-start | bytes 221192 | tf_op jit(solution)/shard_map/ppermute | solution.py:700
  133.2 30.5 %collective-permute-start.22 = (f32[6,3,8,128]{3,2,1,0:T(8,128)}, f32[6,3,8,128]{3,2,1,0:T(8,128)S(1)}, u32[]{:S(2)}, u32[]{:S(2)}) collective-permute-start(f32[6,3,8,128]{3,2,1,0:T(8,128)} %get-tuple-element.73), channel_id=1, source_target_pairs={{1,4},{4,1},{3,6},{6,3},{5,8},{8,5},{7,10},{10,7},{9,12},{12,9},{1... | collective-permute-start | bytes 221192 | tf_op jit(solution)/shard_map/ppermute | solution.py:710
  137.6 7.7 %copy-start.5 = (f32[2,4,24,8,128]{4,3,2,1,0:T(8,128)}, f32[2,4,24,8,128]{4,3,2,1,0:T(8,128)S(1)}, u32[]{:S(2)}) copy-start(f32[2,4,24,8,128]{4,3,2,1,0:T(8,128)S(1)} %collective-permute-done.27.g_far) | copy-start | bytes 2359300
  137.6 26.1 %collective-permute-start.23 = (f32[6,3,8,128]{3,2,1,0:T(8,128)}, f32[6,3,8,128]{3,2,1,0:T(8,128)S(1)}, u32[]{:S(2)}, u32[]{:S(2)}) collective-permute-start(f32[6,3,8,128]{3,2,1,0:T(8,128)} %get-tuple-element.73), channel_id=1, source_target_pairs={{1,6},{6,1},{3,4},{4,3},{5,10},{10,5},{7,8},{8,7},{9,14},{14,9},{1... | collective-permute-start | bytes 221192 | tf_op jit(solution)/shard_map/ppermute | solution.py:710
  163.8 0.7 copy-start.20
  163.8 0.8 copy-start.10
  164.5 36.2 %copy-start.23 = (f32[3,16,8,128]{3,2,1,0:T(8,128)S(1)}, f32[3,16,8,128]{3,2,1,0:T(8,128)}, u32[]{:S(2)}) copy-start(f32[3,16,8,128]{3,2,1,0:T(8,128)} %get-tuple-element.70) | copy-start | bytes 589828
  196.5 25.4 %collective-permute-start.28 = (f32[16,16,8,128]{3,2,1,0:T(8,128)}, f32[16,16,8,128]{3,2,1,0:T(8,128)S(1)}, u32[]{:S(2)}, u32[]{:S(2)}) collective-permute-start(f32[16,16,8,128]{3,2,1,0:T(8,128)} %get-tuple-element.86), channel_id=1, source_target_pairs={{0,1},{1,0},{2,3},{3,2},{4,5},{5,4},{6,7},{7,6},{8,9},{9,8},{10,11... | collective-permute-start | bytes 3145736 | tf_op jit(solution)/shard_map/ppermute | solution.py:692
  200.2 12.4 %collective-permute-start.29 = (f32[6,16,8,128]{3,2,1,0:T(8,128)}, f32[6,16,8,128]{3,2,1,0:T(8,128)S(1)}, u32[]{:S(2)}, u32[]{:S(2)}) collective-permute-start(f32[6,16,8,128]{3,2,1,0:T(8,128)} %get-tuple-element.88), channel_id=1, source_target_pairs={{0,2},{1,3},{2,0},{3,1},{4,6},{5,7},{6,4},{7,5},{8,10},{9,11},{10,... | collective-permute-start | bytes 1179656 | tf_op jit(solution)/shard_map/ppermute | solution.py:696
  200.7 16.2 %collective-permute-start.18 = (f32[3,16,8,128]{3,2,1,0:T(8,128)S(1)}, f32[3,16,8,128]{3,2,1,0:T(8,128)S(1)}, u32[]{:S(2)}, u32[]{:S(2)}) collective-permute-start(f32[3,16,8,128]{3,2,1,0:T(8,128)S(1)} %copy-done.23), channel_id=1, source_target_pairs={{0,1},{1,0},{2,3},{3,2},{4,5},{5,4},{6,7},{7,6},{8,9},{9,8},{10,11... | collective-permute-start | bytes 589832 | tf_op jit(solution)/shard_map/ppermute | solution.py:692
  212.6 0.7 copy-start.9
  216.0 3.4 %collective-permute-start.30 = (f32[3,16,8,128]{3,2,1,0:T(8,128)}, f32[3,16,8,128]{3,2,1,0:T(8,128)S(1)}, u32[]{:S(2)}, u32[]{:S(2)}) collective-permute-start(f32[3,16,8,128]{3,2,1,0:T(8,128)} %get-tuple-element.90), channel_id=1, source_target_pairs={{0,1},{1,0},{2,3},{3,2},{4,5},{5,4},{6,7},{7,6},{8,9},{9,8},{10,11... | collective-permute-start | bytes 589832 | tf_op jit(solution)/shard_map/ppermute | solution.py:692
  221.9 1.0 copy-start.4
  (7 other events, 4.6 us)

commit v2 on v1

--- a/solution.py
+++ b/solution.py
@@ -38,26 +38,30 @@
     return therm // 2, therm % 2
 
 
-def tile_spec(n):
-    return [pl.BlockSpec(memory_space=pltpu.VMEM)] * n
-
-
 def shaped(*dims):
     return jax.ShapeDtypeStruct(dims + (8, 128), F32)
 
 
-def call(kernel, outs, scratch=(), scalars=0, cost=0):
+def call(kernel, outs, scratch=(), scalars=0, cost=0, raw_in=False, raw_out=False, room=4):
+    def held(out):
+        return out if raw_out else pltpu.VMEM(out.shape, out.dtype)
+
     def run(*args):
         smem = [pl.BlockSpec(memory_space=pltpu.SMEM)] * scalars
+        fields = args[scalars:]
+        space = pltpu.HBM if raw_in else pltpu.VMEM
+        fields = [pltpu.with_memory_space_constraint(v, space) for v in fields]
+        own = [pltpu.VMEM(v.shape, v.dtype) for v in fields] if raw_in else []
+        own += [pltpu.SemaphoreType.DMA((4,))] if raw_in else []
         return pl.pallas_call(
             kernel,
-            out_shape=outs,
-            in_specs=smem + tile_spec(len(args) - scalars),
+            out_shape=jax.tree.map(held, outs),
+            in_specs=smem + [pl.BlockSpec(memory_space=space)] * len(fields),
             out_specs=jax.tree.map(lambda _: pl.BlockSpec(memory_space=pltpu.VMEM), outs),
-            scratch_shapes=[pltpu.VMEM(dims + (8, 128), F32) for dims in scratch],
-            compiler_params=pltpu.CompilerParams(vmem_limit_bytes=56 * 1024 * 1024),
-            cost_estimate=pl.CostEstimate(flops=cost * 2000, bytes_accessed=cost * 3000, transcendentals=0),
-        )(*args)
+            scratch_shapes=[pltpu.VMEM(dims + (8, 128), F32) for dims in scratch] + own,
+            compiler_params=pltpu.CompilerParams(vmem_limit_bytes=room * 1024 * 1024),
+            cost_estimate=pl.CostEstimate(flops=0, bytes_accessed=int(cost * 3.4e6), transcendentals=0),
+        )(*args[:scalars], *fields)
 
     return run
 
@@ -110,19 +114,40 @@
     return a * b * inverse(jnp.maximum(a + b, TINY))
 
 
-def pack_kernel(value, own, send):
+def pack_kernel(value, own, send, held, sems):
     _, core = place()
-
-    def body(n):
-        for row in range(ROWS):
-            own[n, row] = at_row(value, n, core, row)
-            send[n, row] = at_row(value, n, 1 - core, row)
-
-    loop(value.shape[0], body)
-
-
-def pack_args_kernel(classes, sink, category, link, contact, own, send):
+    parts = sems.shape[0]
+    size = value.shape[0] // parts
+    copies = [
+        pltpu.make_async_copy(value.at[pl.ds(p * size, size)], held.at[pl.ds(p * size, size)], sems.at[p])
+        for p in range(parts)
+    ]
+    for copy in copies:
+        copy.start()
+    for p, copy in enumerate(copies):
+        copy.wait()
+
+        def body(i, p=p):
+            n = p * size + i
+            for row in range(ROWS):
+                own[n, row] = at_row(held, n, core, row)
+                send[n, row] = at_row(held, n, 1 - core, row)
+
+        loop(size, body)
+
+
+def pack_args_kernel(classes, sink, category, link, contact, own, send, *held_sems):
     _, core = place()
+    held, sems = held_sems[:4], held_sems[4]
+    copies = [
+        pltpu.make_async_copy(ref, to, sems.at[p])
+        for p, (ref, to) in enumerate(zip((sink, category, link, contact), held))
+    ]
+    for copy in copies:
+        copy.start()
+    for copy in copies:
+        copy.wait()
+    sink, category, link, contact = held
 
     def body(n):
         for row in range(ROWS):
@@ -141,7 +166,7 @@
     loop(OWN, body)
 
 
-def weigh(weights, stride, parts, acc):
+def weigh(weights, parts, acc):
     def rows(block):
         total = [jnp.zeros((8, 128), F32)] * (4 * LAYERS)
         for ref, first, base in parts:
@@ -150,7 +175,7 @@
                 field = [ref[first + z, block * 4 + k] for k in range(4)]
                 out = []
                 for layer in range(LAYERS):
-                    w = weights[layer * stride + base + z]
+                    w = weights[layer, base + z]
                     out += [total[layer * 4 + k] + w * field[k] for k in range(4)]
                 return tuple(out)
 
@@ -162,14 +187,17 @@
     loop(ROWS // 4, rows)
 
 
-def heat_kernel(weights, t_own, t_got, a_own, a_got, part, a6, s_far, s_core_far, s_tile_far, s_core, s_tile):
+def heat_kernel(weights, t_own, t_got, part):
     far, core = place()
     weigh(
         weights,
-        DEPTHS,
         ((t_own, 0, SLAB * far + DEEP * core), (t_got, 0, SLAB * far + DEEP * (1 - core))),
         part,
     )
+
+
+def merge_kernel(part, a_own, a_got, a6, s_far, s_core_far, s_tile_far, s_core, s_tile):
+    far, core = place()
 
     def merge(n):
         for row in range(ROWS):
@@ -601,7 +629,7 @@
         def depth(n, carry):
             total = [zero] * 4
             for layer in range(LAYERS):
-                w = split[(base + n) * LAYERS + layer]
+                w = split[layer, base + n]
                 total = [total[k] + w * field[layer][k] for k in range(4)]
             for k in range(4):
                 source[n, block * 4 + k] = total[k]
@@ -641,7 +669,6 @@
     loop(DEEP, outs)
     weigh(
         weights,
-        DEPTHS,
         ((out, 0, SLAB * far + DEEP * core), (s_out, 0, SLAB * far + DEEP * (1 - core))),
         final,
     )
@@ -680,12 +707,12 @@
 def unpack(own, got):
     n = own.shape[0]
     out = jax.ShapeDtypeStruct((n, 4, 64, 128), F32)
-    return raw_back(call(unpack_kernel, out, cost=n)(own, got))
+    return raw_back(call(unpack_kernel, out, cost=n / 10, raw_out=True)(own, got))
 
 
 def pack(value):
     n = value.shape[0]
-    return call(pack_kernel, [shaped(n, ROWS)] * 2, cost=n)(raw_view(value))
+    return call(pack_kernel, [shaped(n, ROWS)] * 2, cost=2, raw_in=True)(raw_view(value))
 
 
 def to_core(value):
@@ -710,29 +737,38 @@
     return lax.ppermute(value, ("tile", "therm"), pairs)
 
 
-def total_of(values):
-    def add(a, b):
-        high, low = pair_add((a[0], a[1]), (b[0], b[1]))
-        return jnp.stack([high, low])
-
-    values = add(values, to_core(values))
-    x_peers = []
-    for bits in (1, 2, 3):
-        pairs = []
-        for t in range(lax.axis_size("tile")):
-            for h in range(4):
-                pairs.append((4 * t + h, 4 * (t ^ (bits & 1)) + (h ^ (bits & 2))))
-        x_peers.append(lax.ppermute(values, ("tile", "therm"), pairs))
-    for peer in x_peers:
-        values = add(values, peer)
-    for unit in (2, 8):
-        peers = [
-            lax.ppermute(values, "tile", [(t, t ^ (unit * k)) for t in range(lax.axis_size("tile"))])
-            for k in (1, 2, 3)
+def add_pairs(a, b):
+    high, low = pair_add((a[0], a[1]), (b[0], b[1]))
+    return jnp.stack([high, low])
+
+
+def along_core_and_x(values):
+    values = add_pairs(values, to_core(values))
+    peers = []
+    for bits in (2, 3, 1):
+        pairs = [
+            (4 * t + h, 4 * (t ^ (bits & 1)) + (h ^ (bits & 2)))
+            for t in range(lax.axis_size("tile"))
+            for h in range(4)
         ]
-        for peer in peers:
-            values = add(values, peer)
+        peers.append(lax.ppermute(values, ("tile", "therm"), pairs))
+    for peer in peers:
+        values = add_pairs(values, peer)
     return values
+
+
+def along_tile(values, unit):
+    peers = [
+        lax.ppermute(values, "tile", [(t, t ^ (unit * k)) for t in range(lax.axis_size("tile"))])
+        for k in (2, 1, 3)
+    ]
+    for peer in peers:
+        values = add_pairs(values, peer)
+    return values
+
+
+def tied(value, to):
+    return lax.optimization_barrier((value, to))[0]
 
 
 def per_device(
@@ -746,22 +782,18 @@
     dissipation_split,
     probe_weighting,
 ):
-    weights = probe_weighting.reshape(-1)
-    split = dissipation_split.reshape(-1)
+    weights, split = probe_weighting, dissipation_split.T
     t_own, t_send = pack(beginning_warmth)
     t_got = to_core(t_send)
-    a_own, a_send = call(pack_args_kernel, [shaped(4 * OWN, ROWS)] * 2, scalars=1, cost=12)(
+    a_own, a_send = call(pack_args_kernel, [shaped(4 * OWN, ROWS)] * 2, scalars=1, cost=3, raw_in=True)(
         baseline_admittance,
         *[raw_view(v) for v in (sink_current, metal_category, upward_link_flag, supply_contact_flag)],
     )
     a_got = to_core(a_send)
-    k_own, k_send = pack(cell_diffusivity)
-    k_got = to_core(k_send)
-
-    part, a6, s_far, s_core_far, s_tile_far, s_core, s_tile = call(
-        heat_kernel,
+    part = call(heat_kernel, shaped(LAYERS, ROWS), scalars=1, cost=3, room=2)(weights, t_own, t_got)
+    a6, s_far, s_core_far, s_tile_far, s_core, s_tile = call(
+        merge_kernel,
         [
-            shaped(LAYERS, ROWS),
             shaped(4, HALF, ROWS),
             shaped(HEATED + 2, ROWS),
             shaped(HEATED + 2, RIM),
@@ -769,14 +801,16 @@
             shaped(HEATED + 4 * HALF, RIM),
             shaped(HEATED + 4 * HALF, RIM),
         ],
-        scalars=1,
-        cost=24,
-    )(weights, t_own, t_got, a_own, a_got)
+        cost=1.5,
+        room=2,
+    )(part, a_own, a_got)
     g_far = to_far(s_far)
     g_tile = to_tile(s_tile)
     g_tile_far = to_tile(s_tile_far, 1)
     g_core_far = to_core_far(s_core_far)
     g_core = to_core(s_core)
+
+    k_own, k_send = pack(tied(cell_diffusivity, s_far))
 
     field = shaped(HALF + 2, EXT)
     coef = shaped(HALF, EXT)
@@ -784,32 +818,36 @@
         basis_kernel,
         [field, field, field, coef, coef, coef, shaped(HALF + 1, EXT), coef, shaped(2, EXT - 4)],
         scratch=((HEATED, EXT), (HALF, EXT)),
-        cost=16,
+        cost=3,
     )(part, a6, g_far, g_core_far, g_tile_far, g_core, g_tile)
     g_basis = to_far(s_basis)
-    w2, sums = call(moments_kernel, [field, shaped(2)], cost=10)(
-        v0, v1, v2, diag, row_edge, col_edge, vert, g_basis
-    )
-    total = total_of(sums)
-
+    k_got = to_core(tied(k_send, s_basis))
     rim = shaped(2, SLAB, SWEEPS)
-    k_core, k_tile = call(slab_rim_kernel, [rim, rim], cost=8)(t_own, t_got, k_own, k_got)
-    wide, s_deep = call(slab_wide_kernel, [shaped(2, SLAB, WIDE), shaped(2, SWEEPS, WIDE)], cost=24)(
+    k_core, k_tile = call(slab_rim_kernel, [rim, rim], cost=0.4)(t_own, t_got, k_own, k_got)
+    wide, s_deep = call(slab_wide_kernel, [shaped(2, SLAB, WIDE), shaped(2, SWEEPS, WIDE)], cost=0.6)(
         t_own, t_got, k_own, k_got, to_core(k_core), to_tile(k_tile)
     )
+    w2, sums = call(moments_kernel, [field, shaped(2)], cost=0.9)(
+        tied(v0, k_tile), v1, v2, diag, row_edge, col_edge, vert, g_basis
+    )
+    values = along_core_and_x(sums)
+    values, s_deep = lax.optimization_barrier((values, s_deep))
+    values = along_tile(values, 2)
+    total = along_tile(values, 8)
     thick = shaped(THICK, WIDE)
     warm, deep_edge, row_heat, col_heat, turn = call(
         slab_edges_kernel,
         [shaped(THICK + 2, WIDE), shaped(THICK + 1, WIDE), thick, thick, thick],
         scratch=((THICK, WIDE),),
-        cost=64,
+        cost=9.5,
+        room=5,
     )(wide, to_far(s_deep))
 
     power, p_core, p_tile, loss, s_loss = call(
         power_kernel,
         [shaped(HALF, ROWS), shaped(HALF, RIM), shaped(HALF, RIM), shaped(OWN, ROWS), shaped(OWN, ROWS)],
         scratch=((HALF + 2, EXT),),
-        cost=10,
+        cost=1.4,
     )(total, v0, v1, w2, diag, row_edge, col_edge, vert, ground, g_basis)
     p_far = to_far(power)
     q_tile = to_tile(p_tile)
@@ -823,11 +861,13 @@
         [shaped(DEEP, ROWS), shaped(DEEP, ROWS), shaped(LAYERS, ROWS), shaped(HALF, ROWS)],
         scratch=((LAYERS, WIDE), (THICK, WIDE), (THICK + 2, WIDE), (THICK + 2, WIDE)),
         scalars=2,
-        cost=128,
+        cost=25,
+        room=14,
     )(split, weights, power, p_far, q_core, q_core_far, q_tile, q_tile_far, warm, deep_edge, row_heat, col_heat, turn)
     g_final = to_far(s_final)
     final_warmth = unpack(out, to_core(s_out))
-    mine, s_mine = call(update_kernel, [shaped(OWN, ROWS)] * 2, cost=4)(final, g_final, a6)
+    g_final = tied(g_final, final_warmth)
+    mine, s_mine = call(update_kernel, [shaped(OWN, ROWS)] * 2, cost=0.4)(final, g_final, a6)
     updated_admittance = unpack(mine, to_core(s_mine))
     return voltage_loss, final_warmth, updated_admittance
 

time: 227 us -> 164 us (0.72)
  Pallas kernels: 102 us -> 53.7 us
  local copies, waits for them, and re-layouts: 10.4 us -> 0.67 us
  waiting for transfers between devices: 51.4 us -> 48.2 us
    pallas_call x15 -> x16, Pallas kernels: 102 us -> 53.7 us  [run(): pl.pallas_call(kernel, out_shape=jax.tree.map(held, outs), in_specs=smem...]
    ppermute x9, waiting for transfers between devices: 6 us -> 20.7 us  [the longest x3 16.5 us: along_core_and_x(): peers.append(lax.ppermute(values, ('tile', 'therm'), pairs))]
    ppermute x5, waiting for transfers between devices: 11 us -> 0.01 us  [to_tile(): return lax.ppermute(value, ('tile', 'therm'), pairs)]
    unnamed x49 -> x6, local copies, waits for them, and re-layouts: 9.04 us -> 0.67 us
    ppermute x10, starting transfers between devices: 13.6 us -> 7.56 us  [to_core(): return lax.ppermute(value, 'therm', [(i, i ^ 1) for i in range(4)])]
    ppermute x5, waiting for transfers between devices: 18.6 us -> 13.5 us  [to_far(): return lax.ppermute(value, 'therm', [(i, i ^ 2) for i in range(4)])]
    ppermute x2, starting transfers between devices: 8.51 us -> 12.1 us  [to_core_far(): return lax.ppermute(value, 'therm', [(i, i ^ 3) for i in range(4)])]
  transfers between devices with their start and end apart: 31 -> 31, of which waited for: 11 -> 11; matrix products, arithmetic and copies ran while one was open for 1% -> 0% of each run, Pallas kernels for 25% -> 13%
where the time goes in v2:
time: 164 us; the launch traced here: 162 us
  starting transfers between devices  58.8 us (36%)
  Pallas kernels  53.7 us (33%)
  waiting for transfers between devices  48.2 us (29%)
    pallas_call x16, Pallas kernels, run(): pl.pallas_call(kernel, out_shape=jax.tree.map(held, outs), in_specs=smem...  53.7 us
    ppermute x5, starting transfers between devices, to_tile(): return lax.ppermute(value, ('tile', 'therm'), pairs)  18.5 us
    ppermute x3, waiting for transfers between devices, along_core_and_x(): peers.append(lax.ppermute(values, ('tile', 'therm'), pairs))  16.5 us
    ppermute x5, waiting for transfers between devices, to_far(): return lax.ppermute(value, 'therm', [(i, i ^ 2) for i in range(4)])  13.5 us
    ppermute x2, waiting for transfers between devices, to_core_far(): return lax.ppermute(value, 'therm', [(i, i ^ 3) for i in range(4)])  12.3 us
    ppermute x2, starting transfers between devices, to_core_far(): return lax.ppermute(value, 'therm', [(i, i ^ 3) for i in range(4)])  12.1 us
    ppermute x6, starting transfers between devices, along_tile(): lax.ppermute(values, 'tile', [(t, t ^ unit * k) for t in range(lax.axis_s...  8.77 us
    ppermute x5, starting transfers between devices, to_far(): return lax.ppermute(value, 'therm', [(i, i ^ 2) for i in range(4)])  8.51 us
  transfers between devices with their start and end apart: 31, of which 11 were waited for; matrix products, arithmetic and copies ran while one was open for 0% of the time, Pallas kernels for 13%

profile of v2, /device:TPU:25, one launch (start us, length us, event | category | flops | bytes accessed | tf_op | source)
XLA Modules:
  0.0 162.5 jit_solution(8509865691029078264)
XLA Ops:
  0.6 1.7 %shard_map.112 = (f32[16,16,8,128]{3,2,1,0:T(8,128)S(1)}, f32[16,16,8,128]{3,2,1,0:T(8,128)S(1)}) custom-call(f32[16,4,64,128]{3,2,1,0:T(8,128)} %bitcast.47), custom_call_target="tpu_custom_call" | custom-call | bytes 6800000 | tf_op jit(solution)/shard_map/pallas_call | solution.py:56
  2.3 0.8 collective-permute-start
  3.1 0.7 copy-done.2
  3.7 2.3 %shard_map.114 = (f32[12,16,8,128]{3,2,1,0:T(8,128)S(1)}, f32[12,16,8,128]{3,2,1,0:T(8,128)S(1)}) custom-call(f32[8]{0:T(128)S(1)} %copy-done.2, f32[3,4,64,128]{3,2,1,0:T(8,128)} %bitcast.52, s32[3,4,64,128]{3,2,1,0:T(8,128)} %bitcast.53, s32[3,4,64,128]{3,2,1,0:T(8,128)} %bitcast.54, s32[3,4,64,128]{3,2,1,0:T(8,128)} %bitcast.55), custom_call_target="tpu_custom_call" | custom-call | bytes 10200000 | tf_op jit(solution)/shard_map/pallas_call | solution.py:56
  6.2 3.0 %shard_map.113.part = f32[12,16,8,128]{3,2,1,0:T(8,128)S(1)} custom-call(f32[12,64]{1,0:T(8,128)S(1)} %copy-done, f32[16,16,8,128]{3,2,1,0:T(8,128)S(1)} %get-tuple-element.52.t_own, f32[16,16,8,128]{3,2,1,0:T(8,128)S(1)} %collective-permute-done.t_got), custom_call_target="tpu_custom_call" | custom-call | bytes 10200000 | tf_op jit(solution)/shard_map/pallas_call | solution.py:56
  9.6 2.8 %collective-permute-start.2 = (f32[9,16,8,128]{3,2,1,0:T(8,128)S(1)}, f32[9,16,8,128]{3,2,1,0:T(8,128)S(1)}, u32[]{:S(2)}, u32[]{:S(2)}) collective-permute-start(f32[9,16,8,128]{3,2,1,0:T(8,128)S(1)} %get-tuple-element.57), channel_id=1, source_target_pairs={{0,2},{1,3},{2,0},{3,1},{4,6},{5,7},{6,4},{7,5},{8,10},{9,11},{10,... | collective-permute-start | bytes 1769480 | tf_op jit(solution)/shard_map/ppermute | solution.py:723
  12.4 0.8 collective-permute-start.5
  13.1 2.1 %collective-permute-start.6 = (f32[31,3,8,128]{3,2,1,0:T(8,128)S(1)}, f32[31,3,8,128]{3,2,1,0:T(8,128)S(1)}, u32[]{:S(2)}, u32[]{:S(2)}) collective-permute-start(f32[31,3,8,128]{3,2,1,0:T(8,128)S(1)} %get-tuple-element.61), channel_id=1, source_target_pairs={{1,4},{4,1},{3,6},{6,3},{5,8},{8,5},{7,10},{10,7},{9,12},{12,9},{1... | collective-permute-start | bytes 1142792 | tf_op jit(solution)/shard_map/ppermute | solution.py:737
  15.3 5.9 %collective-permute-start.3 = (f32[9,3,8,128]{3,2,1,0:T(8,128)S(1)}, f32[9,3,8,128]{3,2,1,0:T(8,128)S(1)}, u32[]{:S(2)}, u32[]{:S(2)}) collective-permute-start(f32[9,3,8,128]{3,2,1,0:T(8,128)S(1)} %get-tuple-element.58), channel_id=1, source_target_pairs={{0,3},{1,2},{2,1},{3,0},{4,7},{5,6},{6,5},{7,4},{8,11},{9,10},{10,... | collective-permute-start | bytes 331784 | tf_op jit(solution)/shard_map/ppermute | solution.py:727
  21.1 1.9 %collective-permute-start.4 = (f32[9,3,8,128]{3,2,1,0:T(8,128)S(1)}, f32[9,3,8,128]{3,2,1,0:T(8,128)S(1)}, u32[]{:S(2)}, u32[]{:S(2)}) collective-permute-start(f32[9,3,8,128]{3,2,1,0:T(8,128)S(1)} %get-tuple-element.59), channel_id=1, source_target_pairs={{1,6},{6,1},{3,4},{4,3},{5,10},{10,5},{7,8},{8,7},{9,14},{14,9},{1... | collective-permute-start | bytes 331784 | tf_op jit(solution)/shard_map/ppermute | solution.py:737
  23.0 1.7 %shard_map.117 = (f32[16,16,8,128]{3,2,1,0:T(8,128)S(1)}, f32[16,16,8,128]{3,2,1,0:T(8,128)S(1)}) custom-call(f32[16,4,64,128]{3,2,1,0:T(8,128)} %bitcast.48), custom_call_target="tpu_custom_call" | custom-call | bytes 6800000 | tf_op jit(solution)/shard_map/pallas_call | solution.py:56
  24.7 12.3 %collective-permute-done.3.g_core_far = f32[9,3,8,128]{3,2,1,0:T(8,128)S(1)} collective-permute-done((f32[9,3,8,128]{3,2,1,0:T(8,128)S(1)}, f32[9,3,8,128]{3,2,1,0:T(8,128)S(1)}, u32[]{:S(2)}, u32[]{:S(2)}) %collective-permute-start.3) | collective-permute-done | bytes 110624 | tf_op jit(solution)/shard_map/ppermute | solution.py:727
  37.1 3.1 %shard_map.116 = (f32[8,22,8,128]{3,2,1,0:T(8,128)S(1)}, f32[8,22,8,128]{3,2,1,0:T(8,128)S(1)}, f32[8,22,8,128]{3,2,1,0:T(8,128)S(1)}, f32[6,22,8,128]{3,2,1,0:T...) custom-call(f32[12,16,8,128]{3,2,1,0:T(8,128)S(1)} %shard_map.113.pa, ...), custom_call_target="tpu_custom_call" | custom-call | bytes 10200000 | tf_op jit(solution)/shard_map/pallas_call | solution.py:56
  40.2 0.9 collective-permute-start.7
  41.1 1.7 %collective-permute-start.8 = (f32[2,18,8,128]{3,2,1,0:T(8,128)S(1)}, f32[2,18,8,128]{3,2,1,0:T(8,128)S(1)}, u32[]{:S(2)}, u32[]{:S(2)}) collective-permute-start(f32[2,18,8,128]{3,2,1,0:T(8,128)S(1)} %get-tuple-element.66), channel_id=1, source_target_pairs={{0,2},{1,3},{2,0},{3,1},{4,6},{5,7},{6,4},{7,5},{8,10},{9,11},{10,... | collective-permute-start | bytes 442376 | tf_op jit(solution)/shard_map/ppermute | solution.py:723
  44.1 2.4 %collective-permute-start.14 = (f32[2,32,4,8,128]{4,3,2,1,0:T(8,128)S(1)}, f32[2,32,4,8,128]{4,3,2,1,0:T(8,128)S(1)}, u32[]{:S(2)}, u32[]{:S(2)}) collective-permute-start(f32[2,32,4,8,128]{4,3,2,1,0:T(8,128)S(1)} %get-tuple-element.68), channel_id=1, source_target_pairs={{1,4},{4,1},{3,6},{6,3},{5,8},{8,5},{7,10},{10,7},{9,12},{12,9},{1... | collective-permute-start | bytes 3145736 | tf_op jit(solution)/shard_map/ppermute | solution.py:737
  46.4 1.6 collective-permute-done.8.got
  48.0 0.9 shard_map.119
  48.9 2.4 %collective-permute-start.9 = (f32[2,8,128]{2,1,0:T(8,128)S(1)}, f32[2,8,128]{2,1,0:T(8,128)S(1)}, u32[]{:S(2)}, u32[]{:S(2)}) collective-permute-start(f32[2,8,128]{2,1,0:T(8,128)S(1)} %get-tuple-element.76), channel_id=1, source_target_pairs={{0,1},{1,0},{2,3},{3,2},{4,5},{5,4},{6,7},{7,6},{8,9},{9,8},{10,11... | collective-permute-start | bytes 24584 | tf_op jit(solution)/shard_map/ppermute | solution.py:719
  51.3 0.8 collective-permute-done.9
  52.2 2.7 %collective-permute-start.11 = (f32[2,8,128]{2,1,0:T(8,128)S(1)}, f32[2,8,128]{2,1,0:T(8,128)S(1)}, u32[]{:S(2)}, u32[]{:S(2)}) collective-permute-start(f32[2,8,128]{2,1,0:T(8,128)S(1)} %pad_maximum_fusion), channel_id=1, source_target_pairs={{0,6},{1,7},{2,4},{3,5},{4,2},{5,3},{6,0},{7,1},{8,14},{9,15},{10,... | collective-permute-start | bytes 24584 | tf_op jit(solution)/shard_map/ppermute | solution.py:754
  55.4 16.5 %collective-permute-done.12 = f32[2,8,128]{2,1,0:T(8,128)S(1)} collective-permute-done((f32[2,8,128]{2,1,0:T(8,128)S(1)}, f32[2,8,128]{2,1,0:T(8,128)S(1)}, u32[]{:S(2)}, u32[]{:S(2)}) %collective-permute-start.12) | collective-permute-done | bytes 8224 | tf_op jit(solution)/shard_map/ppermute | solution.py:754
  72.0 0.7 shard_map.120
  72.7 2.3 %collective-permute-start.16 = (f32[2,8,128]{2,1,0:T(8,128)S(1)}, f32[2,8,128]{2,1,0:T(8,128)S(1)}, u32[]{:S(2)}, u32[]{:S(2)}) collective-permute-start(f32[2,8,128]{2,1,0:T(8,128)S(1)} %pad_maximum_fusion.1), channel_id=1, source_target_pairs={{0,8},{4,12},{8,0},{12,4},{16,24},{20,28},{24,16},{28,20},{32,40},... | collective-permute-start | bytes 24584 | tf_op jit(solution)/shard_map/ppermute | solution.py:762
  75.1 2.1 %collective-permute-start.15 = (f32[2,8,128]{2,1,0:T(8,128)S(1)}, f32[2,8,128]{2,1,0:T(8,128)S(1)}, u32[]{:S(2)}, u32[]{:S(2)}) collective-permute-start(f32[2,8,128]{2,1,0:T(8,128)S(1)} %pad_maximum_fusion.1), channel_id=1, source_target_pairs={{0,16},{4,20},{8,24},{12,28},{16,0},{20,4},{24,8},{28,12},{32,48},... | collective-permute-start | bytes 24584 | tf_op jit(solution)/shard_map/ppermute | solution.py:762
  77.5 1.5 collective-permute-done.15
  79.1 1.8 %collective-permute-done.17 = f32[2,8,128]{2,1,0:T(8,128)S(1)} collective-permute-done((f32[2,8,128]{2,1,0:T(8,128)S(1)}, f32[2,8,128]{2,1,0:T(8,128)S(1)}, u32[]{:S(2)}, u32[]{:S(2)}) %collective-permute-start.17) | collective-permute-done | bytes 8224 | tf_op jit(solution)/shard_map/ppermute | solution.py:762
  80.9 1.1 collective-permute-start.20
  82.0 0.7 collective-permute-start.19
  82.7 2.1 %collective-permute-start.18 = (f32[2,8,128]{2,1,0:T(8,128)S(1)}, f32[2,8,128]{2,1,0:T(8,128)S(1)}, u32[]{:S(2)}, u32[]{:S(2)}) collective-permute-start(f32[2,8,128]{2,1,0:T(8,128)S(1)} %pad_maximum_fusion.2), channel_id=1, source_target_pairs={{0,64},{4,68},{8,72},{12,76},{16,80},{20,84},{24,88},{28,92},{32,9... | collective-permute-start | bytes 24584 | tf_op jit(solution)/shard_map/ppermute | solution.py:762
  84.9 1.0 collective-permute-start.27
  85.9 0.8 collective-permute-done.18
  86.8 1.4 shard_map.121
  88.2 1.2 collective-permute-start.22
  89.4 6.3 %collective-permute-start.24 = (f32[6,3,8,128]{3,2,1,0:T(8,128)S(1)}, f32[6,3,8,128]{3,2,1,0:T(8,128)S(1)}, u32[]{:S(2)}, u32[]{:S(2)}) collective-permute-start(f32[6,3,8,128]{3,2,1,0:T(8,128)S(1)} %get-tuple-element.85), channel_id=1, source_target_pairs={{0,3},{1,2},{2,1},{3,0},{4,7},{5,6},{6,5},{7,4},{8,11},{9,10},{10,... | collective-permute-start | bytes 221192 | tf_op jit(solution)/shard_map/ppermute | solution.py:727
  95.7 2.6 %collective-permute-start.26 = (f32[6,3,8,128]{3,2,1,0:T(8,128)S(1)}, f32[6,3,8,128]{3,2,1,0:T(8,128)S(1)}, u32[]{:S(2)}, u32[]{:S(2)}) collective-permute-start(f32[6,3,8,128]{3,2,1,0:T(8,128)S(1)} %get-tuple-element.86), channel_id=1, source_target_pairs={{1,6},{6,1},{3,4},{4,3},{5,10},{10,5},{7,8},{8,7},{9,14},{14,9},{1... | collective-permute-start | bytes 221192 | tf_op jit(solution)/shard_map/ppermute | solution.py:737
  98.3 3.9 %collective-permute-done.27.g_far = f32[2,4,24,8,128]{4,3,2,1,0:T(8,128)S(1)} collective-permute-done((f32[2,4,24,8,128]{4,3,2,1,0:T(8,128)S(1)}, f32[2,4,24,8,128]{4,3,2,1,0:T(8,128)S(1)}, u32[]{:S(2)}, u32[]{:S(2)}) %collective-permute-start.27) | collective-permute-done | bytes 786464 | tf_op jit(solution)/shard_map/ppermute | solution.py:723
  102.1 9.6 %collective-permute-start.25 = (f32[6,3,8,128]{3,2,1,0:T(8,128)S(1)}, f32[6,3,8,128]{3,2,1,0:T(8,128)S(1)}, u32[]{:S(2)}, u32[]{:S(2)}) collective-permute-start(f32[6,3,8,128]{3,2,1,0:T(8,128)S(1)} %get-tuple-element.86), channel_id=1, source_target_pairs={{1,4},{4,1},{3,6},{6,3},{5,8},{8,5},{7,10},{10,7},{9,12},{12,9},{1... | collective-permute-start | bytes 221192 | tf_op jit(solution)/shard_map/ppermute | solution.py:737
  111.7 9.5 %shard_map.123 = (f32[38,24,8,128]{3,2,1,0:T(8,128)S(1)}, f32[37,24,8,128]{3,2,1,0:T(8,128)S(1)}, f32[36,24,8,128]{3,2,1,0:T(8,128)S(1)}, f32[36,24,8,128]{3,2,1,0:T(8,128)S(1)}, f32[36,24,8,128]{3,2,1,0:T(8,128)S(1)}) custom-call(f32[2,32,24,8,128]{4,3,2,1,0:T(8,128)S(1)} %get-tuple-element.87.wide, f32[2,4,24,8,128]{4,3,2,1,0:T(8,128)S(1)} %collective-permute-done.27.g_far), custom_call_target="tpu_custom_call" | custom-call | bytes 32300000 | tf_op jit(solution)/shard_map/pallas_call | solution.py:56
  121.3 25.4 %shard_map.124 = (f32[16,16,8,128]{3,2,1,0:T(8,128)S(1)}, f32[16,16,8,128]{3,2,1,0:T(8,128)S(1)}, f32[12,16,8,128]{3,2,1,0:T(8,128)S(1)}, f32[6,16,8,128]{3,2,1,0:T(8,128)S(1)}) custom-call(f32[12,64]{1,0:T(8,128)S(1)} %bitcast.46, f32[12,64]{1,0:T(8,128)S(1)} %copy-done, f32[6,16,8,128]{3,2,1,0:T(8,128)S(1)} %get-tuple-element.84.power, ...), custom_call_target="tpu_custom_call" | custom-call | bytes 85000000 | tf_op jit(solution)/shard_map/pallas_call | solution.py:56
  146.7 0.6 collective-permute-start.28
  147.3 1.7 %collective-permute-start.29 = (f32[6,16,8,128]{3,2,1,0:T(8,128)S(1)}, f32[6,16,8,128]{3,2,1,0:T(8,128)S(1)}, u32[]{:S(2)}, u32[]{:S(2)}) collective-permute-start(f32[6,16,8,128]{3,2,1,0:T(8,128)S(1)} %get-tuple-element.97), channel_id=1, source_target_pairs={{0,2},{1,3},{2,0},{3,1},{4,6},{5,7},{6,4},{7,5},{8,10},{9,11},{10,... | collective-permute-start | bytes 1179656 | tf_op jit(solution)/shard_map/ppermute | solution.py:723
  149.0 0.7 collective-permute-start.21
  149.7 1.7 %shard_map.125 = f32[16,4,64,128]{3,2,1,0:T(8,128)} custom-call(f32[16,16,8,128]{3,2,1,0:T(8,128)S(1)} %get-tuple-element.94.own, f32[16,16,8,128]{3,2,1,0:T(8,128)S(1)} %collective-permute-done.28.got), custom_call_target="tpu_custom_call" | custom-call | bytes 5440000 | tf_op jit(solution)/shard_map/pallas_call | solution.py:56
  151.4 8.1 %collective-permute-done.29.got = f32[6,16,8,128]{3,2,1,0:T(8,128)S(1)} collective-permute-done((f32[6,16,8,128]{3,2,1,0:T(8,128)S(1)}, f32[6,16,8,128]{3,2,1,0:T(8,128)S(1)}, u32[]{:S(2)}, u32[]{:S(2)}) %collective-permute-start.29) | collective-permute-done | bytes 393248 | tf_op jit(solution)/shard_map/ppermute | solution.py:723
  159.7 1.0 collective-permute-start.30
  160.6 0.8 shard_map.122
  161.7 0.8 shard_map.127
  (48 shorter events, 3.3 us)
Async XLA Ops:
  0.6 5.5 %copy-start = (f32[12,64]{1,0:T(8,128)S(1)}, f32[12,64]{1,0:T(8,128)}, u32[]{:S(2)}) copy-start(f32[12,64]{1,0:T(8,128)} %weights.3) | copy-start | bytes 9220
  2.3 3.8 %collective-permute-start = (f32[16,16,8,128]{3,2,1,0:T(8,128)S(1)}, f32[16,16,8,128]{3,2,1,0:T(8,128)S(1)}, u32[]{:S(2)}, u32[]{:S(2)}) collective-permute-start(f32[16,16,8,128]{3,2,1,0:T(8,128)S(1)} %get-tuple-element.53), channel_id=1, source_target_pairs={{0,1},{1,0},{2,3},{3,2},{4,5},{5,4},{6,7},{7,6},{8,9},{9,8},{10,11... | collective-permute-start | bytes 3145736 | tf_op jit(solution)/shard_map/ppermute | solution.py:719
  3.1 0.7 copy-start.2
  6.1 3.1 %collective-permute-start.1 = (f32[12,16,8,128]{3,2,1,0:T(8,128)S(1)}, f32[12,16,8,128]{3,2,1,0:T(8,128)S(1)}, u32[]{:S(2)}, u32[]{:S(2)}) collective-permute-start(f32[12,16,8,128]{3,2,1,0:T(8,128)S(1)} %get-tuple-element.55), channel_id=1, source_target_pairs={{0,1},{1,0},{2,3},{3,2},{4,5},{5,4},{6,7},{7,6},{8,9},{9,8},{10,11... | collective-permute-start | bytes 2359304 | tf_op jit(solution)/shard_map/ppermute | solution.py:719
  9.6 27.5 %collective-permute-start.2 = (f32[9,16,8,128]{3,2,1,0:T(8,128)S(1)}, f32[9,16,8,128]{3,2,1,0:T(8,128)S(1)}, u32[]{:S(2)}, u32[]{:S(2)}) collective-permute-start(f32[9,16,8,128]{3,2,1,0:T(8,128)S(1)} %get-tuple-element.57), channel_id=1, source_target_pairs={{0,2},{1,3},{2,0},{3,1},{4,6},{5,7},{6,4},{7,5},{8,10},{9,11},{10,... | collective-permute-start | bytes 1769480 | tf_op jit(solution)/shard_map/ppermute | solution.py:723
  12.4 24.6 %collective-permute-start.5 = (f32[31,3,8,128]{3,2,1,0:T(8,128)S(1)}, f32[31,3,8,128]{3,2,1,0:T(8,128)S(1)}, u32[]{:S(2)}, u32[]{:S(2)}) collective-permute-start(f32[31,3,8,128]{3,2,1,0:T(8,128)S(1)} %get-tuple-element.60), channel_id=1, source_target_pairs={{0,1},{1,0},{2,3},{3,2},{4,5},{5,4},{6,7},{7,6},{8,9},{9,8},{10,11... | collective-permute-start | bytes 1142792 | tf_op jit(solution)/shard_map/ppermute | solution.py:719
  13.1 23.9 %collective-permute-start.6 = (f32[31,3,8,128]{3,2,1,0:T(8,128)S(1)}, f32[31,3,8,128]{3,2,1,0:T(8,128)S(1)}, u32[]{:S(2)}, u32[]{:S(2)}) collective-permute-start(f32[31,3,8,128]{3,2,1,0:T(8,128)S(1)} %get-tuple-element.61), channel_id=1, source_target_pairs={{1,4},{4,1},{3,6},{6,3},{5,8},{8,5},{7,10},{10,7},{9,12},{12,9},{1... | collective-permute-start | bytes 1142792 | tf_op jit(solution)/shard_map/ppermute | solution.py:737
  15.3 21.8 %collective-permute-start.3 = (f32[9,3,8,128]{3,2,1,0:T(8,128)S(1)}, f32[9,3,8,128]{3,2,1,0:T(8,128)S(1)}, u32[]{:S(2)}, u32[]{:S(2)}) collective-permute-start(f32[9,3,8,128]{3,2,1,0:T(8,128)S(1)} %get-tuple-element.58), channel_id=1, source_target_pairs={{0,3},{1,2},{2,1},{3,0},{4,7},{5,6},{6,5},{7,4},{8,11},{9,10},{10,... | collective-permute-start | bytes 331784 | tf_op jit(solution)/shard_map/ppermute | solution.py:727
  21.1 15.9 %collective-permute-start.4 = (f32[9,3,8,128]{3,2,1,0:T(8,128)S(1)}, f32[9,3,8,128]{3,2,1,0:T(8,128)S(1)}, u32[]{:S(2)}, u32[]{:S(2)}) collective-permute-start(f32[9,3,8,128]{3,2,1,0:T(8,128)S(1)} %get-tuple-element.59), channel_id=1, source_target_pairs={{1,6},{6,1},{3,4},{4,3},{5,10},{10,5},{7,8},{8,7},{9,14},{14,9},{1... | collective-permute-start | bytes 331784 | tf_op jit(solution)/shard_map/ppermute | solution.py:737
  40.2 3.2 %collective-permute-start.7 = (f32[16,16,8,128]{3,2,1,0:T(8,128)S(1)}, f32[16,16,8,128]{3,2,1,0:T(8,128)S(1)}, u32[]{:S(2)}, u32[]{:S(2)}) collective-permute-start(f32[16,16,8,128]{3,2,1,0:T(8,128)S(1)} %get-tuple-element.67), channel_id=1, source_target_pairs={{0,1},{1,0},{2,3},{3,2},{4,5},{5,4},{6,7},{7,6},{8,9},{9,8},{10,11... | collective-permute-start | bytes 3145736 | tf_op jit(solution)/shard_map/ppermute | solution.py:719
  41.1 6.9 %collective-permute-start.8 = (f32[2,18,8,128]{3,2,1,0:T(8,128)S(1)}, f32[2,18,8,128]{3,2,1,0:T(8,128)S(1)}, u32[]{:S(2)}, u32[]{:S(2)}) collective-permute-start(f32[2,18,8,128]{3,2,1,0:T(8,128)S(1)} %get-tuple-element.66), channel_id=1, source_target_pairs={{0,2},{1,3},{2,0},{3,1},{4,6},{5,7},{6,4},{7,5},{8,10},{9,11},{10,... | collective-permute-start | bytes 442376 | tf_op jit(solution)/shard_map/ppermute | solution.py:723
  43.6 28.4 %collective-permute-start.13 = (f32[2,32,4,8,128]{4,3,2,1,0:T(8,128)S(1)}, f32[2,32,4,8,128]{4,3,2,1,0:T(8,128)S(1)}, u32[]{:S(2)}, u32[]{:S(2)}) collective-permute-start(f32[2,32,4,8,128]{4,3,2,1,0:T(8,128)S(1)} %get-tuple-element.77), channel_id=1, source_target_pairs={{0,1},{1,0},{2,3},{3,2},{4,5},{5,4},{6,7},{7,6},{8,9},{9,8},{10,11... | collective-permute-start | bytes 3145736 | tf_op jit(solution)/shard_map/ppermute | solution.py:719
  44.1 28.0 %collective-permute-start.14 = (f32[2,32,4,8,128]{4,3,2,1,0:T(8,128)S(1)}, f32[2,32,4,8,128]{4,3,2,1,0:T(8,128)S(1)}, u32[]{:S(2)}, u32[]{:S(2)}) collective-permute-start(f32[2,32,4,8,128]{4,3,2,1,0:T(8,128)S(1)} %get-tuple-element.68), channel_id=1, source_target_pairs={{1,4},{4,1},{3,6},{6,3},{5,8},{8,5},{7,10},{10,7},{9,12},{12,9},{1... | collective-permute-start | bytes 3145736 | tf_op jit(solution)/shard_map/ppermute | solution.py:737
  48.9 3.2 %collective-permute-start.9 = (f32[2,8,128]{2,1,0:T(8,128)S(1)}, f32[2,8,128]{2,1,0:T(8,128)S(1)}, u32[]{:S(2)}, u32[]{:S(2)}) collective-permute-start(f32[2,8,128]{2,1,0:T(8,128)S(1)} %get-tuple-element.76), channel_id=1, source_target_pairs={{0,1},{1,0},{2,3},{3,2},{4,5},{5,4},{6,7},{7,6},{8,9},{9,8},{10,11... | collective-permute-start | bytes 24584 | tf_op jit(solution)/shard_map/ppermute | solution.py:719
  52.1 19.8 %collective-permute-start.12 = (f32[2,8,128]{2,1,0:T(8,128)S(1)}, f32[2,8,128]{2,1,0:T(8,128)S(1)}, u32[]{:S(2)}, u32[]{:S(2)}) collective-permute-start(f32[2,8,128]{2,1,0:T(8,128)S(1)} %pad_maximum_fusion), channel_id=1, source_target_pairs={{0,4},{1,5},{2,6},{3,7},{4,0},{5,1},{6,2},{7,3},{8,12},{9,13},{10,... | collective-permute-start | bytes 24584 | tf_op jit(solution)/shard_map/ppermute | solution.py:754
  52.2 19.8 %collective-permute-start.11 = (f32[2,8,128]{2,1,0:T(8,128)S(1)}, f32[2,8,128]{2,1,0:T(8,128)S(1)}, u32[]{:S(2)}, u32[]{:S(2)}) collective-permute-start(f32[2,8,128]{2,1,0:T(8,128)S(1)} %pad_maximum_fusion), channel_id=1, source_target_pairs={{0,6},{1,7},{2,4},{3,5},{4,2},{5,3},{6,0},{7,1},{8,14},{9,15},{10,... | collective-permute-start | bytes 24584 | tf_op jit(solution)/shard_map/ppermute | solution.py:754
  54.9 17.0 %collective-permute-start.10 = (f32[2,8,128]{2,1,0:T(8,128)S(1)}, f32[2,8,128]{2,1,0:T(8,128)S(1)}, u32[]{:S(2)}, u32[]{:S(2)}) collective-permute-start(f32[2,8,128]{2,1,0:T(8,128)S(1)} %pad_maximum_fusion), channel_id=1, source_target_pairs={{0,2},{1,3},{2,0},{3,1},{4,6},{5,7},{6,4},{7,5},{8,10},{9,11},{10,... | collective-permute-start | bytes 24584 | tf_op jit(solution)/shard_map/ppermute | solution.py:754
  72.7 4.8 %collective-permute-start.16 = (f32[2,8,128]{2,1,0:T(8,128)S(1)}, f32[2,8,128]{2,1,0:T(8,128)S(1)}, u32[]{:S(2)}, u32[]{:S(2)}) collective-permute-start(f32[2,8,128]{2,1,0:T(8,128)S(1)} %pad_maximum_fusion.1), channel_id=1, source_target_pairs={{0,8},{4,12},{8,0},{12,4},{16,24},{20,28},{24,16},{28,20},{32,40},... | collective-permute-start | bytes 24584 | tf_op jit(solution)/shard_map/ppermute | solution.py:762
  75.1 4.0 %collective-permute-start.15 = (f32[2,8,128]{2,1,0:T(8,128)S(1)}, f32[2,8,128]{2,1,0:T(8,128)S(1)}, u32[]{:S(2)}, u32[]{:S(2)}) collective-permute-start(f32[2,8,128]{2,1,0:T(8,128)S(1)} %pad_maximum_fusion.1), channel_id=1, source_target_pairs={{0,16},{4,20},{8,24},{12,28},{16,0},{20,4},{24,8},{28,12},{32,48},... | collective-permute-start | bytes 24584 | tf_op jit(solution)/shard_map/ppermute | solution.py:762
  77.2 3.7 %collective-permute-start.17 = (f32[2,8,128]{2,1,0:T(8,128)S(1)}, f32[2,8,128]{2,1,0:T(8,128)S(1)}, u32[]{:S(2)}, u32[]{:S(2)}) collective-permute-start(f32[2,8,128]{2,1,0:T(8,128)S(1)} %pad_maximum_fusion.1), channel_id=1, source_target_pairs={{0,24},{4,28},{8,16},{12,20},{16,8},{20,12},{24,0},{28,4},{32,56},... | collective-permute-start | bytes 24584 | tf_op jit(solution)/shard_map/ppermute | solution.py:762
  80.9 5.0 %collective-permute-start.20 = (f32[2,8,128]{2,1,0:T(8,128)S(1)}, f32[2,8,128]{2,1,0:T(8,128)S(1)}, u32[]{:S(2)}, u32[]{:S(2)}) collective-permute-start(f32[2,8,128]{2,1,0:T(8,128)S(1)} %pad_maximum_fusion.2), channel_id=1, source_target_pairs={{0,96},{4,100},{8,104},{12,108},{16,112},{20,116},{24,120},{28,124... | collective-permute-start | bytes 24584 | tf_op jit(solution)/shard_map/ppermute | solution.py:762
  82.0 3.9 %collective-permute-start.19 = (f32[2,8,128]{2,1,0:T(8,128)S(1)}, f32[2,8,128]{2,1,0:T(8,128)S(1)}, u32[]{:S(2)}, u32[]{:S(2)}) collective-permute-start(f32[2,8,128]{2,1,0:T(8,128)S(1)} %pad_maximum_fusion.2), channel_id=1, source_target_pairs={{0,32},{4,36},{8,40},{12,44},{16,48},{20,52},{24,56},{28,60},{32,0... | collective-permute-start | bytes 24584 | tf_op jit(solution)/shard_map/ppermute | solution.py:762
  82.7 4.0 %collective-permute-start.18 = (f32[2,8,128]{2,1,0:T(8,128)S(1)}, f32[2,8,128]{2,1,0:T(8,128)S(1)}, u32[]{:S(2)}, u32[]{:S(2)}) collective-permute-start(f32[2,8,128]{2,1,0:T(8,128)S(1)} %pad_maximum_fusion.2), channel_id=1, source_target_pairs={{0,64},{4,68},{8,72},{12,76},{16,80},{20,84},{24,88},{28,92},{32,9... | collective-permute-start | bytes 24584 | tf_op jit(solution)/shard_map/ppermute | solution.py:762
  84.9 17.3 %collective-permute-start.27 = (f32[2,4,24,8,128]{4,3,2,1,0:T(8,128)S(1)}, f32[2,4,24,8,128]{4,3,2,1,0:T(8,128)S(1)}, u32[]{:S(2)}, u32[]{:S(2)}) collective-permute-start(f32[2,4,24,8,128]{4,3,2,1,0:T(8,128)S(1)} %get-tuple-element.88), channel_id=1, source_target_pairs={{0,2},{1,3},{2,0},{3,1},{4,6},{5,7},{6,4},{7,5},{8,10},{9,11},{10,... | collective-permute-start | bytes 2359304 | tf_op jit(solution)/shard_map/ppermute | solution.py:723
  88.2 33.1 %collective-permute-start.22 = (f32[6,16,8,128]{3,2,1,0:T(8,128)S(1)}, f32[6,16,8,128]{3,2,1,0:T(8,128)S(1)}, u32[]{:S(2)}, u32[]{:S(2)}) collective-permute-start(f32[6,16,8,128]{3,2,1,0:T(8,128)S(1)} %get-tuple-element.84.power), channel_id=1, source_target_pairs={{0,2},{1,3},{2,0},{3,1},{4,6},{5,7},{6,4},{7,5},{8,10},{9,11},{10,... | collective-permute-start | bytes 1179656 | tf_op jit(solution)/shard_map/ppermute | solution.py:723
  89.4 31.9 %collective-permute-start.24 = (f32[6,3,8,128]{3,2,1,0:T(8,128)S(1)}, f32[6,3,8,128]{3,2,1,0:T(8,128)S(1)}, u32[]{:S(2)}, u32[]{:S(2)}) collective-permute-start(f32[6,3,8,128]{3,2,1,0:T(8,128)S(1)} %get-tuple-element.85), channel_id=1, source_target_pairs={{0,3},{1,2},{2,1},{3,0},{4,7},{5,6},{6,5},{7,4},{8,11},{9,10},{10,... | collective-permute-start | bytes 221192 | tf_op jit(solution)/shard_map/ppermute | solution.py:727
  95.7 25.6 %collective-permute-start.23 = (f32[6,3,8,128]{3,2,1,0:T(8,128)S(1)}, f32[6,3,8,128]{3,2,1,0:T(8,128)S(1)}, u32[]{:S(2)}, u32[]{:S(2)}) collective-permute-start(f32[6,3,8,128]{3,2,1,0:T(8,128)S(1)} %get-tuple-element.85), channel_id=1, source_target_pairs={{0,1},{1,0},{2,3},{3,2},{4,5},{5,4},{6,7},{7,6},{8,9},{9,8},{10,11... | collective-permute-start | bytes 221192 | tf_op jit(solution)/shard_map/ppermute | solution.py:719
  95.7 25.6 %collective-permute-start.26 = (f32[6,3,8,128]{3,2,1,0:T(8,128)S(1)}, f32[6,3,8,128]{3,2,1,0:T(8,128)S(1)}, u32[]{:S(2)}, u32[]{:S(2)}) collective-permute-start(f32[6,3,8,128]{3,2,1,0:T(8,128)S(1)} %get-tuple-element.86), channel_id=1, source_target_pairs={{1,6},{6,1},{3,4},{4,3},{5,10},{10,5},{7,8},{8,7},{9,14},{14,9},{1... | collective-permute-start | bytes 221192 | tf_op jit(solution)/shard_map/ppermute | solution.py:737
  102.1 19.1 %collective-permute-start.25 = (f32[6,3,8,128]{3,2,1,0:T(8,128)S(1)}, f32[6,3,8,128]{3,2,1,0:T(8,128)S(1)}, u32[]{:S(2)}, u32[]{:S(2)}) collective-permute-start(f32[6,3,8,128]{3,2,1,0:T(8,128)S(1)} %get-tuple-element.86), channel_id=1, source_target_pairs={{1,4},{4,1},{3,6},{6,3},{5,8},{8,5},{7,10},{10,7},{9,12},{12,9},{1... | collective-permute-start | bytes 221192 | tf_op jit(solution)/shard_map/ppermute | solution.py:737
  111.7 9.6 %copy-start.1 = (f32[64,12]{0,1:T(8,128)S(1)}, f32[64,12]{0,1:T(8,128)}, u32[]{:S(2)}) copy-start(f32[64,12]{0,1:T(8,128)} %param.16) | copy-start | bytes 9220
  146.7 3.0 %collective-permute-start.28 = (f32[16,16,8,128]{3,2,1,0:T(8,128)S(1)}, f32[16,16,8,128]{3,2,1,0:T(8,128)S(1)}, u32[]{:S(2)}, u32[]{:S(2)}) collective-permute-start(f32[16,16,8,128]{3,2,1,0:T(8,128)S(1)} %get-tuple-element.95), channel_id=1, source_target_pairs={{0,1},{1,0},{2,3},{3,2},{4,5},{5,4},{6,7},{7,6},{8,9},{9,8},{10,11... | collective-permute-start | bytes 3145736 | tf_op jit(solution)/shard_map/ppermute | solution.py:719
  147.3 12.2 %collective-permute-start.29 = (f32[6,16,8,128]{3,2,1,0:T(8,128)S(1)}, f32[6,16,8,128]{3,2,1,0:T(8,128)S(1)}, u32[]{:S(2)}, u32[]{:S(2)}) collective-permute-start(f32[6,16,8,128]{3,2,1,0:T(8,128)S(1)} %get-tuple-element.97), channel_id=1, source_target_pairs={{0,2},{1,3},{2,0},{3,1},{4,6},{5,7},{6,4},{7,5},{8,10},{9,11},{10,... | collective-permute-start | bytes 1179656 | tf_op jit(solution)/shard_map/ppermute | solution.py:723
  149.0 11.6 %collective-permute-start.21 = (f32[3,16,8,128]{3,2,1,0:T(8,128)S(1)}, f32[3,16,8,128]{3,2,1,0:T(8,128)S(1)}, u32[]{:S(2)}, u32[]{:S(2)}) collective-permute-start(f32[3,16,8,128]{3,2,1,0:T(8,128)S(1)} %get-tuple-element.83), channel_id=1, source_target_pairs={{0,1},{1,0},{2,3},{3,2},{4,5},{5,4},{6,7},{7,6},{8,9},{9,8},{10,11... | collective-permute-start | bytes 589832 | tf_op jit(solution)/shard_map/ppermute | solution.py:719
  159.7 2.0 %collective-permute-start.30 = (f32[3,16,8,128]{3,2,1,0:T(8,128)S(1)}, f32[3,16,8,128]{3,2,1,0:T(8,128)S(1)}, u32[]{:S(2)}, u32[]{:S(2)}) collective-permute-start(f32[3,16,8,128]{3,2,1,0:T(8,128)S(1)} %get-tuple-element.100), channel_id=1, source_target_pairs={{0,1},{1,0},{2,3},{3,2},{4,5},{5,4},{6,7},{7,6},{8,9},{9,8},{10,11... | collective-permute-start | bytes 589832 | tf_op jit(solution)/shard_map/ppermute | solution.py:719

commit v3 on v2

--- a/solution.py
+++ b/solution.py
@@ -42,7 +42,7 @@
     return jax.ShapeDtypeStruct(dims + (8, 128), F32)
 
 
-def call(kernel, outs, scratch=(), scalars=0, cost=0, raw_in=False, raw_out=False, room=4):
+def call(kernel, outs, scratch=(), scalars=0, cost=0, raw_in=False, raw_out=False, room=4, alias={}):
     def held(out):
         return out if raw_out else pltpu.VMEM(out.shape, out.dtype)
 
@@ -57,6 +57,7 @@
             kernel,
             out_shape=jax.tree.map(held, outs),
             in_specs=smem + [pl.BlockSpec(memory_space=space)] * len(fields),
+            input_output_aliases=alias,
             out_specs=jax.tree.map(lambda _: pl.BlockSpec(memory_space=pltpu.VMEM), outs),
             scratch_shapes=[pltpu.VMEM(dims + (8, 128), F32) for dims in scratch] + own,
             compiler_params=pltpu.CompilerParams(vmem_limit_bytes=room * 1024 * 1024),
@@ -82,12 +83,12 @@
     return ref[n, chunk * 2 + row // 8, pl.ds(row % 8, 8, stride=8), :]
 
 
-def loop(count, body):
+def loop(count, body, unroll=4):
     def step(i, carry):
         body(i)
         return carry
 
-    lax.fori_loop(0, count, step, 0)
+    lax.fori_loop(0, count, step, 0, unroll=min(unroll, count))
 
 
 def iotas():
@@ -179,7 +180,7 @@
                     out += [total[layer * 4 + k] + w * field[k] for k in range(4)]
                 return tuple(out)
 
-            total = lax.fori_loop(0, DEEP, step, tuple(total), unroll=4)
+            total = lax.fori_loop(0, DEEP, step, tuple(total), unroll=16)
         for layer in range(LAYERS):
             for k in range(4):
                 acc[layer, block * 4 + k] = total[layer * 4 + k]
@@ -525,74 +526,174 @@
     loop(DEEP, body)
 
 
-def slab_wide_kernel(t_own, t_got, k_own, k_got, g_core, g_tile, wide, s_far):
+def deep_rows(step):
+    return range(step, WIDE - step), sum(WIDE - 2 * k for k in range(1, step))
+
+
+DEEP_ROWS = deep_rows(SWEEPS + 1)[1]
+
+
+def slab_deep_kernel(t_own, t_got, k_own, k_got, g_core, g_tile, s_far):
     far, core = place()
-    from_core, from_tile = (WIDE - SWEEPS) * (1 - core), (WIDE - SWEEPS) * core
+
+    def side(half, number):
+        fields = (t_own, k_own) if number == 1 - half else (t_got, k_got)
+        top, bottom = (g_core, g_tile) if number else (g_tile, g_core)
+        for step in range(1, SWEEPS + 1):
+            rows, start = deep_rows(step)
+            n = step - 1 if half else DEEP - step
+            z = step - 1 if half else SLAB - step
+            for i, row in enumerate(rows):
+                for f in range(2):
+                    if row < SWEEPS:
+                        s_far[f, start + i] = top[f, z, row]
+                    elif row < SWEEPS + ROWS:
+                        s_far[f, start + i] = fields[f][n, row - SWEEPS]
+                    else:
+                        s_far[f, start + i] = bottom[f, z, row - SWEEPS - ROWS]
+
+    for half in range(2):
+        for number in range(2):
+            pl.when((far == half) & (core == number))(functools.partial(side, half, number))
+
+
+def row_edges_of(n, rows, cond, row_edge):
+    for row in rows:
+        row_edge[n, row] = harmonic(cond[n, row], cond[n, row + 1])
+
+
+def col_edges_of(n, rows, cond, col_edge):
+    sub, lane = iotas()
+    last = (sub == 7) & (lane == 127)
+    for row in rows:
+        here = cond[n, row]
+        col_edge[n, row] = jnp.where(last, 0.0, harmonic(here, after(here, lane)))
+
+
+def deep_edges_of(n, rows, cond, deep_edge):
+    for row in rows:
+        deep_edge[n + 1, row] = harmonic(cond[n, row], cond[n + 1, row])
+
+
+def turns_of(n, rows, deep_edge, row_edge, col_edge, turn):
+    _, lane = iotas()
+    for row in rows:
+        ce = col_edge[n, row]
+        turn[n, row] = inverse(
+            sink_level + deep_edge[n, row] + deep_edge[n + 1, row]
+            + row_edge[n, row - 1] + row_edge[n, row] + ce + before(ce, lane)
+        )
+
+
+OUTER = (*range(1, SWEEPS), *range(SWEEPS + ROWS, WIDE - 1))
+
+
+def slab_inner_kernel(t_own, t_got, k_own, k_got, warm, cond, deep_edge, row_edge, col_edge, turn):
+    far, core = place()
+    zero = jnp.zeros((8, 128), F32)
+    base = SWEEPS * far
 
     def body(n):
-        for f, (own, got) in enumerate(((t_own, t_got), (k_own, k_got))):
+        for own, got, out, up in ((t_own, t_got, warm, 1), (k_own, k_got, cond, 0)):
             for ref, z in ((own, DEEP * core + n), (got, DEEP * (1 - core) + n)):
                 for k in range(ROWS):
-                    wide[f, z, SWEEPS + k] = ref[n, k]
-                for k in range(SWEEPS):
-                    wide[f, z, from_core + k] = g_core[f, z, k]
-                    wide[f, z, from_tile + k] = g_tile[f, z, k]
+                    out[up + base + z, SWEEPS + k] = ref[n, k]
 
     loop(DEEP, body)
-    first = (SLAB - SWEEPS) * (1 - far)
-
-    def send(n):
-        for f in range(2):
-            for row in range(WIDE):
-                s_far[f, n, row] = wide[f, first + n, row]
-
-    loop(SWEEPS, send)
-
-
-def slab_edges_kernel(wide, g_far, warm, deep_edge, row_edge, col_edge, turn, cond):
-    far, _ = place()
-    sub, lane = iotas()
-    zero = jnp.zeros((8, 128), F32)
-
-    def body(n):
-        for row in range(WIDE):
-            warm[1 + SWEEPS * far + n, row] = wide[0, n, row]
-            cond[SWEEPS * far + n, row] = wide[1, n, row]
-
-    loop(SLAB, body)
-
-    def rim(n):
-        for row in range(WIDE):
-            warm[1 + SLAB * (1 - far) + n, row] = g_far[0, n, row]
-            cond[SLAB * (1 - far) + n, row] = g_far[1, n, row]
-
-    loop(SWEEPS, rim)
     for row in range(WIDE):
         for n in (0, THICK + 1):
             warm[n, row] = zero
         for n in (0, THICK):
             deep_edge[n, row] = zero
-
-    def deep(n):
-        for row in range(WIDE):
-            deep_edge[n + 1, row] = harmonic(cond[n, row], cond[n + 1, row])
-
-    loop(THICK - 1, deep)
-    last = (sub == 7) & (lane == 127)
-
-    def edges(n):
-        for row in range(WIDE - 1):
-            row_edge[n, row] = harmonic(cond[n, row], cond[n, row + 1])
-        for row in range(1, WIDE - 1):
-            here = cond[n, row]
-            ce = jnp.where(last, 0.0, harmonic(here, after(here, lane)))
-            col_edge[n, row] = ce
-            turn[n, row] = inverse(
-                sink_level + deep_edge[n, row] + deep_edge[n + 1, row]
-                + row_edge[n, row - 1] + row_edge[n, row] + ce + before(ce, lane)
-            )
-
-    loop(THICK, edges)
+    mid = range(SWEEPS, SWEEPS + ROWS)
+
+    def between(z):
+        deep_edges_of(base + z, mid, cond, deep_edge)
+
+    loop(SLAB - 1, between)
+
+    def level(z):
+        row_edges_of(base + z, mid[:-1], cond, row_edge)
+        col_edges_of(base + z, mid, cond, col_edge)
+
+    loop(SLAB, level)
+
+    def turns(z):
+        turns_of(base + 1 + z, mid[1:-1], deep_edge, row_edge, col_edge, turn)
+
+    loop(SLAB - 2, turns)
+
+
+def slab_outer_kernel(
+    warm_in, cond_in, deep_in, row_in, col_in, turn_in, g_core, g_tile, g_far,
+    warm, cond, deep_edge, row_edge, col_edge, turn,
+):
+    far, core = place()
+    zero = jnp.zeros((8, 128), F32)
+    base = SWEEPS * far
+    from_core, from_tile = (WIDE - SWEEPS) * (1 - core), (WIDE - SWEEPS) * core
+
+    def body(z):
+        for f, out, up in ((0, warm, 1), (1, cond, 0)):
+            for k in range(SWEEPS):
+                out[up + base + z, from_core + k] = g_core[f, z, k]
+                out[up + base + z, from_tile + k] = g_tile[f, z, k]
+
+    loop(SLAB, body)
+    for step in range(1, SWEEPS + 1):
+        at = jnp.where(far == 0, SLAB + step - 1, SWEEPS - step)
+        rows, start = deep_rows(step)
+        for f, out, up in ((0, warm, 1), (1, cond, 0)):
+            for row in range(WIDE):
+                out[up + at, row] = g_far[f, start + row - step] if row in rows else zero
+    every = range(1, WIDE - 1)
+
+    def between(n):
+        deep_edges_of(n, OUTER, cond, deep_edge)
+
+    loop(THICK - 1, between)
+
+    def meeting(i):
+        deep_edges_of((SLAB - 1) * (1 - far) + i, range(SWEEPS, SWEEPS + ROWS), cond, deep_edge)
+
+    loop(SWEEPS, meeting)
+
+    def level(z):
+        row_edges_of(base + z, (*range(SWEEPS), *range(SWEEPS + ROWS - 1, WIDE - 1)), cond, row_edge)
+        col_edges_of(base + z, OUTER, cond, col_edge)
+
+    loop(SLAB, level)
+
+    def halo_level(i):
+        n = SLAB * (1 - far) + i
+        row_edges_of(n, range(WIDE - 1), cond, row_edge)
+        col_edges_of(n, every, cond, col_edge)
+
+    loop(SWEEPS, halo_level)
+
+    def turns(z):
+        rows = (*range(1, SWEEPS + 1), *range(SWEEPS + ROWS - 1, WIDE - 1))
+        turns_of(base + z, rows, deep_edge, row_edge, col_edge, turn)
+
+    loop(SLAB, turns)
+
+    def more_turns(i):
+        turns_of((SLAB - 1) * (1 - far) + far + i, every, deep_edge, row_edge, col_edge, turn)
+
+    loop(SWEEPS, more_turns)
+    turns_of(0, every, deep_edge, row_edge, col_edge, turn)
+    turns_of(THICK - 1, every, deep_edge, row_edge, col_edge, turn)
+
+
+def relax(n, src, rows, put, source, deep_edge, row_edge, col_edge, turn, lane):
+    above, here, e_above = src[n + 1, rows[0] - 1], src[n + 1, rows[0]], row_edge[n, rows[0] - 1]
+    for row in rows:
+        under, e_under, ce = src[n + 1, row + 1], row_edge[n, row], col_edge[n, row]
+        flow = source[n, row] + ce * after(here, lane) + before(ce * here, lane)
+        flow = flow + e_above * above + e_under * under
+        flow = flow + deep_edge[n, row] * src[n, row] + deep_edge[n + 1, row] * src[n + 2, row]
+        put(row, flow * turn[n, row])
+        above, here, e_above = here, under, e_under
 
 
 def sweeps_kernel(
@@ -635,7 +736,7 @@
                 source[n, block * 4 + k] = total[k]
             return carry
 
-        lax.fori_loop(0, THICK, depth, 0)
+        lax.fori_loop(0, THICK, depth, 0, unroll=4)
 
     loop(WIDE // 4, sources)
     for ref in (one, two):
@@ -643,30 +744,27 @@
             ref[0, row] = zero
             ref[THICK + 1, row] = zero
 
-    before_ref = warm
-    for sweep in range(1, SWEEPS + 1):
-        after_ref = one if sweep % 2 else two
-        start = sweep * far
-
-        def step(i, src=before_ref, dst=after_ref, sweep=sweep, start=start):
-            n = start + i
-            for row in range(sweep, WIDE - sweep):
-                here = src[n + 1, row]
-                ce = col_edge[n, row]
-                flow = source[n, row] + ce * after(here, lane) + before(ce * here, lane)
-                flow = flow + row_edge[n, row - 1] * src[n + 1, row - 1] + row_edge[n, row] * src[n + 1, row + 1]
-                flow = flow + deep_edge[n, row] * src[n, row] + deep_edge[n + 1, row] * src[n + 2, row]
-                dst[n + 1, row] = flow * turn[n, row]
-
-        loop(THICK - sweep, step)
-        before_ref = after_ref
-
-    def outs(n):
-        for k in range(ROWS):
-            out[n, k] = before_ref[1 + SWEEPS * far + DEEP * core + n, SWEEPS + k]
-            s_out[n, k] = before_ref[1 + SWEEPS * far + DEEP * (1 - core) + n, SWEEPS + k]
-
-    loop(DEEP, outs)
+    fields = (source, deep_edge, row_edge, col_edge, turn, lane)
+    for sweep, src, dst in ((1, warm, one), (2, one, two), (3, two, one)):
+
+        def step(i, sweep=sweep, src=src, dst=dst):
+            n = sweep * far + i
+
+            def put(row, value):
+                dst[n + 1, row] = value
+
+            relax(n, src, range(sweep, WIDE - sweep), put, *fields)
+
+        loop(THICK - sweep, step, 5)
+    for ref, half in ((out, core), (s_out, 1 - core)):
+
+        def final_step(i, ref=ref, half=half):
+            def put(row, value):
+                ref[i, row - SWEEPS] = value
+
+            relax(SWEEPS * far + DEEP * half + i, one, range(SWEEPS, SWEEPS + ROWS), put, *fields)
+
+        loop(DEEP, final_step)
     weigh(
         weights,
         ((out, 0, SLAB * far + DEEP * core), (s_out, 0, SLAB * far + DEEP * (1 - core))),
@@ -824,24 +922,20 @@
     k_got = to_core(tied(k_send, s_basis))
     rim = shaped(2, SLAB, SWEEPS)
     k_core, k_tile = call(slab_rim_kernel, [rim, rim], cost=0.4)(t_own, t_got, k_own, k_got)
-    wide, s_deep = call(slab_wide_kernel, [shaped(2, SLAB, WIDE), shaped(2, SWEEPS, WIDE)], cost=0.6)(
-        t_own, t_got, k_own, k_got, to_core(k_core), to_tile(k_tile)
-    )
+    g_core, g_rim = to_core(k_core), to_tile(k_tile)
+    s_deep = call(slab_deep_kernel, shaped(2, DEEP_ROWS), cost=0.3)(t_own, t_got, k_own, k_got, g_core, g_rim)
     w2, sums = call(moments_kernel, [field, shaped(2)], cost=0.9)(
         tied(v0, k_tile), v1, v2, diag, row_edge, col_edge, vert, g_basis
     )
+    thick = shaped(THICK, WIDE)
+    inner = call(
+        slab_inner_kernel, [shaped(THICK + 2, WIDE), thick, shaped(THICK + 1, WIDE), thick, thick, thick], cost=5.5
+    )(tied(t_own, sums), t_got, k_own, k_got)
     values = along_core_and_x(sums)
-    values, s_deep = lax.optimization_barrier((values, s_deep))
+    values, s_deep, inner = lax.optimization_barrier((values, s_deep, inner))
     values = along_tile(values, 2)
     total = along_tile(values, 8)
-    thick = shaped(THICK, WIDE)
-    warm, deep_edge, row_heat, col_heat, turn = call(
-        slab_edges_kernel,
-        [shaped(THICK + 2, WIDE), shaped(THICK + 1, WIDE), thick, thick, thick],
-        scratch=((THICK, WIDE),),
-        cost=9.5,
-        room=5,
-    )(wide, to_far(s_deep))
+    total, g_deep = lax.optimization_barrier((total, to_far(s_deep)))
 
     power, p_core, p_tile, loss, s_loss = call(
         power_kernel,
@@ -856,6 +950,12 @@
     q_core = to_core(p_core)
     voltage_loss = unpack(loss, to_core(s_loss))
 
+    warm, _, *edges = call(
+        slab_outer_kernel,
+        [shaped(THICK + 2, WIDE), thick, shaped(THICK + 1, WIDE), thick, thick, thick],
+        cost=4,
+        alias={i: i for i in range(6)},
+    )(*inner, g_core, g_rim, g_deep)
     out, s_out, final, s_final = call(
         sweeps_kernel,
         [shaped(DEEP, ROWS), shaped(DEEP, ROWS), shaped(LAYERS, ROWS), shaped(HALF, ROWS)],
@@ -863,7 +963,7 @@
         scalars=2,
         cost=25,
         room=14,
-    )(split, weights, power, p_far, q_core, q_core_far, q_tile, q_tile_far, warm, deep_edge, row_heat, col_heat, turn)
+    )(split, weights, power, p_far, q_core, q_core_far, q_tile, q_tile_far, warm, *edges)
     g_final = to_far(s_final)
     final_warmth = unpack(out, to_core(s_out))
     g_final = tied(g_final, final_warmth)

time: 164 us -> 143 us (0.87)
  Pallas kernels: 53.7 us -> 38.8 us
  starting transfers between devices: 58.8 us -> 53 us
    pallas_call x16 -> x17, Pallas kernels: 53.7 us -> 38.8 us  [run(): pl.pallas_call(kernel, out_shape=jax.tree.map(held, outs), in_specs=smem...]
    ppermute x10, starting transfers between devices: 7.56 us -> 14.3 us  [to_core(): return lax.ppermute(value, 'therm', [(i, i ^ 1) for i in range(4)])]
    ppermute x5, starting transfers between devices: 18.5 us -> 12 us  [to_tile(): return lax.ppermute(value, ('tile', 'therm'), pairs)]
    ppermute x2, starting transfers between devices: 12.1 us -> 7.82 us  [to_core_far(): return lax.ppermute(value, 'therm', [(i, i ^ 3) for i in range(4)])]
    ppermute x3, waiting for transfers between devices: 16.5 us -> 12.4 us  [along_core_and_x(): peers.append(lax.ppermute(values, ('tile', 'therm'), pairs))]
    ppermute x5, waiting for transfers between devices: 13.5 us -> 15.8 us  [to_far(): return lax.ppermute(value, 'therm', [(i, i ^ 2) for i in range(4)])]
    ppermute x5, starting transfers between devices: 8.51 us -> 6.76 us  [to_far(): return lax.ppermute(value, 'therm', [(i, i ^ 2) for i in range(4)])]
  transfers between devices with their start and end apart: 31 -> 31, of which waited for: 11 -> 16; matrix products, arithmetic and copies ran while one was open for 0% -> 0% of each run, Pallas kernels for 13% -> 13%
where the time goes in v3:
time: 143 us
  starting transfers between devices  53 us (37%)
  waiting for transfers between devices  49.3 us (34%)
  Pallas kernels  38.8 us (27%)
    pallas_call x17, Pallas kernels, run(): pl.pallas_call(kernel, out_shape=jax.tree.map(held, outs), in_specs=smem...  38.8 us
    ppermute x5, waiting for transfers between devices, to_far(): return lax.ppermute(value, 'therm', [(i, i ^ 2) for i in range(4)])  15.8 us
    ppermute x10, starting transfers between devices, to_core(): return lax.ppermute(value, 'therm', [(i, i ^ 1) for i in range(4)])  14.3 us
    ppermute x2, waiting for transfers between devices, to_core_far(): return lax.ppermute(value, 'therm', [(i, i ^ 3) for i in range(4)])  12.8 us
    ppermute x3, waiting for transfers between devices, along_core_and_x(): peers.append(lax.ppermute(values, ('tile', 'therm'), pairs))  12.4 us
    ppermute x5, starting transfers between devices, to_tile(): return lax.ppermute(value, ('tile', 'therm'), pairs)  12 us
    ppermute x6, starting transfers between devices, along_tile(): lax.ppermute(values, 'tile', [(t, t ^ unit * k) for t in range(lax.axis_s...  8.75 us
    ppermute x2, starting transfers between devices, to_core_far(): return lax.ppermute(value, 'therm', [(i, i ^ 3) for i in range(4)])  7.82 us
  transfers between devices with their start and end apart: 31, of which 16 were waited for; matrix products, arithmetic and copies ran while one was open for 0% of the time, Pallas kernels for 13%

profile of v3, /device:TPU:25, one launch (start us, length us, event | category | flops | bytes accessed | tf_op | source)
XLA Modules:
  0.0 142.8 jit_solution(15800260857536779029)
XLA Ops:
  0.6 1.7 %shard_map.112 = (f32[16,16,8,128]{3,2,1,0:T(8,128)S(1)}, f32[16,16,8,128]{3,2,1,0:T(8,128)S(1)}) custom-call(f32[16,4,64,128]{3,2,1,0:T(8,128)} %bitcast.47), custom_call_target="tpu_custom_call" | custom-call | bytes 6800000 | tf_op jit(solution)/shard_map/pallas_call | solution.py:56
  2.3 0.8 collective-permute-start
  3.1 0.7 copy-done.2
  3.7 2.3 %shard_map.114 = (f32[12,16,8,128]{3,2,1,0:T(8,128)S(1)}, f32[12,16,8,128]{3,2,1,0:T(8,128)S(1)}) custom-call(f32[8]{0:T(128)S(1)} %copy-done.2, f32[3,4,64,128]{3,2,1,0:T(8,128)} %bitcast.52, s32[3,4,64,128]{3,2,1,0:T(8,128)} %bitcast.53, s32[3,4,64,128]{3,2,1,0:T(8,128)} %bitcast.54, s32[3,4,64,128]{3,2,1,0:T(8,128)} %bitcast.55), custom_call_target="tpu_custom_call" | custom-call | bytes 10200000 | tf_op jit(solution)/shard_map/pallas_call | solution.py:56
  6.1 2.8 %shard_map.113.part = f32[12,16,8,128]{3,2,1,0:T(8,128)S(1)} custom-call(f32[12,64]{1,0:T(8,128)S(1)} %copy-done, f32[16,16,8,128]{3,2,1,0:T(8,128)S(1)} %get-tuple-element.91.t_own, f32[16,16,8,128]{3,2,1,0:T(8,128)S(1)} %collective-permute-done.t_got), custom_call_target="tpu_custom_call" | custom-call | bytes 10200000 | tf_op jit(solution)/shard_map/pallas_call | solution.py:56
  9.2 2.8 %collective-permute-start.2 = (f32[9,16,8,128]{3,2,1,0:T(8,128)S(1)}, f32[9,16,8,128]{3,2,1,0:T(8,128)S(1)}, u32[]{:S(2)}, u32[]{:S(2)}) collective-permute-start(f32[9,16,8,128]{3,2,1,0:T(8,128)S(1)} %get-tuple-element.70), channel_id=1, source_target_pairs={{0,2},{1,3},{2,0},{3,1},{4,6},{5,7},{6,4},{7,5},{8,10},{9,11},{10,... | collective-permute-start | bytes 1769480 | tf_op jit(solution)/shard_map/ppermute | solution.py:821
  12.0 0.7 collective-permute-start.5
  12.8 2.1 %collective-permute-start.6 = (f32[31,3,8,128]{3,2,1,0:T(8,128)S(1)}, f32[31,3,8,128]{3,2,1,0:T(8,128)S(1)}, u32[]{:S(2)}, u32[]{:S(2)}) collective-permute-start(f32[31,3,8,128]{3,2,1,0:T(8,128)S(1)} %get-tuple-element.74), channel_id=1, source_target_pairs={{1,4},{4,1},{3,6},{6,3},{5,8},{8,5},{7,10},{10,7},{9,12},{12,9},{1... | collective-permute-start | bytes 1142792 | tf_op jit(solution)/shard_map/ppermute | solution.py:835
  14.9 5.9 %collective-permute-start.3 = (f32[9,3,8,128]{3,2,1,0:T(8,128)S(1)}, f32[9,3,8,128]{3,2,1,0:T(8,128)S(1)}, u32[]{:S(2)}, u32[]{:S(2)}) collective-permute-start(f32[9,3,8,128]{3,2,1,0:T(8,128)S(1)} %get-tuple-element.71), channel_id=1, source_target_pairs={{0,3},{1,2},{2,1},{3,0},{4,7},{5,6},{6,5},{7,4},{8,11},{9,10},{10,... | collective-permute-start | bytes 331784 | tf_op jit(solution)/shard_map/ppermute | solution.py:825
  20.7 1.9 %collective-permute-start.4 = (f32[9,3,8,128]{3,2,1,0:T(8,128)S(1)}, f32[9,3,8,128]{3,2,1,0:T(8,128)S(1)}, u32[]{:S(2)}, u32[]{:S(2)}) collective-permute-start(f32[9,3,8,128]{3,2,1,0:T(8,128)S(1)} %get-tuple-element.72), channel_id=1, source_target_pairs={{1,6},{6,1},{3,4},{4,3},{5,10},{10,5},{7,8},{8,7},{9,14},{14,9},{1... | collective-permute-start | bytes 331784 | tf_op jit(solution)/shard_map/ppermute | solution.py:835
  22.6 1.7 %shard_map.117 = (f32[16,16,8,128]{3,2,1,0:T(8,128)S(1)}, f32[16,16,8,128]{3,2,1,0:T(8,128)S(1)}) custom-call(f32[16,4,64,128]{3,2,1,0:T(8,128)} %bitcast.48), custom_call_target="tpu_custom_call" | custom-call | bytes 6800000 | tf_op jit(solution)/shard_map/pallas_call | solution.py:56
  24.3 12.4 %collective-permute-done.3.g_core_far = f32[9,3,8,128]{3,2,1,0:T(8,128)S(1)} collective-permute-done((f32[9,3,8,128]{3,2,1,0:T(8,128)S(1)}, f32[9,3,8,128]{3,2,1,0:T(8,128)S(1)}, u32[]{:S(2)}, u32[]{:S(2)}) %collective-permute-start.3) | collective-permute-done | bytes 110624 | tf_op jit(solution)/shard_map/ppermute | solution.py:825
  36.7 2.3 %shard_map.116 = (f32[8,22,8,128]{3,2,1,0:T(8,128)S(1)}, f32[8,22,8,128]{3,2,1,0:T(8,128)S(1)}, f32[8,22,8,128]{3,2,1,0:T(8,128)S(1)}, f32[6,22,8,128]{3,2,1,0:T...) custom-call(f32[12,16,8,128]{3,2,1,0:T(8,128)S(1)} %shard_map.113.pa, ...), custom_call_target="tpu_custom_call" | custom-call | bytes 10200000 | tf_op jit(solution)/shard_map/pallas_call | solution.py:56
  39.0 0.9 collective-permute-start.7
  40.0 1.7 %collective-permute-start.8 = (f32[2,18,8,128]{3,2,1,0:T(8,128)S(1)}, f32[2,18,8,128]{3,2,1,0:T(8,128)S(1)}, u32[]{:S(2)}, u32[]{:S(2)}) collective-permute-start(f32[2,18,8,128]{3,2,1,0:T(8,128)S(1)} %get-tuple-element.79), channel_id=1, source_target_pairs={{0,2},{1,3},{2,0},{3,1},{4,6},{5,7},{6,4},{7,5},{8,10},{9,11},{10,... | collective-permute-start | bytes 442376 | tf_op jit(solution)/shard_map/ppermute | solution.py:821
  42.9 2.4 %collective-permute-start.14 = (f32[2,32,4,8,128]{4,3,2,1,0:T(8,128)S(1)}, f32[2,32,4,8,128]{4,3,2,1,0:T(8,128)S(1)}, u32[]{:S(2)}, u32[]{:S(2)}) collective-permute-start(f32[2,32,4,8,128]{4,3,2,1,0:T(8,128)S(1)} %get-tuple-element.81), channel_id=1, source_target_pairs={{1,4},{4,1},{3,6},{6,3},{5,8},{8,5},{7,10},{10,7},{9,12},{12,9},{1... | collective-permute-start | bytes 3145736 | tf_op jit(solution)/shard_map/ppermute | solution.py:835
  45.2 1.6 %collective-permute-done.8.got = f32[2,18,8,128]{3,2,1,0:T(8,128)S(1)} collective-permute-done((f32[2,18,8,128]{3,2,1,0:T(8,128)S(1)}, f32[2,18,8,128]{3,2,1,0:T(8,128)S(1)}, u32[]{:S(2)}, u32[]{:S(2)}) %collective-permute-start.8) | collective-permute-done | bytes 147488 | tf_op jit(solution)/shard_map/ppermute | solution.py:821
  46.9 0.9 shard_map.119
  47.8 2.3 %collective-permute-start.9 = (f32[2,8,128]{2,1,0:T(8,128)S(1)}, f32[2,8,128]{2,1,0:T(8,128)S(1)}, u32[]{:S(2)}, u32[]{:S(2)}) collective-permute-start(f32[2,8,128]{2,1,0:T(8,128)S(1)} %get-tuple-element.89), channel_id=1, source_target_pairs={{0,1},{1,0},{2,3},{3,2},{4,5},{5,4},{6,7},{7,6},{8,9},{9,8},{10,11... | collective-permute-start | bytes 24584 | tf_op jit(solution)/shard_map/ppermute | solution.py:817
  50.1 0.8 collective-permute-done.9
  51.0 2.7 %collective-permute-start.11 = (f32[2,8,128]{2,1,0:T(8,128)S(1)}, f32[2,8,128]{2,1,0:T(8,128)S(1)}, u32[]{:S(2)}, u32[]{:S(2)}) collective-permute-start(f32[2,8,128]{2,1,0:T(8,128)S(1)} %pad_maximum_fusion), channel_id=1, source_target_pairs={{0,6},{1,7},{2,4},{3,5},{4,2},{5,3},{6,0},{7,1},{8,14},{9,15},{10,... | collective-permute-start | bytes 24584 | tf_op jit(solution)/shard_map/ppermute | solution.py:852
  54.2 4.2 %shard_map.121 = (f32[38,24,8,128]{3,2,1,0:T(8,128)S(1)}, f32[36,24,8,128]{3,2,1,0:T(8,128)S(1)}, f32[37,24,8,128]{3,2,1,0:T(8,128)S(1)}, f32[36,24,8,128]{3,2,1...) custom-call(f32[16,16,8,128]{3,2,1,0:T(8,128)S(1)} %get-tuple-element.91.t_own, ...), custom_call_target="tpu_custom_call" | custom-call | bytes 18700000 | tf_op jit(solution)/shard_map/pallas_call | solution.py:56
  58.4 12.4 %collective-permute-done.12 = f32[2,8,128]{2,1,0:T(8,128)S(1)} collective-permute-done((f32[2,8,128]{2,1,0:T(8,128)S(1)}, f32[2,8,128]{2,1,0:T(8,128)S(1)}, u32[]{:S(2)}, u32[]{:S(2)}) %collective-permute-start.12) | collective-permute-done | bytes 8224 | tf_op jit(solution)/shard_map/ppermute | solution.py:852
  70.9 2.3 %collective-permute-start.16 = (f32[2,8,128]{2,1,0:T(8,128)S(1)}, f32[2,8,128]{2,1,0:T(8,128)S(1)}, u32[]{:S(2)}, u32[]{:S(2)}) collective-permute-start(f32[2,8,128]{2,1,0:T(8,128)S(1)} %pad_maximum_fusion.1), channel_id=1, source_target_pairs={{0,8},{4,12},{8,0},{12,4},{16,24},{20,28},{24,16},{28,20},{32,40},... | collective-permute-start | bytes 24584 | tf_op jit(solution)/shard_map/ppermute | solution.py:860
  73.3 2.1 %collective-permute-start.15 = (f32[2,8,128]{2,1,0:T(8,128)S(1)}, f32[2,8,128]{2,1,0:T(8,128)S(1)}, u32[]{:S(2)}, u32[]{:S(2)}) collective-permute-start(f32[2,8,128]{2,1,0:T(8,128)S(1)} %pad_maximum_fusion.1), channel_id=1, source_target_pairs={{0,16},{4,20},{8,24},{12,28},{16,0},{20,4},{24,8},{28,12},{32,48},... | collective-permute-start | bytes 24584 | tf_op jit(solution)/shard_map/ppermute | solution.py:860
  75.8 0.9 collective-permute-start.21
  77.3 1.8 %collective-permute-done.17 = f32[2,8,128]{2,1,0:T(8,128)S(1)} collective-permute-done((f32[2,8,128]{2,1,0:T(8,128)S(1)}, f32[2,8,128]{2,1,0:T(8,128)S(1)}, u32[]{:S(2)}, u32[]{:S(2)}) %collective-permute-start.17) | collective-permute-done | bytes 8224 | tf_op jit(solution)/shard_map/ppermute | solution.py:860
  79.2 1.1 collective-permute-start.20
  80.3 0.8 collective-permute-start.19
  81.0 2.0 %collective-permute-start.18 = (f32[2,8,128]{2,1,0:T(8,128)S(1)}, f32[2,8,128]{2,1,0:T(8,128)S(1)}, u32[]{:S(2)}, u32[]{:S(2)}) collective-permute-start(f32[2,8,128]{2,1,0:T(8,128)S(1)} %pad_maximum_fusion.2), channel_id=1, source_target_pairs={{0,64},{4,68},{8,72},{12,76},{16,80},{20,84},{24,88},{28,92},{32,9... | collective-permute-start | bytes 24584 | tf_op jit(solution)/shard_map/ppermute | solution.py:860
  83.2 2.1 %collective-permute-done.18 = f32[2,8,128]{2,1,0:T(8,128)S(1)} collective-permute-done((f32[2,8,128]{2,1,0:T(8,128)S(1)}, f32[2,8,128]{2,1,0:T(8,128)S(1)}, u32[]{:S(2)}, u32[]{:S(2)}) %collective-permute-start.18) | collective-permute-done | bytes 8224 | tf_op jit(solution)/shard_map/ppermute | solution.py:860
  85.4 5.9 %collective-permute-done.21.g_far = f32[2,76,8,128]{3,2,1,0:T(8,128)S(1)} collective-permute-done((f32[2,76,8,128]{3,2,1,0:T(8,128)S(1)}, f32[2,76,8,128]{3,2,1,0:T(8,128)S(1)}, u32[]{:S(2)}, u32[]{:S(2)}) %collective-permute-start.21) | collective-permute-done | bytes 622624 | tf_op jit(solution)/shard_map/ppermute | solution.py:821
  91.3 1.0 shard_map.122
  92.4 3.6 %collective-permute-start.24 = (f32[6,3,8,128]{3,2,1,0:T(8,128)S(1)}, f32[6,3,8,128]{3,2,1,0:T(8,128)S(1)}, u32[]{:S(2)}, u32[]{:S(2)}) collective-permute-start(f32[6,3,8,128]{3,2,1,0:T(8,128)S(1)} %get-tuple-element.106), channel_id=1, source_target_pairs={{0,1},{1,0},{2,3},{3,2},{4,5},{5,4},{6,7},{7,6},{8,9},{9,8},{10,11... | collective-permute-start | bytes 221192 | tf_op jit(solution)/shard_map/ppermute | solution.py:817
  96.0 2.0 %collective-permute-start.25 = (f32[6,3,8,128]{3,2,1,0:T(8,128)S(1)}, f32[6,3,8,128]{3,2,1,0:T(8,128)S(1)}, u32[]{:S(2)}, u32[]{:S(2)}) collective-permute-start(f32[6,3,8,128]{3,2,1,0:T(8,128)S(1)} %get-tuple-element.106), channel_id=1, source_target_pairs={{0,3},{1,2},{2,1},{3,0},{4,7},{5,6},{6,5},{7,4},{8,11},{9,10},{10,... | collective-permute-start | bytes 221192 | tf_op jit(solution)/shard_map/ppermute | solution.py:825
  97.9 2.8 %collective-permute-start.26 = (f32[6,3,8,128]{3,2,1,0:T(8,128)S(1)}, f32[6,3,8,128]{3,2,1,0:T(8,128)S(1)}, u32[]{:S(2)}, u32[]{:S(2)}) collective-permute-start(f32[6,3,8,128]{3,2,1,0:T(8,128)S(1)} %get-tuple-element.107), channel_id=1, source_target_pairs={{1,4},{4,1},{3,6},{6,3},{5,8},{8,5},{7,10},{10,7},{9,12},{12,9},{1... | collective-permute-start | bytes 221192 | tf_op jit(solution)/shard_map/ppermute | solution.py:835
  100.7 2.9 %collective-permute-start.27 = (f32[6,3,8,128]{3,2,1,0:T(8,128)S(1)}, f32[6,3,8,128]{3,2,1,0:T(8,128)S(1)}, u32[]{:S(2)}, u32[]{:S(2)}) collective-permute-start(f32[6,3,8,128]{3,2,1,0:T(8,128)S(1)} %get-tuple-element.107), channel_id=1, source_target_pairs={{1,6},{6,1},{3,4},{4,3},{5,10},{10,5},{7,8},{8,7},{9,14},{14,9},{1... | collective-permute-start | bytes 221192 | tf_op jit(solution)/shard_map/ppermute | solution.py:835
  103.6 3.3 %shard_map.124 = (f32[38,24,8,128]{3,2,1,0:T(8,128)S(1)}, f32[36,24,8,128]{3,2,1,0:T(8,128)S(1)}, f32[37,24,8,128]{3,2,1,0:T(8,128)S(1)}, f32[36,24,8,128]{3,2,1...) custom-call(f32[38,24,8,128]{3,2,1,0:T(8,128)S(1)} %get-tuple-elemen, ...), custom_call_target="tpu_custom_call", output_to_operand_aliasing={{0}: (0, {}), {1}: (1, {}), {2}: (2, {}), {3}: (3, {}), {4}... | custom-call | bytes 13600000 | tf_op jit(solution)/shard_map/pallas_call | solution.py:56
  107.5 1.2 collective-permute-done.27.p_tile_far
  108.7 14.8 %shard_map.125 = (f32[16,16,8,128]{3,2,1,0:T(8,128)S(1)}, f32[16,16,8,128]{3,2,1,0:T(8,128)S(1)}, f32[12,16,8,128]{3,2,1,0:T(8,128)S(1)}, f32[6,16,8,128]{3,2,1,0:T(8,128)S(1)}) custom-call(f32[12,64]{1,0:T(8,128)S(1)} %bitcast.46, f32[12,64]{1,0:T(8,128)S(1)} %copy-done, f32[6,16,8,128]{3,2,1,0:T(8,128)S(1)} %get-tuple-element.105.power, ...), custom_call_target="tpu_custom_call" | custom-call | bytes 85000000 | tf_op jit(solution)/shard_map/pallas_call | solution.py:56
  123.5 4.2 %collective-permute-start.28 = (f32[16,16,8,128]{3,2,1,0:T(8,128)S(1)}, f32[16,16,8,128]{3,2,1,0:T(8,128)S(1)}, u32[]{:S(2)}, u32[]{:S(2)}) collective-permute-start(f32[16,16,8,128]{3,2,1,0:T(8,128)S(1)} %get-tuple-element.121), channel_id=1, source_target_pairs={{0,1},{1,0},{2,3},{3,2},{4,5},{5,4},{6,7},{7,6},{8,9},{9,8},{10,11... | collective-permute-start | bytes 3145736 | tf_op jit(solution)/shard_map/ppermute | solution.py:817
  127.7 1.2 collective-permute-start.29
  129.2 0.7 collective-permute-done.28.got
  129.9 1.6 %shard_map.126 = f32[16,4,64,128]{3,2,1,0:T(8,128)} custom-call(f32[16,16,8,128]{3,2,1,0:T(8,128)S(1)} %get-tuple-element.120.own, f32[16,16,8,128]{3,2,1,0:T(8,128)S(1)} %collective-permute-done.28.got), custom_call_target="tpu_custom_call" | custom-call | bytes 5440000 | tf_op jit(solution)/shard_map/pallas_call | solution.py:56
  131.6 8.2 %collective-permute-done.29.got = f32[6,16,8,128]{3,2,1,0:T(8,128)S(1)} collective-permute-done((f32[6,16,8,128]{3,2,1,0:T(8,128)S(1)}, f32[6,16,8,128]{3,2,1,0:T(8,128)S(1)}, u32[]{:S(2)}, u32[]{:S(2)}) %collective-permute-start.29) | collective-permute-done | bytes 393248 | tf_op jit(solution)/shard_map/ppermute | solution.py:821
  140.0 1.0 collective-permute-start.30
  141.0 0.8 shard_map.123
  142.0 0.8 shard_map.128
  (49 shorter events, 4.9 us)
Async XLA Ops:
  0.6 5.5 %copy-start = (f32[12,64]{1,0:T(8,128)S(1)}, f32[12,64]{1,0:T(8,128)}, u32[]{:S(2)}) copy-start(f32[12,64]{1,0:T(8,128)} %weights.3) | copy-start | bytes 9220
  2.3 3.8 %collective-permute-start = (f32[16,16,8,128]{3,2,1,0:T(8,128)S(1)}, f32[16,16,8,128]{3,2,1,0:T(8,128)S(1)}, u32[]{:S(2)}, u32[]{:S(2)}) collective-permute-start(f32[16,16,8,128]{3,2,1,0:T(8,128)S(1)} %get-tuple-element.66), channel_id=1, source_target_pairs={{0,1},{1,0},{2,3},{3,2},{4,5},{5,4},{6,7},{7,6},{8,9},{9,8},{10,11... | collective-permute-start | bytes 3145736 | tf_op jit(solution)/shard_map/ppermute | solution.py:817
  3.1 0.7 copy-start.2
  6.0 2.9 %collective-permute-start.1 = (f32[12,16,8,128]{3,2,1,0:T(8,128)S(1)}, f32[12,16,8,128]{3,2,1,0:T(8,128)S(1)}, u32[]{:S(2)}, u32[]{:S(2)}) collective-permute-start(f32[12,16,8,128]{3,2,1,0:T(8,128)S(1)} %get-tuple-element.68), channel_id=1, source_target_pairs={{0,1},{1,0},{2,3},{3,2},{4,5},{5,4},{6,7},{7,6},{8,9},{9,8},{10,11... | collective-permute-start | bytes 2359304 | tf_op jit(solution)/shard_map/ppermute | solution.py:817
  9.2 27.5 %collective-permute-start.2 = (f32[9,16,8,128]{3,2,1,0:T(8,128)S(1)}, f32[9,16,8,128]{3,2,1,0:T(8,128)S(1)}, u32[]{:S(2)}, u32[]{:S(2)}) collective-permute-start(f32[9,16,8,128]{3,2,1,0:T(8,128)S(1)} %get-tuple-element.70), channel_id=1, source_target_pairs={{0,2},{1,3},{2,0},{3,1},{4,6},{5,7},{6,4},{7,5},{8,10},{9,11},{10,... | collective-permute-start | bytes 1769480 | tf_op jit(solution)/shard_map/ppermute | solution.py:821
  12.0 24.6 %collective-permute-start.5 = (f32[31,3,8,128]{3,2,1,0:T(8,128)S(1)}, f32[31,3,8,128]{3,2,1,0:T(8,128)S(1)}, u32[]{:S(2)}, u32[]{:S(2)}) collective-permute-start(f32[31,3,8,128]{3,2,1,0:T(8,128)S(1)} %get-tuple-element.73), channel_id=1, source_target_pairs={{0,1},{1,0},{2,3},{3,2},{4,5},{5,4},{6,7},{7,6},{8,9},{9,8},{10,11... | collective-permute-start | bytes 1142792 | tf_op jit(solution)/shard_map/ppermute | solution.py:817
  12.8 23.9 %collective-permute-start.6 = (f32[31,3,8,128]{3,2,1,0:T(8,128)S(1)}, f32[31,3,8,128]{3,2,1,0:T(8,128)S(1)}, u32[]{:S(2)}, u32[]{:S(2)}) collective-permute-start(f32[31,3,8,128]{3,2,1,0:T(8,128)S(1)} %get-tuple-element.74), channel_id=1, source_target_pairs={{1,4},{4,1},{3,6},{6,3},{5,8},{8,5},{7,10},{10,7},{9,12},{12,9},{1... | collective-permute-start | bytes 1142792 | tf_op jit(solution)/shard_map/ppermute | solution.py:835
  14.9 21.8 %collective-permute-start.3 = (f32[9,3,8,128]{3,2,1,0:T(8,128)S(1)}, f32[9,3,8,128]{3,2,1,0:T(8,128)S(1)}, u32[]{:S(2)}, u32[]{:S(2)}) collective-permute-start(f32[9,3,8,128]{3,2,1,0:T(8,128)S(1)} %get-tuple-element.71), channel_id=1, source_target_pairs={{0,3},{1,2},{2,1},{3,0},{4,7},{5,6},{6,5},{7,4},{8,11},{9,10},{10,... | collective-permute-start | bytes 331784 | tf_op jit(solution)/shard_map/ppermute | solution.py:825
  20.7 15.9 %collective-permute-start.4 = (f32[9,3,8,128]{3,2,1,0:T(8,128)S(1)}, f32[9,3,8,128]{3,2,1,0:T(8,128)S(1)}, u32[]{:S(2)}, u32[]{:S(2)}) collective-permute-start(f32[9,3,8,128]{3,2,1,0:T(8,128)S(1)} %get-tuple-element.72), channel_id=1, source_target_pairs={{1,6},{6,1},{3,4},{4,3},{5,10},{10,5},{7,8},{8,7},{9,14},{14,9},{1... | collective-permute-start | bytes 331784 | tf_op jit(solution)/shard_map/ppermute | solution.py:835
  39.0 3.2 %collective-permute-start.7 = (f32[16,16,8,128]{3,2,1,0:T(8,128)S(1)}, f32[16,16,8,128]{3,2,1,0:T(8,128)S(1)}, u32[]{:S(2)}, u32[]{:S(2)}) collective-permute-start(f32[16,16,8,128]{3,2,1,0:T(8,128)S(1)} %get-tuple-element.80), channel_id=1, source_target_pairs={{0,1},{1,0},{2,3},{3,2},{4,5},{5,4},{6,7},{7,6},{8,9},{9,8},{10,11... | collective-permute-start | bytes 3145736 | tf_op jit(solution)/shard_map/ppermute | solution.py:817
  40.0 6.9 %collective-permute-start.8 = (f32[2,18,8,128]{3,2,1,0:T(8,128)S(1)}, f32[2,18,8,128]{3,2,1,0:T(8,128)S(1)}, u32[]{:S(2)}, u32[]{:S(2)}) collective-permute-start(f32[2,18,8,128]{3,2,1,0:T(8,128)S(1)} %get-tuple-element.79), channel_id=1, source_target_pairs={{0,2},{1,3},{2,0},{3,1},{4,6},{5,7},{6,4},{7,5},{8,10},{9,11},{10,... | collective-permute-start | bytes 442376 | tf_op jit(solution)/shard_map/ppermute | solution.py:821
  42.4 28.4 %collective-permute-start.13 = (f32[2,32,4,8,128]{4,3,2,1,0:T(8,128)S(1)}, f32[2,32,4,8,128]{4,3,2,1,0:T(8,128)S(1)}, u32[]{:S(2)}, u32[]{:S(2)}) collective-permute-start(f32[2,32,4,8,128]{4,3,2,1,0:T(8,128)S(1)} %get-tuple-element.90), channel_id=1, source_target_pairs={{0,1},{1,0},{2,3},{3,2},{4,5},{5,4},{6,7},{7,6},{8,9},{9,8},{10,11... | collective-permute-start | bytes 3145736 | tf_op jit(solution)/shard_map/ppermute | solution.py:817
  42.9 28.0 %collective-permute-start.14 = (f32[2,32,4,8,128]{4,3,2,1,0:T(8,128)S(1)}, f32[2,32,4,8,128]{4,3,2,1,0:T(8,128)S(1)}, u32[]{:S(2)}, u32[]{:S(2)}) collective-permute-start(f32[2,32,4,8,128]{4,3,2,1,0:T(8,128)S(1)} %get-tuple-element.81), channel_id=1, source_target_pairs={{1,4},{4,1},{3,6},{6,3},{5,8},{8,5},{7,10},{10,7},{9,12},{12,9},{1... | collective-permute-start | bytes 3145736 | tf_op jit(solution)/shard_map/ppermute | solution.py:835
  47.8 3.1 %collective-permute-start.9 = (f32[2,8,128]{2,1,0:T(8,128)S(1)}, f32[2,8,128]{2,1,0:T(8,128)S(1)}, u32[]{:S(2)}, u32[]{:S(2)}) collective-permute-start(f32[2,8,128]{2,1,0:T(8,128)S(1)} %get-tuple-element.89), channel_id=1, source_target_pairs={{0,1},{1,0},{2,3},{3,2},{4,5},{5,4},{6,7},{7,6},{8,9},{9,8},{10,11... | collective-permute-start | bytes 24584 | tf_op jit(solution)/shard_map/ppermute | solution.py:817
  50.9 19.9 %collective-permute-start.12 = (f32[2,8,128]{2,1,0:T(8,128)S(1)}, f32[2,8,128]{2,1,0:T(8,128)S(1)}, u32[]{:S(2)}, u32[]{:S(2)}) collective-permute-start(f32[2,8,128]{2,1,0:T(8,128)S(1)} %pad_maximum_fusion), channel_id=1, source_target_pairs={{0,4},{1,5},{2,6},{3,7},{4,0},{5,1},{6,2},{7,3},{8,12},{9,13},{10,... | collective-permute-start | bytes 24584 | tf_op jit(solution)/shard_map/ppermute | solution.py:852
  51.0 19.8 %collective-permute-start.11 = (f32[2,8,128]{2,1,0:T(8,128)S(1)}, f32[2,8,128]{2,1,0:T(8,128)S(1)}, u32[]{:S(2)}, u32[]{:S(2)}) collective-permute-start(f32[2,8,128]{2,1,0:T(8,128)S(1)} %pad_maximum_fusion), channel_id=1, source_target_pairs={{0,6},{1,7},{2,4},{3,5},{4,2},{5,3},{6,0},{7,1},{8,14},{9,15},{10,... | collective-permute-start | bytes 24584 | tf_op jit(solution)/shard_map/ppermute | solution.py:852
  53.7 17.1 %collective-permute-start.10 = (f32[2,8,128]{2,1,0:T(8,128)S(1)}, f32[2,8,128]{2,1,0:T(8,128)S(1)}, u32[]{:S(2)}, u32[]{:S(2)}) collective-permute-start(f32[2,8,128]{2,1,0:T(8,128)S(1)} %pad_maximum_fusion), channel_id=1, source_target_pairs={{0,2},{1,3},{2,0},{3,1},{4,6},{5,7},{6,4},{7,5},{8,10},{9,11},{10,... | collective-permute-start | bytes 24584 | tf_op jit(solution)/shard_map/ppermute | solution.py:852
  70.9 5.7 %collective-permute-start.16 = (f32[2,8,128]{2,1,0:T(8,128)S(1)}, f32[2,8,128]{2,1,0:T(8,128)S(1)}, u32[]{:S(2)}, u32[]{:S(2)}) collective-permute-start(f32[2,8,128]{2,1,0:T(8,128)S(1)} %pad_maximum_fusion.1), channel_id=1, source_target_pairs={{0,8},{4,12},{8,0},{12,4},{16,24},{20,28},{24,16},{28,20},{32,40},... | collective-permute-start | bytes 24584 | tf_op jit(solution)/shard_map/ppermute | solution.py:860
  73.3 4.0 %collective-permute-start.15 = (f32[2,8,128]{2,1,0:T(8,128)S(1)}, f32[2,8,128]{2,1,0:T(8,128)S(1)}, u32[]{:S(2)}, u32[]{:S(2)}) collective-permute-start(f32[2,8,128]{2,1,0:T(8,128)S(1)} %pad_maximum_fusion.1), channel_id=1, source_target_pairs={{0,16},{4,20},{8,24},{12,28},{16,0},{20,4},{24,8},{28,12},{32,48},... | collective-permute-start | bytes 24584 | tf_op jit(solution)/shard_map/ppermute | solution.py:860
  75.4 3.7 %collective-permute-start.17 = (f32[2,8,128]{2,1,0:T(8,128)S(1)}, f32[2,8,128]{2,1,0:T(8,128)S(1)}, u32[]{:S(2)}, u32[]{:S(2)}) collective-permute-start(f32[2,8,128]{2,1,0:T(8,128)S(1)} %pad_maximum_fusion.1), channel_id=1, source_target_pairs={{0,24},{4,28},{8,16},{12,20},{16,8},{20,12},{24,0},{28,4},{32,56},... | collective-permute-start | bytes 24584 | tf_op jit(solution)/shard_map/ppermute | solution.py:860
  75.8 15.5 %collective-permute-start.21 = (f32[2,76,8,128]{3,2,1,0:T(8,128)S(1)}, f32[2,76,8,128]{3,2,1,0:T(8,128)S(1)}, u32[]{:S(2)}, u32[]{:S(2)}) collective-permute-start(f32[2,76,8,128]{3,2,1,0:T(8,128)S(1)} %shard_map.120), channel_id=1, source_target_pairs={{0,2},{1,3},{2,0},{3,1},{4,6},{5,7},{6,4},{7,5},{8,10},{9,11},{10,... | collective-permute-start | bytes 1867784 | tf_op jit(solution)/shard_map/ppermute | solution.py:821
  79.2 4.1 %collective-permute-start.20 = (f32[2,8,128]{2,1,0:T(8,128)S(1)}, f32[2,8,128]{2,1,0:T(8,128)S(1)}, u32[]{:S(2)}, u32[]{:S(2)}) collective-permute-start(f32[2,8,128]{2,1,0:T(8,128)S(1)} %pad_maximum_fusion.2), channel_id=1, source_target_pairs={{0,96},{4,100},{8,104},{12,108},{16,112},{20,116},{24,120},{28,124... | collective-permute-start | bytes 24584 | tf_op jit(solution)/shard_map/ppermute | solution.py:860
  80.3 3.0 %collective-permute-start.19 = (f32[2,8,128]{2,1,0:T(8,128)S(1)}, f32[2,8,128]{2,1,0:T(8,128)S(1)}, u32[]{:S(2)}, u32[]{:S(2)}) collective-permute-start(f32[2,8,128]{2,1,0:T(8,128)S(1)} %pad_maximum_fusion.2), channel_id=1, source_target_pairs={{0,32},{4,36},{8,40},{12,44},{16,48},{20,52},{24,56},{28,60},{32,0... | collective-permute-start | bytes 24584 | tf_op jit(solution)/shard_map/ppermute | solution.py:860
  81.0 4.3 %collective-permute-start.18 = (f32[2,8,128]{2,1,0:T(8,128)S(1)}, f32[2,8,128]{2,1,0:T(8,128)S(1)}, u32[]{:S(2)}, u32[]{:S(2)}) collective-permute-start(f32[2,8,128]{2,1,0:T(8,128)S(1)} %pad_maximum_fusion.2), channel_id=1, source_target_pairs={{0,64},{4,68},{8,72},{12,76},{16,80},{20,84},{24,88},{28,92},{32,9... | collective-permute-start | bytes 24584 | tf_op jit(solution)/shard_map/ppermute | solution.py:860
  92.3 16.4 %collective-permute-start.23 = (f32[6,16,8,128]{3,2,1,0:T(8,128)S(1)}, f32[6,16,8,128]{3,2,1,0:T(8,128)S(1)}, u32[]{:S(2)}, u32[]{:S(2)}) collective-permute-start(f32[6,16,8,128]{3,2,1,0:T(8,128)S(1)} %get-tuple-element.105.power), channel_id=1, source_target_pairs={{0,2},{1,3},{2,0},{3,1},{4,6},{5,7},{6,4},{7,5},{8,10},{9,11},{10,... | collective-permute-start | bytes 1179656 | tf_op jit(solution)/shard_map/ppermute | solution.py:821
  92.4 14.5 %collective-permute-start.24 = (f32[6,3,8,128]{3,2,1,0:T(8,128)S(1)}, f32[6,3,8,128]{3,2,1,0:T(8,128)S(1)}, u32[]{:S(2)}, u32[]{:S(2)}) collective-permute-start(f32[6,3,8,128]{3,2,1,0:T(8,128)S(1)} %get-tuple-element.106), channel_id=1, source_target_pairs={{0,1},{1,0},{2,3},{3,2},{4,5},{5,4},{6,7},{7,6},{8,9},{9,8},{10,11... | collective-permute-start | bytes 221192 | tf_op jit(solution)/shard_map/ppermute | solution.py:817
  96.0 11.4 %collective-permute-start.25 = (f32[6,3,8,128]{3,2,1,0:T(8,128)S(1)}, f32[6,3,8,128]{3,2,1,0:T(8,128)S(1)}, u32[]{:S(2)}, u32[]{:S(2)}) collective-permute-start(f32[6,3,8,128]{3,2,1,0:T(8,128)S(1)} %get-tuple-element.106), channel_id=1, source_target_pairs={{0,3},{1,2},{2,1},{3,0},{4,7},{5,6},{6,5},{7,4},{8,11},{9,10},{10,... | collective-permute-start | bytes 221192 | tf_op jit(solution)/shard_map/ppermute | solution.py:825
  97.9 10.7 %copy-start.1 = (f32[64,12]{0,1:T(8,128)S(1)}, f32[64,12]{0,1:T(8,128)}, u32[]{:S(2)}) copy-start(f32[64,12]{0,1:T(8,128)} %param.16) | copy-start | bytes 9220
  97.9 9.6 %collective-permute-start.26 = (f32[6,3,8,128]{3,2,1,0:T(8,128)S(1)}, f32[6,3,8,128]{3,2,1,0:T(8,128)S(1)}, u32[]{:S(2)}, u32[]{:S(2)}) collective-permute-start(f32[6,3,8,128]{3,2,1,0:T(8,128)S(1)} %get-tuple-element.107), channel_id=1, source_target_pairs={{1,4},{4,1},{3,6},{6,3},{5,8},{8,5},{7,10},{10,7},{9,12},{12,9},{1... | collective-permute-start | bytes 221192 | tf_op jit(solution)/shard_map/ppermute | solution.py:835
  100.7 8.0 %collective-permute-start.27 = (f32[6,3,8,128]{3,2,1,0:T(8,128)S(1)}, f32[6,3,8,128]{3,2,1,0:T(8,128)S(1)}, u32[]{:S(2)}, u32[]{:S(2)}) collective-permute-start(f32[6,3,8,128]{3,2,1,0:T(8,128)S(1)} %get-tuple-element.107), channel_id=1, source_target_pairs={{1,6},{6,1},{3,4},{4,3},{5,10},{10,5},{7,8},{8,7},{9,14},{14,9},{1... | collective-permute-start | bytes 221192 | tf_op jit(solution)/shard_map/ppermute | solution.py:835
  123.5 6.4 %collective-permute-start.28 = (f32[16,16,8,128]{3,2,1,0:T(8,128)S(1)}, f32[16,16,8,128]{3,2,1,0:T(8,128)S(1)}, u32[]{:S(2)}, u32[]{:S(2)}) collective-permute-start(f32[16,16,8,128]{3,2,1,0:T(8,128)S(1)} %get-tuple-element.121), channel_id=1, source_target_pairs={{0,1},{1,0},{2,3},{3,2},{4,5},{5,4},{6,7},{7,6},{8,9},{9,8},{10,11... | collective-permute-start | bytes 3145736 | tf_op jit(solution)/shard_map/ppermute | solution.py:817
  127.7 12.2 %collective-permute-start.29 = (f32[6,16,8,128]{3,2,1,0:T(8,128)S(1)}, f32[6,16,8,128]{3,2,1,0:T(8,128)S(1)}, u32[]{:S(2)}, u32[]{:S(2)}) collective-permute-start(f32[6,16,8,128]{3,2,1,0:T(8,128)S(1)} %get-tuple-element.123), channel_id=1, source_target_pairs={{0,2},{1,3},{2,0},{3,1},{4,6},{5,7},{6,4},{7,5},{8,10},{9,11},{10,... | collective-permute-start | bytes 1179656 | tf_op jit(solution)/shard_map/ppermute | solution.py:821
  128.9 12.1 %collective-permute-start.22 = (f32[3,16,8,128]{3,2,1,0:T(8,128)S(1)}, f32[3,16,8,128]{3,2,1,0:T(8,128)S(1)}, u32[]{:S(2)}, u32[]{:S(2)}) collective-permute-start(f32[3,16,8,128]{3,2,1,0:T(8,128)S(1)} %get-tuple-element.104), channel_id=1, source_target_pairs={{0,1},{1,0},{2,3},{3,2},{4,5},{5,4},{6,7},{7,6},{8,9},{9,8},{10,11... | collective-permute-start | bytes 589832 | tf_op jit(solution)/shard_map/ppermute | solution.py:817
  140.0 2.0 %collective-permute-start.30 = (f32[3,16,8,128]{3,2,1,0:T(8,128)S(1)}, f32[3,16,8,128]{3,2,1,0:T(8,128)S(1)}, u32[]{:S(2)}, u32[]{:S(2)}) collective-permute-start(f32[3,16,8,128]{3,2,1,0:T(8,128)S(1)} %get-tuple-element.126), channel_id=1, source_target_pairs={{0,1},{1,0},{2,3},{3,2},{4,5},{5,4},{6,7},{7,6},{8,9},{9,8},{10,11... | collective-permute-start | bytes 589832 | tf_op jit(solution)/shard_map/ppermute | solution.py:817

commit v4 on v3

--- a/solution.py
+++ b/solution.py
@@ -16,9 +16,11 @@
 DEEP = 16
 ROWS = 16
 RIM = 3
+SIDE = 2 * RIM + 2 * (RIM - 1)
 EXT = ROWS + 2 * RIM
 HEATED = 7
 SWEEPS = 4
+PARTS = 4
 WIDE = ROWS + 2 * SWEEPS
 THICK = SLAB + SWEEPS
 SCALE = 1.0 / 16.0
@@ -42,7 +44,7 @@
     return jax.ShapeDtypeStruct(dims + (8, 128), F32)
 
 
-def call(kernel, outs, scratch=(), scalars=0, cost=0, raw_in=False, raw_out=False, room=4, alias={}):
+def call(kernel, outs, scratch=(), scalars=0, cost=0, raw_in=False, raw_out=False, room=4, alias={}, hold=lambda i: True):
     def held(out):
         return out if raw_out else pltpu.VMEM(out.shape, out.dtype)
 
@@ -51,8 +53,8 @@
         fields = args[scalars:]
         space = pltpu.HBM if raw_in else pltpu.VMEM
         fields = [pltpu.with_memory_space_constraint(v, space) for v in fields]
-        own = [pltpu.VMEM(v.shape, v.dtype) for v in fields] if raw_in else []
-        own += [pltpu.SemaphoreType.DMA((4,))] if raw_in else []
+        own = [(pltpu.VMEM if v.ndim > 1 else pltpu.SMEM)(v.shape, v.dtype) for i, v in enumerate(fields) if hold(i)] if raw_in else []
+        own += [pltpu.SemaphoreType.DMA((PARTS + len(fields),))] if raw_in else []
         return pl.pallas_call(
             kernel,
             out_shape=jax.tree.map(held, outs),
@@ -115,50 +117,62 @@
     return a * b * inverse(jnp.maximum(a + b, TINY))
 
 
-def pack_kernel(value, own, send, held, sems):
-    _, core = place()
-    parts = sems.shape[0]
-    size = value.shape[0] // parts
+def pack_field(value, held, sems):
+    size = value.shape[0] // PARTS
     copies = [
         pltpu.make_async_copy(value.at[pl.ds(p * size, size)], held.at[pl.ds(p * size, size)], sems.at[p])
-        for p in range(parts)
+        for p in range(PARTS)
     ]
     for copy in copies:
         copy.start()
-    for p, copy in enumerate(copies):
-        copy.wait()
-
-        def body(i, p=p):
-            n = p * size + i
-            for row in range(ROWS):
-                own[n, row] = at_row(held, n, core, row)
-                send[n, row] = at_row(held, n, 1 - core, row)
-
-        loop(size, body)
-
-
-def pack_args_kernel(classes, sink, category, link, contact, own, send, *held_sems):
-    _, core = place()
-    held, sems = held_sems[:4], held_sems[4]
-    copies = [
-        pltpu.make_async_copy(ref, to, sems.at[p])
-        for p, (ref, to) in enumerate(zip((sink, category, link, contact), held))
-    ]
+
+    def finish(own, send):
+        _, core = place()
+        for p, copy in enumerate(copies):
+            copy.wait()
+
+            def body(i, p=p):
+                n = p * size + i
+                for row in range(ROWS):
+                    own[n, row] = at_row(held, n, core, row)
+                    send[n, row] = at_row(held, n, 1 - core, row)
+
+            loop(size, body)
+
+    return finish
+
+
+def pack_kernel(value, own, send, held, sems):
+    pack_field(value, held, sems)(own, send)
+
+
+def first_pack_kernel(
+    value, sink, category, link, contact, classes, t_own, t_send, sink_, category_, link_, contact_, table, held, classes_, sems
+):
+    finish = pack_field(value, held, sems)
+    raw = ((classes, classes_), (sink, sink_), (category, category_), (link, link_), (contact, contact_))
+    copies = [pltpu.make_async_copy(ref, to, sems.at[PARTS + p]) for p, (ref, to) in enumerate(raw)]
     for copy in copies:
         copy.start()
+    finish(t_own, t_send)
     for copy in copies:
         copy.wait()
-    sink, category, link, contact = held
+    for number in range(8):
+        table[number] = jnp.full((8, 128), classes_[number] * SCALE, F32)
+
+
+def pack_args_kernel(sink, category, link, contact, classes, own, send):
+    _, core = place()
 
     def body(n):
         for row in range(ROWS):
             for chunk, out in ((core, own), (1 - core, send)):
                 kind = at_row(category, n, chunk, row)
-                table = jnp.full((8, 128), classes[0], F32)
+                table = classes[0]
                 for number in range(1, 8):
                     table = jnp.where(kind == number, classes[number], table)
                 out[n, row] = at_row(sink, n, chunk, row)
-                out[OWN + n, row] = table * SCALE
+                out[OWN + n, row] = table
                 out[2 * OWN + n, row] = at_row(link, n, chunk, row).astype(F32) * (via_conductance * SCALE)
                 out[3 * OWN + n, row] = at_row(contact, n, chunk, row).astype(F32) * (
                     pad_conductance * SCALE
@@ -167,34 +181,32 @@
     loop(OWN, body)
 
 
-def weigh(weights, parts, acc):
-    def rows(block):
-        total = [jnp.zeros((8, 128), F32)] * (4 * LAYERS)
+def weigh(weights, parts, acc, first_layer=0):
+    layers, rows = acc.shape[:2]
+    size = 48 // layers
+
+    def block_of(block):
+        total = [jnp.zeros((8, 128), F32)] * (size * layers)
         for ref, first, base in parts:
 
             def step(z, total):
-                field = [ref[first + z, block * 4 + k] for k in range(4)]
+                field = [ref[first + z, block * size + k] for k in range(size)]
                 out = []
-                for layer in range(LAYERS):
-                    w = weights[layer, base + z]
-                    out += [total[layer * 4 + k] + w * field[k] for k in range(4)]
+                for layer in range(layers):
+                    w = weights[first_layer + layer, base + z]
+                    out += [total[layer * size + k] + w * field[k] for k in range(size)]
                 return tuple(out)
 
             total = lax.fori_loop(0, DEEP, step, tuple(total), unroll=16)
-        for layer in range(LAYERS):
-            for k in range(4):
-                acc[layer, block * 4 + k] = total[layer * 4 + k]
-
-    loop(ROWS // 4, rows)
+        for layer in range(layers):
+            for k in range(size):
+                acc[layer, block * size + k] = total[layer * size + k]
+
+    loop(rows // size, block_of, 1)
 
 
 def heat_kernel(weights, t_own, t_got, part):
-    far, core = place()
-    weigh(
-        weights,
-        ((t_own, 0, SLAB * far + DEEP * core), (t_got, 0, SLAB * far + DEEP * (1 - core))),
-        part,
-    )
+    weigh(weights, heat_parts(t_own, t_got), part)
 
 
 def merge_kernel(part, a_own, a_got, a6, s_far, s_core_far, s_tile_far, s_core, s_tile):
@@ -216,7 +228,7 @@
             s_core_far[n, k] = part[5 * (1 - far) + n, to_core + k]
             s_tile_far[n, k] = part[5 * (1 - far) + n, to_tile + k]
             s_core[n, k] = part[5 * far + n, to_core + k]
-            s_tile[n, k] = part[5 * far + n, to_tile + k]
+            s_tile[n * RIM + k] = part[5 * far + n, to_tile + k]
 
     loop(HEATED, heats)
     edge = 5 * (1 - far)
@@ -231,7 +243,13 @@
         for ch in range(4):
             for k in range(RIM):
                 s_core[HEATED + ch * HALF + o, k] = a6[ch, o, to_core + k]
-                s_tile[HEATED + ch * HALF + o, k] = a6[ch, o, to_tile + k]
+        first = HEATED * RIM + o * SIDE
+        for k in range(RIM):
+            s_tile[first + k] = a6[0, o, to_tile + k]
+            s_tile[first + RIM + k] = a6[1, o, to_tile + k]
+        for k in range(RIM - 1):
+            s_tile[first + 2 * RIM + k] = a6[2, o, to_tile + core + k]
+            s_tile[first + 3 * RIM - 1 + k] = a6[3, o, to_tile + core + k]
 
     loop(HALF, args)
 
@@ -267,7 +285,7 @@
             one(RIM + k, part[5 * far + n, k] + g_far[n, k])
         for k in range(RIM):
             one(from_core + k, g_core[n, k] + g_core_far[n, k])
-            one(from_tile + k, g_tile[n, k] + g_tile_far[n, k])
+            one(from_tile + k, g_tile[n * RIM + k] + g_tile_far[n, k])
 
     loop(HEATED, heats)
     lower = far.astype(F32)
@@ -300,7 +318,14 @@
             one(RIM + k, *[a6[ch, o, k] for ch in range(4)])
         for k in range(RIM):
             one(from_core + k, *[g_core[HEATED + ch * HALF + o, k] for ch in range(4)])
-            one(from_tile + k, *[g_tile[HEATED + ch * HALF + o, k] for ch in range(4)])
+        first = HEATED * RIM + o * SIDE
+        for k in range(RIM):
+            v0[o + 1, from_tile + k] = g_tile[first + k]
+            lat[o, from_tile + k] = g_tile[first + RIM + k] * inv[o + far, from_tile + k]
+        for k in range(RIM - 1):
+            row = from_tile + 1 - core + k
+            vert[o + 1, row] = g_tile[first + 2 * RIM + k] * inv[o + far, row]
+            ground[o, row] = g_tile[first + 3 * RIM - 1 + k]
 
     loop(HALF, fields)
     last = (sub == 7) & (lane == 127)
@@ -699,7 +724,7 @@
 def sweeps_kernel(
     split, weights, power, p_far, p_core, p_core_far, p_tile, p_tile_far,
     warm, deep_edge, row_edge, col_edge, turn,
-    out, s_out, final, s_final,
+    out, s_out, s_final,
     joule, source, one, two,
 ):
     far, core = place()
@@ -756,6 +781,7 @@
             relax(n, src, range(sweep, WIDE - sweep), put, *fields)
 
         loop(THICK - sweep, step, 5)
+
     for ref, half in ((out, core), (s_out, 1 - core)):
 
         def final_step(i, ref=ref, half=half):
@@ -765,27 +791,27 @@
             relax(SWEEPS * far + DEEP * half + i, one, range(SWEEPS, SWEEPS + ROWS), put, *fields)
 
         loop(DEEP, final_step)
-    weigh(
-        weights,
-        ((out, 0, SLAB * far + DEEP * core), (s_out, 0, SLAB * far + DEEP * (1 - core))),
-        final,
-    )
-
-    def sends(o):
-        for k in range(ROWS):
-            s_final[o, k] = final[HALF * (1 - far) + o, k]
-
-    loop(HALF, sends)
+    weigh(weights, heat_parts(out, s_out), s_final, HALF * (1 - far))
+
+
+def heat_parts(own, got):
+    far, core = place()
+    return ((own, 0, SLAB * far + DEEP * core), (got, 0, SLAB * far + DEEP * (1 - core)))
+
+
+def own_heat_kernel(weights, out, s_out, final):
+    far, _ = place()
+    weigh(weights, heat_parts(out, s_out), final, HALF * far)
 
 
 def update_kernel(final, got, a6, mine, send):
-    far, core = place()
+    _, core = place()
 
     def body(n):
         for half, out in ((core, mine), (1 - core, send)):
             o = OWN * half + n
             for k in range(ROWS):
-                heat = final[HALF * far + o, k] + got[o, k]
+                heat = final[o, k] + got[o, k]
                 out[n, k] = (16.0 * a6[1, o, k]) * inverse(1.0 + thermal_slope * heat)
 
     loop(OWN, body)
@@ -881,12 +907,16 @@
     probe_weighting,
 ):
     weights, split = probe_weighting, dissipation_split.T
-    t_own, t_send = pack(beginning_warmth)
+    args = [raw_view(v) for v in (sink_current, metal_category, upward_link_flag, supply_contact_flag)]
+    t_own, t_send, *fetched = call(
+        first_pack_kernel,
+        [shaped(DEEP, ROWS)] * 2 + [jax.ShapeDtypeStruct(v.shape, v.dtype) for v in args] + [shaped(8)],
+        cost=2,
+        raw_in=True,
+        hold=lambda i: i in (0, len(args) + 1),
+    )(raw_view(beginning_warmth), *args, baseline_admittance)
     t_got = to_core(t_send)
-    a_own, a_send = call(pack_args_kernel, [shaped(4 * OWN, ROWS)] * 2, scalars=1, cost=3, raw_in=True)(
-        baseline_admittance,
-        *[raw_view(v) for v in (sink_current, metal_category, upward_link_flag, supply_contact_flag)],
-    )
+    a_own, a_send = call(pack_args_kernel, [shaped(4 * OWN, ROWS)] * 2, cost=1)(*fetched)
     a_got = to_core(a_send)
     part = call(heat_kernel, shaped(LAYERS, ROWS), scalars=1, cost=3, room=2)(weights, t_own, t_got)
     a6, s_far, s_core_far, s_tile_far, s_core, s_tile = call(
@@ -897,7 +927,7 @@
             shaped(HEATED + 2, RIM),
             shaped(HEATED + 2, RIM),
             shaped(HEATED + 4 * HALF, RIM),
-            shaped(HEATED + 4 * HALF, RIM),
+            shaped(HEATED * RIM + HALF * SIDE),
         ],
         cost=1.5,
         room=2,
@@ -956,15 +986,16 @@
         cost=4,
         alias={i: i for i in range(6)},
     )(*inner, g_core, g_rim, g_deep)
-    out, s_out, final, s_final = call(
+    out, s_out, s_final = call(
         sweeps_kernel,
-        [shaped(DEEP, ROWS), shaped(DEEP, ROWS), shaped(LAYERS, ROWS), shaped(HALF, ROWS)],
+        [shaped(DEEP, ROWS), shaped(DEEP, ROWS), shaped(HALF, ROWS)],
         scratch=((LAYERS, WIDE), (THICK, WIDE), (THICK + 2, WIDE), (THICK + 2, WIDE)),
         scalars=2,
-        cost=25,
+        cost=14,
         room=14,
     )(split, weights, power, p_far, q_core, q_core_far, q_tile, q_tile_far, warm, *edges)
     g_final = to_far(s_final)
+    final = call(own_heat_kernel, shaped(HALF, ROWS), scalars=1, cost=1.4, room=2)(weights, out, s_out)
     final_warmth = unpack(out, to_core(s_out))
     g_final = tied(g_final, final_warmth)
     mine, s_mine = call(update_kernel, [shaped(OWN, ROWS)] * 2, cost=0.4)(final, g_final, a6)

time: 143 us -> 141 us (0.986)
  waiting for transfers between devices: 49.3 us -> 47.8 us
    pallas_call x17 -> x18, Pallas kernels: 38.8 us -> 38.4 us  [run(): pl.pallas_call(kernel, out_shape=jax.tree.map(held, outs), in_specs=smem...]
where the time goes in v4:
time: 141 us
  starting transfers between devices  53.5 us (38%)
  waiting for transfers between devices  47.8 us (34%)
  Pallas kernels  38.4 us (27%)
    pallas_call x18, Pallas kernels, run(): pl.pallas_call(kernel, out_shape=jax.tree.map(held, outs), in_specs=smem...  38.4 us
    ppermute x10, starting transfers between devices, to_core(): return lax.ppermute(value, 'therm', [(i, i ^ 1) for i in range(4)])  14.8 us
    ppermute x5, waiting for transfers between devices, to_far(): return lax.ppermute(value, 'therm', [(i, i ^ 2) for i in range(4)])  14.7 us
    ppermute x3, waiting for transfers between devices, along_core_and_x(): peers.append(lax.ppermute(values, ('tile', 'therm'), pairs))  12.5 us
    ppermute x5, starting transfers between devices, to_tile(): return lax.ppermute(value, ('tile', 'therm'), pairs)  12 us
    ppermute x2, waiting for transfers between devices, to_core_far(): return lax.ppermute(value, 'therm', [(i, i ^ 3) for i in range(4)])  11.5 us
    ppermute x6, starting transfers between devices, along_tile(): lax.ppermute(values, 'tile', [(t, t ^ unit * k) for t in range(lax.axis_s...  8.64 us
    ppermute x2, starting transfers between devices, to_core_far(): return lax.ppermute(value, 'therm', [(i, i ^ 3) for i in range(4)])  7.74 us
  transfers between devices with their start and end apart: 31, of which 16 were waited for; matrix products, arithmetic and copies ran while one was open for 0% of the time, Pallas kernels for 13%

profile of v4, /device:TPU:25, one launch (start us, length us, event | category | flops | bytes accessed | tf_op | source)
XLA Modules:
  0.0 140.8 jit_solution(10798466935821266462)
XLA Ops:
  0.6 2.1 %shard_map.112 = (f32[16,16,8,128]{3,2,1,0:T(8,128)S(1)}, f32[16,16,8,128]{3,2,1,0:T(8,128)S(1)}, f32[3,4,64,128]{3,2,1,0:T(8,128)S(1)}, s32[3,4,64,128]{3,2,1,0...) custom-call(f32[16,4,64,128]{3,2,1,0:T(8,128)} %bitcast.47, ...), custom_call_target="tpu_custom_call" | custom-call | bytes 6800000 | tf_op jit(solution)/shard_map/pallas_call | solution.py:58
  2.7 0.8 collective-permute-start
  4.0 1.8 %collective-permute-done.t_got = f32[16,16,8,128]{3,2,1,0:T(8,128)S(1)} collective-permute-done((f32[16,16,8,128]{3,2,1,0:T(8,128)S(1)}, f32[16,16,8,128]{3,2,1,0:T(8,128)S(1)}, u32[]{:S(2)}, u32[]{:S(2)}) %collective-permute-start) | collective-permute-done | bytes 1048608 | tf_op jit(solution)/shard_map/ppermute | solution.py:843
  5.8 3.0 %shard_map.113.part = f32[12,16,8,128]{3,2,1,0:T(8,128)S(1)} custom-call(f32[12,64]{1,0:T(8,128)S(1)} %copy-done, f32[16,16,8,128]{3,2,1,0:T(8,128)S(1)} %get-tuple-element.100.t_own, f32[16,16,8,128]{3,2,1,0:T(8,128)S(1)} %collective-permute-done.t_got), custom_call_target="tpu_custom_call" | custom-call | bytes 10200000 | tf_op jit(solution)/shard_map/pallas_call | solution.py:58
  9.1 2.8 %collective-permute-start.2 = (f32[9,16,8,128]{3,2,1,0:T(8,128)S(1)}, f32[9,16,8,128]{3,2,1,0:T(8,128)S(1)}, u32[]{:S(2)}, u32[]{:S(2)}) collective-permute-start(f32[9,16,8,128]{3,2,1,0:T(8,128)S(1)} %get-tuple-element.79), channel_id=1, source_target_pairs={{0,2},{1,3},{2,0},{3,1},{4,6},{5,7},{6,4},{7,5},{8,10},{9,11},{10,... | collective-permute-start | bytes 1769480 | tf_op jit(solution)/shard_map/ppermute | solution.py:847
  11.9 0.7 collective-permute-start.5
  12.6 2.1 %collective-permute-start.6 = (f32[81,8,128]{2,1,0:T(8,128)S(1)}, f32[81,8,128]{2,1,0:T(8,128)S(1)}, u32[]{:S(2)}, u32[]{:S(2)}) collective-permute-start(f32[81,8,128]{2,1,0:T(8,128)S(1)} %get-tuple-element.83), channel_id=1, source_target_pairs={{1,4},{4,1},{3,6},{6,3},{5,8},{8,5},{7,10},{10,7},{9,12},{12,9},{1... | collective-permute-start | bytes 995336 | tf_op jit(solution)/shard_map/ppermute | solution.py:861
  14.7 5.9 %collective-permute-start.3 = (f32[9,3,8,128]{3,2,1,0:T(8,128)S(1)}, f32[9,3,8,128]{3,2,1,0:T(8,128)S(1)}, u32[]{:S(2)}, u32[]{:S(2)}) collective-permute-start(f32[9,3,8,128]{3,2,1,0:T(8,128)S(1)} %get-tuple-element.80), channel_id=1, source_target_pairs={{0,3},{1,2},{2,1},{3,0},{4,7},{5,6},{6,5},{7,4},{8,11},{9,10},{10,... | collective-permute-start | bytes 331784 | tf_op jit(solution)/shard_map/ppermute | solution.py:851
  20.5 1.9 %collective-permute-start.4 = (f32[9,3,8,128]{3,2,1,0:T(8,128)S(1)}, f32[9,3,8,128]{3,2,1,0:T(8,128)S(1)}, u32[]{:S(2)}, u32[]{:S(2)}) collective-permute-start(f32[9,3,8,128]{3,2,1,0:T(8,128)S(1)} %get-tuple-element.81), channel_id=1, source_target_pairs={{1,6},{6,1},{3,4},{4,3},{5,10},{10,5},{7,8},{8,7},{9,14},{14,9},{1... | collective-permute-start | bytes 331784 | tf_op jit(solution)/shard_map/ppermute | solution.py:861
  22.4 1.7 %shard_map.117 = (f32[16,16,8,128]{3,2,1,0:T(8,128)S(1)}, f32[16,16,8,128]{3,2,1,0:T(8,128)S(1)}) custom-call(f32[16,4,64,128]{3,2,1,0:T(8,128)} %bitcast.48), custom_call_target="tpu_custom_call" | custom-call | bytes 6800000 | tf_op jit(solution)/shard_map/pallas_call | solution.py:58
  24.1 11.4 %collective-permute-done.3.g_core_far = f32[9,3,8,128]{3,2,1,0:T(8,128)S(1)} collective-permute-done((f32[9,3,8,128]{3,2,1,0:T(8,128)S(1)}, f32[9,3,8,128]{3,2,1,0:T(8,128)S(1)}, u32[]{:S(2)}, u32[]{:S(2)}) %collective-permute-start.3) | collective-permute-done | bytes 110624 | tf_op jit(solution)/shard_map/ppermute | solution.py:851
  35.5 2.3 %shard_map.116 = (f32[8,22,8,128]{3,2,1,0:T(8,128)S(1)}, f32[8,22,8,128]{3,2,1,0:T(8,128)S(1)}, f32[8,22,8,128]{3,2,1,0:T(8,128)S(1)}, f32[6,22,8,128]{3,2,1,0:T...) custom-call(f32[12,16,8,128]{3,2,1,0:T(8,128)S(1)} %shard_map.113.pa, ...), custom_call_target="tpu_custom_call" | custom-call | bytes 10200000 | tf_op jit(solution)/shard_map/pallas_call | solution.py:58
  37.8 1.1 collective-permute-start.7
  38.9 1.7 %collective-permute-start.8 = (f32[2,18,8,128]{3,2,1,0:T(8,128)S(1)}, f32[2,18,8,128]{3,2,1,0:T(8,128)S(1)}, u32[]{:S(2)}, u32[]{:S(2)}) collective-permute-start(f32[2,18,8,128]{3,2,1,0:T(8,128)S(1)} %get-tuple-element.88), channel_id=1, source_target_pairs={{0,2},{1,3},{2,0},{3,1},{4,6},{5,7},{6,4},{7,5},{8,10},{9,11},{10,... | collective-permute-start | bytes 442376 | tf_op jit(solution)/shard_map/ppermute | solution.py:847
  40.6 0.5 collective-permute-done.7.k_got
  41.8 2.3 %collective-permute-start.14 = (f32[2,32,4,8,128]{4,3,2,1,0:T(8,128)S(1)}, f32[2,32,4,8,128]{4,3,2,1,0:T(8,128)S(1)}, u32[]{:S(2)}, u32[]{:S(2)}) collective-permute-start(f32[2,32,4,8,128]{4,3,2,1,0:T(8,128)S(1)} %get-tuple-element.90), channel_id=1, source_target_pairs={{1,4},{4,1},{3,6},{6,3},{5,8},{8,5},{7,10},{10,7},{9,12},{12,9},{1... | collective-permute-start | bytes 3145736 | tf_op jit(solution)/shard_map/ppermute | solution.py:861
  44.1 1.7 %collective-permute-done.8.got = f32[2,18,8,128]{3,2,1,0:T(8,128)S(1)} collective-permute-done((f32[2,18,8,128]{3,2,1,0:T(8,128)S(1)}, f32[2,18,8,128]{3,2,1,0:T(8,128)S(1)}, u32[]{:S(2)}, u32[]{:S(2)}) %collective-permute-start.8) | collective-permute-done | bytes 147488 | tf_op jit(solution)/shard_map/ppermute | solution.py:847
  45.8 0.9 shard_map.119
  46.7 2.2 %collective-permute-start.9 = (f32[2,8,128]{2,1,0:T(8,128)S(1)}, f32[2,8,128]{2,1,0:T(8,128)S(1)}, u32[]{:S(2)}, u32[]{:S(2)}) collective-permute-start(f32[2,8,128]{2,1,0:T(8,128)S(1)} %get-tuple-element.98), channel_id=1, source_target_pairs={{0,1},{1,0},{2,3},{3,2},{4,5},{5,4},{6,7},{7,6},{8,9},{9,8},{10,11... | collective-permute-start | bytes 24584 | tf_op jit(solution)/shard_map/ppermute | solution.py:843
  48.9 0.8 collective-permute-done.9
  49.8 2.7 %collective-permute-start.11 = (f32[2,8,128]{2,1,0:T(8,128)S(1)}, f32[2,8,128]{2,1,0:T(8,128)S(1)}, u32[]{:S(2)}, u32[]{:S(2)}) collective-permute-start(f32[2,8,128]{2,1,0:T(8,128)S(1)} %pad_maximum_fusion), channel_id=1, source_target_pairs={{0,6},{1,7},{2,4},{3,5},{4,2},{5,3},{6,0},{7,1},{8,14},{9,15},{10,... | collective-permute-start | bytes 24584 | tf_op jit(solution)/shard_map/ppermute | solution.py:878
  53.0 4.2 %shard_map.121 = (f32[38,24,8,128]{3,2,1,0:T(8,128)S(1)}, f32[36,24,8,128]{3,2,1,0:T(8,128)S(1)}, f32[37,24,8,128]{3,2,1,0:T(8,128)S(1)}, f32[36,24,8,128]{3,2,1...) custom-call(f32[16,16,8,128]{3,2,1,0:T(8,128)S(1)} %get-tuple-element.100.t_own, ...), custom_call_target="tpu_custom_call" | custom-call | bytes 18700000 | tf_op jit(solution)/shard_map/pallas_call | solution.py:58
  57.2 12.5 %collective-permute-done.12 = f32[2,8,128]{2,1,0:T(8,128)S(1)} collective-permute-done((f32[2,8,128]{2,1,0:T(8,128)S(1)}, f32[2,8,128]{2,1,0:T(8,128)S(1)}, u32[]{:S(2)}, u32[]{:S(2)}) %collective-permute-start.12) | collective-permute-done | bytes 8224 | tf_op jit(solution)/shard_map/ppermute | solution.py:878
  69.9 2.2 %collective-permute-start.16 = (f32[2,8,128]{2,1,0:T(8,128)S(1)}, f32[2,8,128]{2,1,0:T(8,128)S(1)}, u32[]{:S(2)}, u32[]{:S(2)}) collective-permute-start(f32[2,8,128]{2,1,0:T(8,128)S(1)} %pad_maximum_fusion.1), channel_id=1, source_target_pairs={{0,8},{4,12},{8,0},{12,4},{16,24},{20,28},{24,16},{28,20},{32,40},... | collective-permute-start | bytes 24584 | tf_op jit(solution)/shard_map/ppermute | solution.py:886
  72.1 2.1 %collective-permute-start.15 = (f32[2,8,128]{2,1,0:T(8,128)S(1)}, f32[2,8,128]{2,1,0:T(8,128)S(1)}, u32[]{:S(2)}, u32[]{:S(2)}) collective-permute-start(f32[2,8,128]{2,1,0:T(8,128)S(1)} %pad_maximum_fusion.1), channel_id=1, source_target_pairs={{0,16},{4,20},{8,24},{12,28},{16,0},{20,4},{24,8},{28,12},{32,48},... | collective-permute-start | bytes 24584 | tf_op jit(solution)/shard_map/ppermute | solution.py:886
  74.6 1.0 collective-permute-start.21
  76.1 1.8 %collective-permute-done.17 = f32[2,8,128]{2,1,0:T(8,128)S(1)} collective-permute-done((f32[2,8,128]{2,1,0:T(8,128)S(1)}, f32[2,8,128]{2,1,0:T(8,128)S(1)}, u32[]{:S(2)}, u32[]{:S(2)}) %collective-permute-start.17) | collective-permute-done | bytes 8224 | tf_op jit(solution)/shard_map/ppermute | solution.py:886
  78.0 1.1 collective-permute-start.20
  79.1 0.7 collective-permute-start.19
  79.8 2.1 %collective-permute-start.18 = (f32[2,8,128]{2,1,0:T(8,128)S(1)}, f32[2,8,128]{2,1,0:T(8,128)S(1)}, u32[]{:S(2)}, u32[]{:S(2)}) collective-permute-start(f32[2,8,128]{2,1,0:T(8,128)S(1)} %pad_maximum_fusion.2), channel_id=1, source_target_pairs={{0,64},{4,68},{8,72},{12,76},{16,80},{20,84},{24,88},{28,92},{32,9... | collective-permute-start | bytes 24584 | tf_op jit(solution)/shard_map/ppermute | solution.py:886
  82.1 2.0 %collective-permute-done.18 = f32[2,8,128]{2,1,0:T(8,128)S(1)} collective-permute-done((f32[2,8,128]{2,1,0:T(8,128)S(1)}, f32[2,8,128]{2,1,0:T(8,128)S(1)}, u32[]{:S(2)}, u32[]{:S(2)}) %collective-permute-start.18) | collective-permute-done | bytes 8224 | tf_op jit(solution)/shard_map/ppermute | solution.py:886
  84.1 5.8 %collective-permute-done.21.g_far = f32[2,76,8,128]{3,2,1,0:T(8,128)S(1)} collective-permute-done((f32[2,76,8,128]{3,2,1,0:T(8,128)S(1)}, f32[2,76,8,128]{3,2,1,0:T(8,128)S(1)}, u32[]{:S(2)}, u32[]{:S(2)}) %collective-permute-start.21) | collective-permute-done | bytes 622624 | tf_op jit(solution)/shard_map/ppermute | solution.py:847
  89.9 1.0 shard_map.122
  91.1 3.7 %collective-permute-start.24 = (f32[6,3,8,128]{3,2,1,0:T(8,128)S(1)}, f32[6,3,8,128]{3,2,1,0:T(8,128)S(1)}, u32[]{:S(2)}, u32[]{:S(2)}) collective-permute-start(f32[6,3,8,128]{3,2,1,0:T(8,128)S(1)} %get-tuple-element.115), channel_id=1, source_target_pairs={{0,1},{1,0},{2,3},{3,2},{4,5},{5,4},{6,7},{7,6},{8,9},{9,8},{10,11... | collective-permute-start | bytes 221192 | tf_op jit(solution)/shard_map/ppermute | solution.py:843
  94.8 1.9 %collective-permute-start.25 = (f32[6,3,8,128]{3,2,1,0:T(8,128)S(1)}, f32[6,3,8,128]{3,2,1,0:T(8,128)S(1)}, u32[]{:S(2)}, u32[]{:S(2)}) collective-permute-start(f32[6,3,8,128]{3,2,1,0:T(8,128)S(1)} %get-tuple-element.115), channel_id=1, source_target_pairs={{0,3},{1,2},{2,1},{3,0},{4,7},{5,6},{6,5},{7,4},{8,11},{9,10},{10,... | collective-permute-start | bytes 221192 | tf_op jit(solution)/shard_map/ppermute | solution.py:851
  96.7 2.8 %collective-permute-start.26 = (f32[6,3,8,128]{3,2,1,0:T(8,128)S(1)}, f32[6,3,8,128]{3,2,1,0:T(8,128)S(1)}, u32[]{:S(2)}, u32[]{:S(2)}) collective-permute-start(f32[6,3,8,128]{3,2,1,0:T(8,128)S(1)} %get-tuple-element.116), channel_id=1, source_target_pairs={{1,4},{4,1},{3,6},{6,3},{5,8},{8,5},{7,10},{10,7},{9,12},{12,9},{1... | collective-permute-start | bytes 221192 | tf_op jit(solution)/shard_map/ppermute | solution.py:861
  99.5 3.0 %collective-permute-start.27 = (f32[6,3,8,128]{3,2,1,0:T(8,128)S(1)}, f32[6,3,8,128]{3,2,1,0:T(8,128)S(1)}, u32[]{:S(2)}, u32[]{:S(2)}) collective-permute-start(f32[6,3,8,128]{3,2,1,0:T(8,128)S(1)} %get-tuple-element.116), channel_id=1, source_target_pairs={{1,6},{6,1},{3,4},{4,3},{5,10},{10,5},{7,8},{8,7},{9,14},{14,9},{1... | collective-permute-start | bytes 221192 | tf_op jit(solution)/shard_map/ppermute | solution.py:861
  102.5 3.3 %shard_map.124 = (f32[38,24,8,128]{3,2,1,0:T(8,128)S(1)}, f32[36,24,8,128]{3,2,1,0:T(8,128)S(1)}, f32[37,24,8,128]{3,2,1,0:T(8,128)S(1)}, f32[36,24,8,128]{3,2,1...) custom-call(f32[38,24,8,128]{3,2,1,0:T(8,128)S(1)} %get-tuple-elemen, ...), custom_call_target="tpu_custom_call", output_to_operand_aliasing={{0}: (0, {}), {1}: (1, {}), {2}: (2, {}), {3}: (3, {}), {4}... | custom-call | bytes 13600000 | tf_op jit(solution)/shard_map/pallas_call | solution.py:58
  106.3 0.8 collective-permute-done.27.p_tile_far
  107.1 14.0 %shard_map.125 = (f32[16,16,8,128]{3,2,1,0:T(8,128)S(1)}, f32[16,16,8,128]{3,2,1,0:T(8,128)S(1)}, f32[6,16,8,128]{3,2,1,0:T(8,128)S(1)}) custom-call(f32[12,64]{1,0:T(8,128)S(1)} %bitcast.46, f32[12,64]{1,0:T(8,128)S(1)} %copy-done, f32[6,16,8,128]{3,2,1,0:T(8,128)S(1)} %get-tuple-element.114.power, f32[6,16,8,128]{3,2,1,0:T(8,128)S(1)} %collective-permute-done.23.p_far, ...), custom_call_target="tpu_custom_call" | custom-call | bytes 47600000 | tf_op jit(solution)/shard_map/pallas_call | solution.py:58
  121.0 4.5 %collective-permute-start.28 = (f32[16,16,8,128]{3,2,1,0:T(8,128)S(1)}, f32[16,16,8,128]{3,2,1,0:T(8,128)S(1)}, u32[]{:S(2)}, u32[]{:S(2)}) collective-permute-start(f32[16,16,8,128]{3,2,1,0:T(8,128)S(1)} %get-tuple-element.130.s_out), channel_id=1, source_target_pairs={{0,1},{1,0},{2,3},{3,2},{4,5},{5,4},{6,7},{7,6},{8,9},{9,8},{10,11... | collective-permute-start | bytes 3145736 | tf_op jit(solution)/shard_map/ppermute | solution.py:843
  125.6 1.2 collective-permute-start.29
  127.2 1.7 %shard_map.127.final = f32[6,16,8,128]{3,2,1,0:T(8,128)S(1)} custom-call(f32[12,64]{1,0:T(8,128)S(1)} %copy-done, f32[16,16,8,128]{3,2,1,0:T(8,128)S(1)} %get-tuple-element.129.own.out, f32[16,16,8,128]{3,2,1,0:T(8,128)S(1)} %get-tuple-element.130.s_out), custom_call_target="tpu_custom_call" | custom-call | bytes 4760000 | tf_op jit(solution)/shard_map/pallas_call | solution.py:58
  128.8 1.7 %shard_map.126 = f32[16,4,64,128]{3,2,1,0:T(8,128)} custom-call(f32[16,16,8,128]{3,2,1,0:T(8,128)S(1)} %get-tuple-element.129.own.out, f32[16,16,8,128]{3,2,1,0:T(8,128)S(1)} %collective-permute-done.28.got), custom_call_target="tpu_custom_call" | custom-call | bytes 5440000 | tf_op jit(solution)/shard_map/pallas_call | solution.py:58
  130.5 7.2 %collective-permute-done.29.got = f32[6,16,8,128]{3,2,1,0:T(8,128)S(1)} collective-permute-done((f32[6,16,8,128]{3,2,1,0:T(8,128)S(1)}, f32[6,16,8,128]{3,2,1,0:T(8,128)S(1)}, u32[]{:S(2)}, u32[]{:S(2)}) %collective-permute-start.29) | collective-permute-done | bytes 393248 | tf_op jit(solution)/shard_map/ppermute | solution.py:847
  137.9 1.0 collective-permute-start.30
  138.9 0.8 shard_map.123
  140.0 0.8 shard_map.129
  (48 shorter events, 4.8 us)
Async XLA Ops:
  0.6 5.1 %copy-start = (f32[12,64]{1,0:T(8,128)S(1)}, f32[12,64]{1,0:T(8,128)}, u32[]{:S(2)}) copy-start(f32[12,64]{1,0:T(8,128)} %weights.5) | copy-start | bytes 9220
  2.7 3.0 %collective-permute-start = (f32[16,16,8,128]{3,2,1,0:T(8,128)S(1)}, f32[16,16,8,128]{3,2,1,0:T(8,128)S(1)}, u32[]{:S(2)}, u32[]{:S(2)}) collective-permute-start(f32[16,16,8,128]{3,2,1,0:T(8,128)S(1)} %get-tuple-element.70), channel_id=1, source_target_pairs={{0,1},{1,0},{2,3},{3,2},{4,5},{5,4},{6,7},{7,6},{8,9},{9,8},{10,11... | collective-permute-start | bytes 3145736 | tf_op jit(solution)/shard_map/ppermute | solution.py:843
  3.9 4.9 %collective-permute-start.1 = (f32[12,16,8,128]{3,2,1,0:T(8,128)S(1)}, f32[12,16,8,128]{3,2,1,0:T(8,128)S(1)}, u32[]{:S(2)}, u32[]{:S(2)}) collective-permute-start(f32[12,16,8,128]{3,2,1,0:T(8,128)S(1)} %get-tuple-element.77), channel_id=1, source_target_pairs={{0,1},{1,0},{2,3},{3,2},{4,5},{5,4},{6,7},{7,6},{8,9},{9,8},{10,11... | collective-permute-start | bytes 2359304 | tf_op jit(solution)/shard_map/ppermute | solution.py:843
  9.1 26.4 %collective-permute-start.2 = (f32[9,16,8,128]{3,2,1,0:T(8,128)S(1)}, f32[9,16,8,128]{3,2,1,0:T(8,128)S(1)}, u32[]{:S(2)}, u32[]{:S(2)}) collective-permute-start(f32[9,16,8,128]{3,2,1,0:T(8,128)S(1)} %get-tuple-element.79), channel_id=1, source_target_pairs={{0,2},{1,3},{2,0},{3,1},{4,6},{5,7},{6,4},{7,5},{8,10},{9,11},{10,... | collective-permute-start | bytes 1769480 | tf_op jit(solution)/shard_map/ppermute | solution.py:847
  11.9 23.6 %collective-permute-start.5 = (f32[31,3,8,128]{3,2,1,0:T(8,128)S(1)}, f32[31,3,8,128]{3,2,1,0:T(8,128)S(1)}, u32[]{:S(2)}, u32[]{:S(2)}) collective-permute-start(f32[31,3,8,128]{3,2,1,0:T(8,128)S(1)} %get-tuple-element.82), channel_id=1, source_target_pairs={{0,1},{1,0},{2,3},{3,2},{4,5},{5,4},{6,7},{7,6},{8,9},{9,8},{10,11... | collective-permute-start | bytes 1142792 | tf_op jit(solution)/shard_map/ppermute | solution.py:843
  12.6 22.9 %collective-permute-start.6 = (f32[81,8,128]{2,1,0:T(8,128)S(1)}, f32[81,8,128]{2,1,0:T(8,128)S(1)}, u32[]{:S(2)}, u32[]{:S(2)}) collective-permute-start(f32[81,8,128]{2,1,0:T(8,128)S(1)} %get-tuple-element.83), channel_id=1, source_target_pairs={{1,4},{4,1},{3,6},{6,3},{5,8},{8,5},{7,10},{10,7},{9,12},{12,9},{1... | collective-permute-start | bytes 995336 | tf_op jit(solution)/shard_map/ppermute | solution.py:861
  14.7 20.8 %collective-permute-start.3 = (f32[9,3,8,128]{3,2,1,0:T(8,128)S(1)}, f32[9,3,8,128]{3,2,1,0:T(8,128)S(1)}, u32[]{:S(2)}, u32[]{:S(2)}) collective-permute-start(f32[9,3,8,128]{3,2,1,0:T(8,128)S(1)} %get-tuple-element.80), channel_id=1, source_target_pairs={{0,3},{1,2},{2,1},{3,0},{4,7},{5,6},{6,5},{7,4},{8,11},{9,10},{10,... | collective-permute-start | bytes 331784 | tf_op jit(solution)/shard_map/ppermute | solution.py:851
  20.5 15.0 %collective-permute-start.4 = (f32[9,3,8,128]{3,2,1,0:T(8,128)S(1)}, f32[9,3,8,128]{3,2,1,0:T(8,128)S(1)}, u32[]{:S(2)}, u32[]{:S(2)}) collective-permute-start(f32[9,3,8,128]{3,2,1,0:T(8,128)S(1)} %get-tuple-element.81), channel_id=1, source_target_pairs={{1,6},{6,1},{3,4},{4,3},{5,10},{10,5},{7,8},{8,7},{9,14},{14,9},{1... | collective-permute-start | bytes 331784 | tf_op jit(solution)/shard_map/ppermute | solution.py:861
  37.8 3.4 %collective-permute-start.7 = (f32[16,16,8,128]{3,2,1,0:T(8,128)S(1)}, f32[16,16,8,128]{3,2,1,0:T(8,128)S(1)}, u32[]{:S(2)}, u32[]{:S(2)}) collective-permute-start(f32[16,16,8,128]{3,2,1,0:T(8,128)S(1)} %get-tuple-element.89), channel_id=1, source_target_pairs={{0,1},{1,0},{2,3},{3,2},{4,5},{5,4},{6,7},{7,6},{8,9},{9,8},{10,11... | collective-permute-start | bytes 3145736 | tf_op jit(solution)/shard_map/ppermute | solution.py:843
  38.9 6.9 %collective-permute-start.8 = (f32[2,18,8,128]{3,2,1,0:T(8,128)S(1)}, f32[2,18,8,128]{3,2,1,0:T(8,128)S(1)}, u32[]{:S(2)}, u32[]{:S(2)}) collective-permute-start(f32[2,18,8,128]{3,2,1,0:T(8,128)S(1)} %get-tuple-element.88), channel_id=1, source_target_pairs={{0,2},{1,3},{2,0},{3,1},{4,6},{5,7},{6,4},{7,5},{8,10},{9,11},{10,... | collective-permute-start | bytes 442376 | tf_op jit(solution)/shard_map/ppermute | solution.py:847
  41.4 28.4 %collective-permute-start.13 = (f32[2,32,4,8,128]{4,3,2,1,0:T(8,128)S(1)}, f32[2,32,4,8,128]{4,3,2,1,0:T(8,128)S(1)}, u32[]{:S(2)}, u32[]{:S(2)}) collective-permute-start(f32[2,32,4,8,128]{4,3,2,1,0:T(8,128)S(1)} %get-tuple-element.99), channel_id=1, source_target_pairs={{0,1},{1,0},{2,3},{3,2},{4,5},{5,4},{6,7},{7,6},{8,9},{9,8},{10,11... | collective-permute-start | bytes 3145736 | tf_op jit(solution)/shard_map/ppermute | solution.py:843
  41.8 28.0 %collective-permute-start.14 = (f32[2,32,4,8,128]{4,3,2,1,0:T(8,128)S(1)}, f32[2,32,4,8,128]{4,3,2,1,0:T(8,128)S(1)}, u32[]{:S(2)}, u32[]{:S(2)}) collective-permute-start(f32[2,32,4,8,128]{4,3,2,1,0:T(8,128)S(1)} %get-tuple-element.90), channel_id=1, source_target_pairs={{1,4},{4,1},{3,6},{6,3},{5,8},{8,5},{7,10},{10,7},{9,12},{12,9},{1... | collective-permute-start | bytes 3145736 | tf_op jit(solution)/shard_map/ppermute | solution.py:861
  46.7 3.0 %collective-permute-start.9 = (f32[2,8,128]{2,1,0:T(8,128)S(1)}, f32[2,8,128]{2,1,0:T(8,128)S(1)}, u32[]{:S(2)}, u32[]{:S(2)}) collective-permute-start(f32[2,8,128]{2,1,0:T(8,128)S(1)} %get-tuple-element.98), channel_id=1, source_target_pairs={{0,1},{1,0},{2,3},{3,2},{4,5},{5,4},{6,7},{7,6},{8,9},{9,8},{10,11... | collective-permute-start | bytes 24584 | tf_op jit(solution)/shard_map/ppermute | solution.py:843
  49.7 20.0 %collective-permute-start.12 = (f32[2,8,128]{2,1,0:T(8,128)S(1)}, f32[2,8,128]{2,1,0:T(8,128)S(1)}, u32[]{:S(2)}, u32[]{:S(2)}) collective-permute-start(f32[2,8,128]{2,1,0:T(8,128)S(1)} %pad_maximum_fusion), channel_id=1, source_target_pairs={{0,4},{1,5},{2,6},{3,7},{4,0},{5,1},{6,2},{7,3},{8,12},{9,13},{10,... | collective-permute-start | bytes 24584 | tf_op jit(solution)/shard_map/ppermute | solution.py:878
  49.8 19.9 %collective-permute-start.11 = (f32[2,8,128]{2,1,0:T(8,128)S(1)}, f32[2,8,128]{2,1,0:T(8,128)S(1)}, u32[]{:S(2)}, u32[]{:S(2)}) collective-permute-start(f32[2,8,128]{2,1,0:T(8,128)S(1)} %pad_maximum_fusion), channel_id=1, source_target_pairs={{0,6},{1,7},{2,4},{3,5},{4,2},{5,3},{6,0},{7,1},{8,14},{9,15},{10,... | collective-permute-start | bytes 24584 | tf_op jit(solution)/shard_map/ppermute | solution.py:878
  52.5 17.2 %collective-permute-start.10 = (f32[2,8,128]{2,1,0:T(8,128)S(1)}, f32[2,8,128]{2,1,0:T(8,128)S(1)}, u32[]{:S(2)}, u32[]{:S(2)}) collective-permute-start(f32[2,8,128]{2,1,0:T(8,128)S(1)} %pad_maximum_fusion), channel_id=1, source_target_pairs={{0,2},{1,3},{2,0},{3,1},{4,6},{5,7},{6,4},{7,5},{8,10},{9,11},{10,... | collective-permute-start | bytes 24584 | tf_op jit(solution)/shard_map/ppermute | solution.py:878
  69.9 5.7 %collective-permute-start.16 = (f32[2,8,128]{2,1,0:T(8,128)S(1)}, f32[2,8,128]{2,1,0:T(8,128)S(1)}, u32[]{:S(2)}, u32[]{:S(2)}) collective-permute-start(f32[2,8,128]{2,1,0:T(8,128)S(1)} %pad_maximum_fusion.1), channel_id=1, source_target_pairs={{0,8},{4,12},{8,0},{12,4},{16,24},{20,28},{24,16},{28,20},{32,40},... | collective-permute-start | bytes 24584 | tf_op jit(solution)/shard_map/ppermute | solution.py:886
  72.1 4.0 %collective-permute-start.15 = (f32[2,8,128]{2,1,0:T(8,128)S(1)}, f32[2,8,128]{2,1,0:T(8,128)S(1)}, u32[]{:S(2)}, u32[]{:S(2)}) collective-permute-start(f32[2,8,128]{2,1,0:T(8,128)S(1)} %pad_maximum_fusion.1), channel_id=1, source_target_pairs={{0,16},{4,20},{8,24},{12,28},{16,0},{20,4},{24,8},{28,12},{32,48},... | collective-permute-start | bytes 24584 | tf_op jit(solution)/shard_map/ppermute | solution.py:886
  74.2 3.7 %collective-permute-start.17 = (f32[2,8,128]{2,1,0:T(8,128)S(1)}, f32[2,8,128]{2,1,0:T(8,128)S(1)}, u32[]{:S(2)}, u32[]{:S(2)}) collective-permute-start(f32[2,8,128]{2,1,0:T(8,128)S(1)} %pad_maximum_fusion.1), channel_id=1, source_target_pairs={{0,24},{4,28},{8,16},{12,20},{16,8},{20,12},{24,0},{28,4},{32,56},... | collective-permute-start | bytes 24584 | tf_op jit(solution)/shard_map/ppermute | solution.py:886
  74.6 15.3 %collective-permute-start.21 = (f32[2,76,8,128]{3,2,1,0:T(8,128)S(1)}, f32[2,76,8,128]{3,2,1,0:T(8,128)S(1)}, u32[]{:S(2)}, u32[]{:S(2)}) collective-permute-start(f32[2,76,8,128]{3,2,1,0:T(8,128)S(1)} %shard_map.120), channel_id=1, source_target_pairs={{0,2},{1,3},{2,0},{3,1},{4,6},{5,7},{6,4},{7,5},{8,10},{9,11},{10,... | collective-permute-start | bytes 1867784 | tf_op jit(solution)/shard_map/ppermute | solution.py:847
  78.0 4.1 %collective-permute-start.20 = (f32[2,8,128]{2,1,0:T(8,128)S(1)}, f32[2,8,128]{2,1,0:T(8,128)S(1)}, u32[]{:S(2)}, u32[]{:S(2)}) collective-permute-start(f32[2,8,128]{2,1,0:T(8,128)S(1)} %pad_maximum_fusion.2), channel_id=1, source_target_pairs={{0,96},{4,100},{8,104},{12,108},{16,112},{20,116},{24,120},{28,124... | collective-permute-start | bytes 24584 | tf_op jit(solution)/shard_map/ppermute | solution.py:886
  79.1 3.0 %collective-permute-start.19 = (f32[2,8,128]{2,1,0:T(8,128)S(1)}, f32[2,8,128]{2,1,0:T(8,128)S(1)}, u32[]{:S(2)}, u32[]{:S(2)}) collective-permute-start(f32[2,8,128]{2,1,0:T(8,128)S(1)} %pad_maximum_fusion.2), channel_id=1, source_target_pairs={{0,32},{4,36},{8,40},{12,44},{16,48},{20,52},{24,56},{28,60},{32,0... | collective-permute-start | bytes 24584 | tf_op jit(solution)/shard_map/ppermute | solution.py:886
  79.8 4.3 %collective-permute-start.18 = (f32[2,8,128]{2,1,0:T(8,128)S(1)}, f32[2,8,128]{2,1,0:T(8,128)S(1)}, u32[]{:S(2)}, u32[]{:S(2)}) collective-permute-start(f32[2,8,128]{2,1,0:T(8,128)S(1)} %pad_maximum_fusion.2), channel_id=1, source_target_pairs={{0,64},{4,68},{8,72},{12,76},{16,80},{20,84},{24,88},{28,92},{32,9... | collective-permute-start | bytes 24584 | tf_op jit(solution)/shard_map/ppermute | solution.py:886
  90.8 16.2 %collective-permute-start.23 = (f32[6,16,8,128]{3,2,1,0:T(8,128)S(1)}, f32[6,16,8,128]{3,2,1,0:T(8,128)S(1)}, u32[]{:S(2)}, u32[]{:S(2)}) collective-permute-start(f32[6,16,8,128]{3,2,1,0:T(8,128)S(1)} %get-tuple-element.114.power), channel_id=1, source_target_pairs={{0,2},{1,3},{2,0},{3,1},{4,6},{5,7},{6,4},{7,5},{8,10},{9,11},{10,... | collective-permute-start | bytes 1179656 | tf_op jit(solution)/shard_map/ppermute | solution.py:847
  91.1 14.7 %collective-permute-start.24 = (f32[6,3,8,128]{3,2,1,0:T(8,128)S(1)}, f32[6,3,8,128]{3,2,1,0:T(8,128)S(1)}, u32[]{:S(2)}, u32[]{:S(2)}) collective-permute-start(f32[6,3,8,128]{3,2,1,0:T(8,128)S(1)} %get-tuple-element.115), channel_id=1, source_target_pairs={{0,1},{1,0},{2,3},{3,2},{4,5},{5,4},{6,7},{7,6},{8,9},{9,8},{10,11... | collective-permute-start | bytes 221192 | tf_op jit(solution)/shard_map/ppermute | solution.py:843
  94.8 11.1 %collective-permute-start.25 = (f32[6,3,8,128]{3,2,1,0:T(8,128)S(1)}, f32[6,3,8,128]{3,2,1,0:T(8,128)S(1)}, u32[]{:S(2)}, u32[]{:S(2)}) collective-permute-start(f32[6,3,8,128]{3,2,1,0:T(8,128)S(1)} %get-tuple-element.115), channel_id=1, source_target_pairs={{0,3},{1,2},{2,1},{3,0},{4,7},{5,6},{6,5},{7,4},{8,11},{9,10},{10,... | collective-permute-start | bytes 221192 | tf_op jit(solution)/shard_map/ppermute | solution.py:851
  96.7 10.3 %copy-start.1 = (f32[64,12]{0,1:T(8,128)S(1)}, f32[64,12]{0,1:T(8,128)}, u32[]{:S(2)}) copy-start(f32[64,12]{0,1:T(8,128)} %param.16) | copy-start | bytes 9220
  96.7 9.6 %collective-permute-start.26 = (f32[6,3,8,128]{3,2,1,0:T(8,128)S(1)}, f32[6,3,8,128]{3,2,1,0:T(8,128)S(1)}, u32[]{:S(2)}, u32[]{:S(2)}) collective-permute-start(f32[6,3,8,128]{3,2,1,0:T(8,128)S(1)} %get-tuple-element.116), channel_id=1, source_target_pairs={{1,4},{4,1},{3,6},{6,3},{5,8},{8,5},{7,10},{10,7},{9,12},{12,9},{1... | collective-permute-start | bytes 221192 | tf_op jit(solution)/shard_map/ppermute | solution.py:861
  99.5 7.6 %collective-permute-start.27 = (f32[6,3,8,128]{3,2,1,0:T(8,128)S(1)}, f32[6,3,8,128]{3,2,1,0:T(8,128)S(1)}, u32[]{:S(2)}, u32[]{:S(2)}) collective-permute-start(f32[6,3,8,128]{3,2,1,0:T(8,128)S(1)} %get-tuple-element.116), channel_id=1, source_target_pairs={{1,6},{6,1},{3,4},{4,3},{5,10},{10,5},{7,8},{8,7},{9,14},{14,9},{1... | collective-permute-start | bytes 221192 | tf_op jit(solution)/shard_map/ppermute | solution.py:861
  121.0 7.8 %collective-permute-start.28 = (f32[16,16,8,128]{3,2,1,0:T(8,128)S(1)}, f32[16,16,8,128]{3,2,1,0:T(8,128)S(1)}, u32[]{:S(2)}, u32[]{:S(2)}) collective-permute-start(f32[16,16,8,128]{3,2,1,0:T(8,128)S(1)} %get-tuple-element.130.s_out), channel_id=1, source_target_pairs={{0,1},{1,0},{2,3},{3,2},{4,5},{5,4},{6,7},{7,6},{8,9},{9,8},{10,11... | collective-permute-start | bytes 3145736 | tf_op jit(solution)/shard_map/ppermute | solution.py:843
  125.6 12.2 %collective-permute-start.29 = (f32[6,16,8,128]{3,2,1,0:T(8,128)S(1)}, f32[6,16,8,128]{3,2,1,0:T(8,128)S(1)}, u32[]{:S(2)}, u32[]{:S(2)}) collective-permute-start(f32[6,16,8,128]{3,2,1,0:T(8,128)S(1)} %get-tuple-element.131), channel_id=1, source_target_pairs={{0,2},{1,3},{2,0},{3,1},{4,6},{5,7},{6,4},{7,5},{8,10},{9,11},{10,... | collective-permute-start | bytes 1179656 | tf_op jit(solution)/shard_map/ppermute | solution.py:847
  126.8 12.1 %collective-permute-start.22 = (f32[3,16,8,128]{3,2,1,0:T(8,128)S(1)}, f32[3,16,8,128]{3,2,1,0:T(8,128)S(1)}, u32[]{:S(2)}, u32[]{:S(2)}) collective-permute-start(f32[3,16,8,128]{3,2,1,0:T(8,128)S(1)} %get-tuple-element.113), channel_id=1, source_target_pairs={{0,1},{1,0},{2,3},{3,2},{4,5},{5,4},{6,7},{7,6},{8,9},{9,8},{10,11... | collective-permute-start | bytes 589832 | tf_op jit(solution)/shard_map/ppermute | solution.py:843
  137.9 2.0 %collective-permute-start.30 = (f32[3,16,8,128]{3,2,1,0:T(8,128)S(1)}, f32[3,16,8,128]{3,2,1,0:T(8,128)S(1)}, u32[]{:S(2)}, u32[]{:S(2)}) collective-permute-start(f32[3,16,8,128]{3,2,1,0:T(8,128)S(1)} %get-tuple-element.134), channel_id=1, source_target_pairs={{0,1},{1,0},{2,3},{3,2},{4,5},{5,4},{6,7},{7,6},{8,9},{9,8},{10,11... | collective-permute-start | bytes 589832 | tf_op jit(solution)/shard_map/ppermute | solution.py:843

commit v5 on v4

--- a/solution.py
+++ b/solution.py
@@ -85,7 +85,7 @@
     return ref[n, chunk * 2 + row // 8, pl.ds(row % 8, 8, stride=8), :]
 
 
-def loop(count, body, unroll=4):
+def loop(count, body, unroll=8):
     def step(i, carry):
         body(i)
         return carry
@@ -761,7 +761,7 @@
                 source[n, block * 4 + k] = total[k]
             return carry
 
-        lax.fori_loop(0, THICK, depth, 0, unroll=4)
+        lax.fori_loop(0, THICK, depth, 0, unroll=9)
 
     loop(WIDE // 4, sources)
     for ref in (one, two):
@@ -780,7 +780,7 @@
 
             relax(n, src, range(sweep, WIDE - sweep), put, *fields)
 
-        loop(THICK - sweep, step, 5)
+        loop(THICK - sweep, step, 7)
 
     for ref, half in ((out, core), (s_out, 1 - core)):
 
@@ -790,7 +790,7 @@
 
             relax(SWEEPS * far + DEEP * half + i, one, range(SWEEPS, SWEEPS + ROWS), put, *fields)
 
-        loop(DEEP, final_step)
+        loop(DEEP, final_step, 8)
     weigh(weights, heat_parts(out, s_out), s_final, HALF * (1 - far))
 
 

time: 141 us -> 140 us (level)
  Pallas kernels: 38.4 us -> 36.4 us
    pallas_call x18, Pallas kernels: 38.4 us -> 36.4 us  [run(): pl.pallas_call(kernel, out_shape=jax.tree.map(held, outs), in_specs=smem...]
  transfers between devices with their start and end apart: 31 -> 31, of which waited for: 16 -> 16; matrix products, arithmetic and copies ran while one was open for 0% -> 0% of each run, Pallas kernels for 13% -> 12%
where the time goes in v5:
time: 140 us; the launch traced here: 139 us
  starting transfers between devices  53.4 us (38%)
  waiting for transfers between devices  48.6 us (35%)
  Pallas kernels  36.4 us (26%)
    pallas_call x18, Pallas kernels, run(): pl.pallas_call(kernel, out_shape=jax.tree.map(held, outs), in_specs=smem...  36.4 us
    ppermute x5, waiting for transfers between devices, to_far(): return lax.ppermute(value, 'therm', [(i, i ^ 2) for i in range(4)])  14.8 us
    ppermute x10, starting transfers between devices, to_core(): return lax.ppermute(value, 'therm', [(i, i ^ 1) for i in range(4)])  14.7 us
    ppermute x3, waiting for transfers between devices, along_core_and_x(): peers.append(lax.ppermute(values, ('tile', 'therm'), pairs))  12.6 us
    ppermute x2, waiting for transfers between devices, to_core_far(): return lax.ppermute(value, 'therm', [(i, i ^ 3) for i in range(4)])  12.1 us
    ppermute x5, starting transfers between devices, to_tile(): return lax.ppermute(value, ('tile', 'therm'), pairs)  12 us
    ppermute x6, starting transfers between devices, along_tile(): lax.ppermute(values, 'tile', [(t, t ^ unit * k) for t in range(lax.axis_s...  8.65 us
    ppermute x2, starting transfers between devices, to_core_far(): return lax.ppermute(value, 'therm', [(i, i ^ 3) for i in range(4)])  7.74 us
  transfers between devices with their start and end apart: 31, of which 16 were waited for; matrix products, arithmetic and copies ran while one was open for 0% of the time, Pallas kernels for 12%

profile of v5, /device:TPU:25, one launch (start us, length us, event | category | flops | bytes accessed | tf_op | source)
XLA Modules:
  0.0 139.5 jit_solution(10108453245913881026)
XLA Ops:
  0.6 2.1 %shard_map.112 = (f32[16,16,8,128]{3,2,1,0:T(8,128)S(1)}, f32[16,16,8,128]{3,2,1,0:T(8,128)S(1)}, f32[3,4,64,128]{3,2,1,0:T(8,128)S(1)}, s32[3,4,64,128]{3,2,1,0...) custom-call(f32[16,4,64,128]{3,2,1,0:T(8,128)} %bitcast.47, ...), custom_call_target="tpu_custom_call" | custom-call | bytes 6800000 | tf_op jit(solution)/shard_map/pallas_call | solution.py:58
  2.7 0.8 collective-permute-start
  4.0 1.8 %collective-permute-done.t_got = f32[16,16,8,128]{3,2,1,0:T(8,128)S(1)} collective-permute-done((f32[16,16,8,128]{3,2,1,0:T(8,128)S(1)}, f32[16,16,8,128]{3,2,1,0:T(8,128)S(1)}, u32[]{:S(2)}, u32[]{:S(2)}) %collective-permute-start) | collective-permute-done | bytes 1048608 | tf_op jit(solution)/shard_map/ppermute | solution.py:843
  5.8 3.0 %shard_map.113.part = f32[12,16,8,128]{3,2,1,0:T(8,128)S(1)} custom-call(f32[12,64]{1,0:T(8,128)S(1)} %copy-done, f32[16,16,8,128]{3,2,1,0:T(8,128)S(1)} %get-tuple-element.100.t_own, f32[16,16,8,128]{3,2,1,0:T(8,128)S(1)} %collective-permute-done.t_got), custom_call_target="tpu_custom_call" | custom-call | bytes 10200000 | tf_op jit(solution)/shard_map/pallas_call | solution.py:58
  9.1 2.8 %collective-permute-start.2 = (f32[9,16,8,128]{3,2,1,0:T(8,128)S(1)}, f32[9,16,8,128]{3,2,1,0:T(8,128)S(1)}, u32[]{:S(2)}, u32[]{:S(2)}) collective-permute-start(f32[9,16,8,128]{3,2,1,0:T(8,128)S(1)} %get-tuple-element.79), channel_id=1, source_target_pairs={{0,2},{1,3},{2,0},{3,1},{4,6},{5,7},{6,4},{7,5},{8,10},{9,11},{10,... | collective-permute-start | bytes 1769480 | tf_op jit(solution)/shard_map/ppermute | solution.py:847
  11.9 0.6 collective-permute-start.5
  12.5 2.1 %collective-permute-start.6 = (f32[81,8,128]{2,1,0:T(8,128)S(1)}, f32[81,8,128]{2,1,0:T(8,128)S(1)}, u32[]{:S(2)}, u32[]{:S(2)}) collective-permute-start(f32[81,8,128]{2,1,0:T(8,128)S(1)} %get-tuple-element.83), channel_id=1, source_target_pairs={{1,4},{4,1},{3,6},{6,3},{5,8},{8,5},{7,10},{10,7},{9,12},{12,9},{1... | collective-permute-start | bytes 995336 | tf_op jit(solution)/shard_map/ppermute | solution.py:861
  14.7 5.9 %collective-permute-start.3 = (f32[9,3,8,128]{3,2,1,0:T(8,128)S(1)}, f32[9,3,8,128]{3,2,1,0:T(8,128)S(1)}, u32[]{:S(2)}, u32[]{:S(2)}) collective-permute-start(f32[9,3,8,128]{3,2,1,0:T(8,128)S(1)} %get-tuple-element.80), channel_id=1, source_target_pairs={{0,3},{1,2},{2,1},{3,0},{4,7},{5,6},{6,5},{7,4},{8,11},{9,10},{10,... | collective-permute-start | bytes 331784 | tf_op jit(solution)/shard_map/ppermute | solution.py:851
  20.5 1.9 %collective-permute-start.4 = (f32[9,3,8,128]{3,2,1,0:T(8,128)S(1)}, f32[9,3,8,128]{3,2,1,0:T(8,128)S(1)}, u32[]{:S(2)}, u32[]{:S(2)}) collective-permute-start(f32[9,3,8,128]{3,2,1,0:T(8,128)S(1)} %get-tuple-element.81), channel_id=1, source_target_pairs={{1,6},{6,1},{3,4},{4,3},{5,10},{10,5},{7,8},{8,7},{9,14},{14,9},{1... | collective-permute-start | bytes 331784 | tf_op jit(solution)/shard_map/ppermute | solution.py:861
  22.4 1.7 %shard_map.117 = (f32[16,16,8,128]{3,2,1,0:T(8,128)S(1)}, f32[16,16,8,128]{3,2,1,0:T(8,128)S(1)}) custom-call(f32[16,4,64,128]{3,2,1,0:T(8,128)} %bitcast.48), custom_call_target="tpu_custom_call" | custom-call | bytes 6800000 | tf_op jit(solution)/shard_map/pallas_call | solution.py:58
  24.1 11.4 %collective-permute-done.3.g_core_far = f32[9,3,8,128]{3,2,1,0:T(8,128)S(1)} collective-permute-done((f32[9,3,8,128]{3,2,1,0:T(8,128)S(1)}, f32[9,3,8,128]{3,2,1,0:T(8,128)S(1)}, u32[]{:S(2)}, u32[]{:S(2)}) %collective-permute-start.3) | collective-permute-done | bytes 110624 | tf_op jit(solution)/shard_map/ppermute | solution.py:851
  35.5 1.9 %shard_map.116 = (f32[8,22,8,128]{3,2,1,0:T(8,128)S(1)}, f32[8,22,8,128]{3,2,1,0:T(8,128)S(1)}, f32[8,22,8,128]{3,2,1,0:T(8,128)S(1)}, f32[6,22,8,128]{3,2,1,0:T...) custom-call(f32[12,16,8,128]{3,2,1,0:T(8,128)S(1)} %shard_map.113.pa, ...), custom_call_target="tpu_custom_call" | custom-call | bytes 10200000 | tf_op jit(solution)/shard_map/pallas_call | solution.py:58
  37.4 1.1 collective-permute-start.7
  38.5 1.8 %collective-permute-start.8 = (f32[2,18,8,128]{3,2,1,0:T(8,128)S(1)}, f32[2,18,8,128]{3,2,1,0:T(8,128)S(1)}, u32[]{:S(2)}, u32[]{:S(2)}) collective-permute-start(f32[2,18,8,128]{3,2,1,0:T(8,128)S(1)} %get-tuple-element.88), channel_id=1, source_target_pairs={{0,2},{1,3},{2,0},{3,1},{4,6},{5,7},{6,4},{7,5},{8,10},{9,11},{10,... | collective-permute-start | bytes 442376 | tf_op jit(solution)/shard_map/ppermute | solution.py:847
  41.4 2.3 %collective-permute-start.14 = (f32[2,32,4,8,128]{4,3,2,1,0:T(8,128)S(1)}, f32[2,32,4,8,128]{4,3,2,1,0:T(8,128)S(1)}, u32[]{:S(2)}, u32[]{:S(2)}) collective-permute-start(f32[2,32,4,8,128]{4,3,2,1,0:T(8,128)S(1)} %get-tuple-element.90), channel_id=1, source_target_pairs={{1,4},{4,1},{3,6},{6,3},{5,8},{8,5},{7,10},{10,7},{9,12},{12,9},{1... | collective-permute-start | bytes 3145736 | tf_op jit(solution)/shard_map/ppermute | solution.py:861
  43.6 1.8 %collective-permute-done.8.got = f32[2,18,8,128]{3,2,1,0:T(8,128)S(1)} collective-permute-done((f32[2,18,8,128]{3,2,1,0:T(8,128)S(1)}, f32[2,18,8,128]{3,2,1,0:T(8,128)S(1)}, u32[]{:S(2)}, u32[]{:S(2)}) %collective-permute-start.8) | collective-permute-done | bytes 147488 | tf_op jit(solution)/shard_map/ppermute | solution.py:847
  45.4 0.9 shard_map.119
  46.3 2.1 %collective-permute-start.9 = (f32[2,8,128]{2,1,0:T(8,128)S(1)}, f32[2,8,128]{2,1,0:T(8,128)S(1)}, u32[]{:S(2)}, u32[]{:S(2)}) collective-permute-start(f32[2,8,128]{2,1,0:T(8,128)S(1)} %get-tuple-element.98), channel_id=1, source_target_pairs={{0,1},{1,0},{2,3},{3,2},{4,5},{5,4},{6,7},{7,6},{8,9},{9,8},{10,11... | collective-permute-start | bytes 24584 | tf_op jit(solution)/shard_map/ppermute | solution.py:843
  48.4 0.8 collective-permute-done.9
  49.3 2.7 %collective-permute-start.11 = (f32[2,8,128]{2,1,0:T(8,128)S(1)}, f32[2,8,128]{2,1,0:T(8,128)S(1)}, u32[]{:S(2)}, u32[]{:S(2)}) collective-permute-start(f32[2,8,128]{2,1,0:T(8,128)S(1)} %pad_maximum_fusion), channel_id=1, source_target_pairs={{0,6},{1,7},{2,4},{3,5},{4,2},{5,3},{6,0},{7,1},{8,14},{9,15},{10,... | collective-permute-start | bytes 24584 | tf_op jit(solution)/shard_map/ppermute | solution.py:878
  52.6 4.1 %shard_map.121 = (f32[38,24,8,128]{3,2,1,0:T(8,128)S(1)}, f32[36,24,8,128]{3,2,1,0:T(8,128)S(1)}, f32[37,24,8,128]{3,2,1,0:T(8,128)S(1)}, f32[36,24,8,128]{3,2,1...) custom-call(f32[16,16,8,128]{3,2,1,0:T(8,128)S(1)} %get-tuple-element.100.t_own, ...), custom_call_target="tpu_custom_call" | custom-call | bytes 18700000 | tf_op jit(solution)/shard_map/pallas_call | solution.py:58
  56.7 12.6 %collective-permute-done.12 = f32[2,8,128]{2,1,0:T(8,128)S(1)} collective-permute-done((f32[2,8,128]{2,1,0:T(8,128)S(1)}, f32[2,8,128]{2,1,0:T(8,128)S(1)}, u32[]{:S(2)}, u32[]{:S(2)}) %collective-permute-start.12) | collective-permute-done | bytes 8224 | tf_op jit(solution)/shard_map/ppermute | solution.py:878
  69.4 2.2 %collective-permute-start.16 = (f32[2,8,128]{2,1,0:T(8,128)S(1)}, f32[2,8,128]{2,1,0:T(8,128)S(1)}, u32[]{:S(2)}, u32[]{:S(2)}) collective-permute-start(f32[2,8,128]{2,1,0:T(8,128)S(1)} %pad_maximum_fusion.1), channel_id=1, source_target_pairs={{0,8},{4,12},{8,0},{12,4},{16,24},{20,28},{24,16},{28,20},{32,40},... | collective-permute-start | bytes 24584 | tf_op jit(solution)/shard_map/ppermute | solution.py:886
  71.7 2.1 %collective-permute-start.15 = (f32[2,8,128]{2,1,0:T(8,128)S(1)}, f32[2,8,128]{2,1,0:T(8,128)S(1)}, u32[]{:S(2)}, u32[]{:S(2)}) collective-permute-start(f32[2,8,128]{2,1,0:T(8,128)S(1)} %pad_maximum_fusion.1), channel_id=1, source_target_pairs={{0,16},{4,20},{8,24},{12,28},{16,0},{20,4},{24,8},{28,12},{32,48},... | collective-permute-start | bytes 24584 | tf_op jit(solution)/shard_map/ppermute | solution.py:886
  74.1 1.0 collective-permute-start.21
  75.7 1.8 %collective-permute-done.17 = f32[2,8,128]{2,1,0:T(8,128)S(1)} collective-permute-done((f32[2,8,128]{2,1,0:T(8,128)S(1)}, f32[2,8,128]{2,1,0:T(8,128)S(1)}, u32[]{:S(2)}, u32[]{:S(2)}) %collective-permute-start.17) | collective-permute-done | bytes 8224 | tf_op jit(solution)/shard_map/ppermute | solution.py:886
  77.5 1.1 collective-permute-start.20
  78.6 0.7 collective-permute-start.19
  79.3 2.1 %collective-permute-start.18 = (f32[2,8,128]{2,1,0:T(8,128)S(1)}, f32[2,8,128]{2,1,0:T(8,128)S(1)}, u32[]{:S(2)}, u32[]{:S(2)}) collective-permute-start(f32[2,8,128]{2,1,0:T(8,128)S(1)} %pad_maximum_fusion.2), channel_id=1, source_target_pairs={{0,64},{4,68},{8,72},{12,76},{16,80},{20,84},{24,88},{28,92},{32,9... | collective-permute-start | bytes 24584 | tf_op jit(solution)/shard_map/ppermute | solution.py:886
  81.6 2.0 %collective-permute-done.18 = f32[2,8,128]{2,1,0:T(8,128)S(1)} collective-permute-done((f32[2,8,128]{2,1,0:T(8,128)S(1)}, f32[2,8,128]{2,1,0:T(8,128)S(1)}, u32[]{:S(2)}, u32[]{:S(2)}) %collective-permute-start.18) | collective-permute-done | bytes 8224 | tf_op jit(solution)/shard_map/ppermute | solution.py:886
  83.7 5.8 %collective-permute-done.21.g_far = f32[2,76,8,128]{3,2,1,0:T(8,128)S(1)} collective-permute-done((f32[2,76,8,128]{3,2,1,0:T(8,128)S(1)}, f32[2,76,8,128]{3,2,1,0:T(8,128)S(1)}, u32[]{:S(2)}, u32[]{:S(2)}) %collective-permute-start.21) | collective-permute-done | bytes 622624 | tf_op jit(solution)/shard_map/ppermute | solution.py:847
  89.5 0.8 shard_map.122
  90.5 3.7 %collective-permute-start.24 = (f32[6,3,8,128]{3,2,1,0:T(8,128)S(1)}, f32[6,3,8,128]{3,2,1,0:T(8,128)S(1)}, u32[]{:S(2)}, u32[]{:S(2)}) collective-permute-start(f32[6,3,8,128]{3,2,1,0:T(8,128)S(1)} %get-tuple-element.115), channel_id=1, source_target_pairs={{0,1},{1,0},{2,3},{3,2},{4,5},{5,4},{6,7},{7,6},{8,9},{9,8},{10,11... | collective-permute-start | bytes 221192 | tf_op jit(solution)/shard_map/ppermute | solution.py:843
  94.2 1.9 %collective-permute-start.25 = (f32[6,3,8,128]{3,2,1,0:T(8,128)S(1)}, f32[6,3,8,128]{3,2,1,0:T(8,128)S(1)}, u32[]{:S(2)}, u32[]{:S(2)}) collective-permute-start(f32[6,3,8,128]{3,2,1,0:T(8,128)S(1)} %get-tuple-element.115), channel_id=1, source_target_pairs={{0,3},{1,2},{2,1},{3,0},{4,7},{5,6},{6,5},{7,4},{8,11},{9,10},{10,... | collective-permute-start | bytes 221192 | tf_op jit(solution)/shard_map/ppermute | solution.py:851
  96.1 2.8 %collective-permute-start.26 = (f32[6,3,8,128]{3,2,1,0:T(8,128)S(1)}, f32[6,3,8,128]{3,2,1,0:T(8,128)S(1)}, u32[]{:S(2)}, u32[]{:S(2)}) collective-permute-start(f32[6,3,8,128]{3,2,1,0:T(8,128)S(1)} %get-tuple-element.116), channel_id=1, source_target_pairs={{1,4},{4,1},{3,6},{6,3},{5,8},{8,5},{7,10},{10,7},{9,12},{12,9},{1... | collective-permute-start | bytes 221192 | tf_op jit(solution)/shard_map/ppermute | solution.py:861
  98.9 3.0 %collective-permute-start.27 = (f32[6,3,8,128]{3,2,1,0:T(8,128)S(1)}, f32[6,3,8,128]{3,2,1,0:T(8,128)S(1)}, u32[]{:S(2)}, u32[]{:S(2)}) collective-permute-start(f32[6,3,8,128]{3,2,1,0:T(8,128)S(1)} %get-tuple-element.116), channel_id=1, source_target_pairs={{1,6},{6,1},{3,4},{4,3},{5,10},{10,5},{7,8},{8,7},{9,14},{14,9},{1... | collective-permute-start | bytes 221192 | tf_op jit(solution)/shard_map/ppermute | solution.py:861
  101.9 2.7 %shard_map.124 = (f32[38,24,8,128]{3,2,1,0:T(8,128)S(1)}, f32[36,24,8,128]{3,2,1,0:T(8,128)S(1)}, f32[37,24,8,128]{3,2,1,0:T(8,128)S(1)}, f32[36,24,8,128]{3,2,1...) custom-call(f32[38,24,8,128]{3,2,1,0:T(8,128)S(1)} %get-tuple-elemen, ...), custom_call_target="tpu_custom_call", output_to_operand_aliasing={{0}: (0, {}), {1}: (1, {}), {2}: (2, {}), {3}: (3, {}), {4}... | custom-call | bytes 13600000 | tf_op jit(solution)/shard_map/pallas_call | solution.py:58
  104.6 0.7 collective-permute-done.25.p_core_far
  105.7 0.9 collective-permute-done.27.p_tile_far
  106.5 13.3 %shard_map.125 = (f32[16,16,8,128]{3,2,1,0:T(8,128)S(1)}, f32[16,16,8,128]{3,2,1,0:T(8,128)S(1)}, f32[6,16,8,128]{3,2,1,0:T(8,128)S(1)}) custom-call(f32[12,64]{1,0:T(8,128)S(1)} %bitcast.46, f32[12,64]{1,0:T(8,128)S(1)} %copy-done, f32[6,16,8,128]{3,2,1,0:T(8,128)S(1)} %get-tuple-element.114.power, f32[6,16,8,128]{3,2,1,0:T(8,128)S(1)} %collective-permute-done.23.p_far, ...), custom_call_target="tpu_custom_call" | custom-call | bytes 47600000 | tf_op jit(solution)/shard_map/pallas_call | solution.py:58
  119.8 4.5 %collective-permute-start.28 = (f32[16,16,8,128]{3,2,1,0:T(8,128)S(1)}, f32[16,16,8,128]{3,2,1,0:T(8,128)S(1)}, u32[]{:S(2)}, u32[]{:S(2)}) collective-permute-start(f32[16,16,8,128]{3,2,1,0:T(8,128)S(1)} %get-tuple-element.130.s_out), channel_id=1, source_target_pairs={{0,1},{1,0},{2,3},{3,2},{4,5},{5,4},{6,7},{7,6},{8,9},{9,8},{10,11... | collective-permute-start | bytes 3145736 | tf_op jit(solution)/shard_map/ppermute | solution.py:843
  124.3 1.2 collective-permute-start.29
  125.9 1.7 %shard_map.127.final = f32[6,16,8,128]{3,2,1,0:T(8,128)S(1)} custom-call(f32[12,64]{1,0:T(8,128)S(1)} %copy-done, f32[16,16,8,128]{3,2,1,0:T(8,128)S(1)} %get-tuple-element.129.own.out, f32[16,16,8,128]{3,2,1,0:T(8,128)S(1)} %get-tuple-element.130.s_out), custom_call_target="tpu_custom_call" | custom-call | bytes 4760000 | tf_op jit(solution)/shard_map/pallas_call | solution.py:58
  127.6 1.7 %shard_map.126 = f32[16,4,64,128]{3,2,1,0:T(8,128)} custom-call(f32[16,16,8,128]{3,2,1,0:T(8,128)S(1)} %get-tuple-element.129.own.out, f32[16,16,8,128]{3,2,1,0:T(8,128)S(1)} %collective-permute-done.28.got), custom_call_target="tpu_custom_call" | custom-call | bytes 5440000 | tf_op jit(solution)/shard_map/pallas_call | solution.py:58
  129.2 7.3 %collective-permute-done.29.got = f32[6,16,8,128]{3,2,1,0:T(8,128)S(1)} collective-permute-done((f32[6,16,8,128]{3,2,1,0:T(8,128)S(1)}, f32[6,16,8,128]{3,2,1,0:T(8,128)S(1)}, u32[]{:S(2)}, u32[]{:S(2)}) %collective-permute-start.29) | collective-permute-done | bytes 393248 | tf_op jit(solution)/shard_map/ppermute | solution.py:847
  136.7 1.0 collective-permute-start.30
  137.6 0.8 shard_map.123
  138.7 0.8 shard_map.129
  (48 shorter events, 5.1 us)
Async XLA Ops:
  0.6 5.1 %copy-start = (f32[12,64]{1,0:T(8,128)S(1)}, f32[12,64]{1,0:T(8,128)}, u32[]{:S(2)}) copy-start(f32[12,64]{1,0:T(8,128)} %weights.5) | copy-start | bytes 9220
  2.7 3.0 %collective-permute-start = (f32[16,16,8,128]{3,2,1,0:T(8,128)S(1)}, f32[16,16,8,128]{3,2,1,0:T(8,128)S(1)}, u32[]{:S(2)}, u32[]{:S(2)}) collective-permute-start(f32[16,16,8,128]{3,2,1,0:T(8,128)S(1)} %get-tuple-element.70), channel_id=1, source_target_pairs={{0,1},{1,0},{2,3},{3,2},{4,5},{5,4},{6,7},{7,6},{8,9},{9,8},{10,11... | collective-permute-start | bytes 3145736 | tf_op jit(solution)/shard_map/ppermute | solution.py:843
  3.9 4.9 %collective-permute-start.1 = (f32[12,16,8,128]{3,2,1,0:T(8,128)S(1)}, f32[12,16,8,128]{3,2,1,0:T(8,128)S(1)}, u32[]{:S(2)}, u32[]{:S(2)}) collective-permute-start(f32[12,16,8,128]{3,2,1,0:T(8,128)S(1)} %get-tuple-element.77), channel_id=1, source_target_pairs={{0,1},{1,0},{2,3},{3,2},{4,5},{5,4},{6,7},{7,6},{8,9},{9,8},{10,11... | collective-permute-start | bytes 2359304 | tf_op jit(solution)/shard_map/ppermute | solution.py:843
  9.1 26.4 %collective-permute-start.2 = (f32[9,16,8,128]{3,2,1,0:T(8,128)S(1)}, f32[9,16,8,128]{3,2,1,0:T(8,128)S(1)}, u32[]{:S(2)}, u32[]{:S(2)}) collective-permute-start(f32[9,16,8,128]{3,2,1,0:T(8,128)S(1)} %get-tuple-element.79), channel_id=1, source_target_pairs={{0,2},{1,3},{2,0},{3,1},{4,6},{5,7},{6,4},{7,5},{8,10},{9,11},{10,... | collective-permute-start | bytes 1769480 | tf_op jit(solution)/shard_map/ppermute | solution.py:847
  11.9 23.6 %collective-permute-start.5 = (f32[31,3,8,128]{3,2,1,0:T(8,128)S(1)}, f32[31,3,8,128]{3,2,1,0:T(8,128)S(1)}, u32[]{:S(2)}, u32[]{:S(2)}) collective-permute-start(f32[31,3,8,128]{3,2,1,0:T(8,128)S(1)} %get-tuple-element.82), channel_id=1, source_target_pairs={{0,1},{1,0},{2,3},{3,2},{4,5},{5,4},{6,7},{7,6},{8,9},{9,8},{10,11... | collective-permute-start | bytes 1142792 | tf_op jit(solution)/shard_map/ppermute | solution.py:843
  12.5 22.9 %collective-permute-start.6 = (f32[81,8,128]{2,1,0:T(8,128)S(1)}, f32[81,8,128]{2,1,0:T(8,128)S(1)}, u32[]{:S(2)}, u32[]{:S(2)}) collective-permute-start(f32[81,8,128]{2,1,0:T(8,128)S(1)} %get-tuple-element.83), channel_id=1, source_target_pairs={{1,4},{4,1},{3,6},{6,3},{5,8},{8,5},{7,10},{10,7},{9,12},{12,9},{1... | collective-permute-start | bytes 995336 | tf_op jit(solution)/shard_map/ppermute | solution.py:861
  14.7 20.8 %collective-permute-start.3 = (f32[9,3,8,128]{3,2,1,0:T(8,128)S(1)}, f32[9,3,8,128]{3,2,1,0:T(8,128)S(1)}, u32[]{:S(2)}, u32[]{:S(2)}) collective-permute-start(f32[9,3,8,128]{3,2,1,0:T(8,128)S(1)} %get-tuple-element.80), channel_id=1, source_target_pairs={{0,3},{1,2},{2,1},{3,0},{4,7},{5,6},{6,5},{7,4},{8,11},{9,10},{10,... | collective-permute-start | bytes 331784 | tf_op jit(solution)/shard_map/ppermute | solution.py:851
  20.5 15.0 %collective-permute-start.4 = (f32[9,3,8,128]{3,2,1,0:T(8,128)S(1)}, f32[9,3,8,128]{3,2,1,0:T(8,128)S(1)}, u32[]{:S(2)}, u32[]{:S(2)}) collective-permute-start(f32[9,3,8,128]{3,2,1,0:T(8,128)S(1)} %get-tuple-element.81), channel_id=1, source_target_pairs={{1,6},{6,1},{3,4},{4,3},{5,10},{10,5},{7,8},{8,7},{9,14},{14,9},{1... | collective-permute-start | bytes 331784 | tf_op jit(solution)/shard_map/ppermute | solution.py:861
  37.4 3.4 %collective-permute-start.7 = (f32[16,16,8,128]{3,2,1,0:T(8,128)S(1)}, f32[16,16,8,128]{3,2,1,0:T(8,128)S(1)}, u32[]{:S(2)}, u32[]{:S(2)}) collective-permute-start(f32[16,16,8,128]{3,2,1,0:T(8,128)S(1)} %get-tuple-element.89), channel_id=1, source_target_pairs={{0,1},{1,0},{2,3},{3,2},{4,5},{5,4},{6,7},{7,6},{8,9},{9,8},{10,11... | collective-permute-start | bytes 3145736 | tf_op jit(solution)/shard_map/ppermute | solution.py:843
  38.5 6.9 %collective-permute-start.8 = (f32[2,18,8,128]{3,2,1,0:T(8,128)S(1)}, f32[2,18,8,128]{3,2,1,0:T(8,128)S(1)}, u32[]{:S(2)}, u32[]{:S(2)}) collective-permute-start(f32[2,18,8,128]{3,2,1,0:T(8,128)S(1)} %get-tuple-element.88), channel_id=1, source_target_pairs={{0,2},{1,3},{2,0},{3,1},{4,6},{5,7},{6,4},{7,5},{8,10},{9,11},{10,... | collective-permute-start | bytes 442376 | tf_op jit(solution)/shard_map/ppermute | solution.py:847
  40.9 28.4 %collective-permute-start.13 = (f32[2,32,4,8,128]{4,3,2,1,0:T(8,128)S(1)}, f32[2,32,4,8,128]{4,3,2,1,0:T(8,128)S(1)}, u32[]{:S(2)}, u32[]{:S(2)}) collective-permute-start(f32[2,32,4,8,128]{4,3,2,1,0:T(8,128)S(1)} %get-tuple-element.99), channel_id=1, source_target_pairs={{0,1},{1,0},{2,3},{3,2},{4,5},{5,4},{6,7},{7,6},{8,9},{9,8},{10,11... | collective-permute-start | bytes 3145736 | tf_op jit(solution)/shard_map/ppermute | solution.py:843
  41.4 28.0 %collective-permute-start.14 = (f32[2,32,4,8,128]{4,3,2,1,0:T(8,128)S(1)}, f32[2,32,4,8,128]{4,3,2,1,0:T(8,128)S(1)}, u32[]{:S(2)}, u32[]{:S(2)}) collective-permute-start(f32[2,32,4,8,128]{4,3,2,1,0:T(8,128)S(1)} %get-tuple-element.90), channel_id=1, source_target_pairs={{1,4},{4,1},{3,6},{6,3},{5,8},{8,5},{7,10},{10,7},{9,12},{12,9},{1... | collective-permute-start | bytes 3145736 | tf_op jit(solution)/shard_map/ppermute | solution.py:861
  46.3 3.0 %collective-permute-start.9 = (f32[2,8,128]{2,1,0:T(8,128)S(1)}, f32[2,8,128]{2,1,0:T(8,128)S(1)}, u32[]{:S(2)}, u32[]{:S(2)}) collective-permute-start(f32[2,8,128]{2,1,0:T(8,128)S(1)} %get-tuple-element.98), channel_id=1, source_target_pairs={{0,1},{1,0},{2,3},{3,2},{4,5},{5,4},{6,7},{7,6},{8,9},{9,8},{10,11... | collective-permute-start | bytes 24584 | tf_op jit(solution)/shard_map/ppermute | solution.py:843
  49.2 20.0 %collective-permute-start.12 = (f32[2,8,128]{2,1,0:T(8,128)S(1)}, f32[2,8,128]{2,1,0:T(8,128)S(1)}, u32[]{:S(2)}, u32[]{:S(2)}) collective-permute-start(f32[2,8,128]{2,1,0:T(8,128)S(1)} %pad_maximum_fusion), channel_id=1, source_target_pairs={{0,4},{1,5},{2,6},{3,7},{4,0},{5,1},{6,2},{7,3},{8,12},{9,13},{10,... | collective-permute-start | bytes 24584 | tf_op jit(solution)/shard_map/ppermute | solution.py:878
  49.3 19.9 %collective-permute-start.11 = (f32[2,8,128]{2,1,0:T(8,128)S(1)}, f32[2,8,128]{2,1,0:T(8,128)S(1)}, u32[]{:S(2)}, u32[]{:S(2)}) collective-permute-start(f32[2,8,128]{2,1,0:T(8,128)S(1)} %pad_maximum_fusion), channel_id=1, source_target_pairs={{0,6},{1,7},{2,4},{3,5},{4,2},{5,3},{6,0},{7,1},{8,14},{9,15},{10,... | collective-permute-start | bytes 24584 | tf_op jit(solution)/shard_map/ppermute | solution.py:878
  52.1 17.2 %collective-permute-start.10 = (f32[2,8,128]{2,1,0:T(8,128)S(1)}, f32[2,8,128]{2,1,0:T(8,128)S(1)}, u32[]{:S(2)}, u32[]{:S(2)}) collective-permute-start(f32[2,8,128]{2,1,0:T(8,128)S(1)} %pad_maximum_fusion), channel_id=1, source_target_pairs={{0,2},{1,3},{2,0},{3,1},{4,6},{5,7},{6,4},{7,5},{8,10},{9,11},{10,... | collective-permute-start | bytes 24584 | tf_op jit(solution)/shard_map/ppermute | solution.py:878
  69.4 5.7 %collective-permute-start.16 = (f32[2,8,128]{2,1,0:T(8,128)S(1)}, f32[2,8,128]{2,1,0:T(8,128)S(1)}, u32[]{:S(2)}, u32[]{:S(2)}) collective-permute-start(f32[2,8,128]{2,1,0:T(8,128)S(1)} %pad_maximum_fusion.1), channel_id=1, source_target_pairs={{0,8},{4,12},{8,0},{12,4},{16,24},{20,28},{24,16},{28,20},{32,40},... | collective-permute-start | bytes 24584 | tf_op jit(solution)/shard_map/ppermute | solution.py:886
  71.7 4.0 %collective-permute-start.15 = (f32[2,8,128]{2,1,0:T(8,128)S(1)}, f32[2,8,128]{2,1,0:T(8,128)S(1)}, u32[]{:S(2)}, u32[]{:S(2)}) collective-permute-start(f32[2,8,128]{2,1,0:T(8,128)S(1)} %pad_maximum_fusion.1), channel_id=1, source_target_pairs={{0,16},{4,20},{8,24},{12,28},{16,0},{20,4},{24,8},{28,12},{32,48},... | collective-permute-start | bytes 24584 | tf_op jit(solution)/shard_map/ppermute | solution.py:886
  73.8 3.7 %collective-permute-start.17 = (f32[2,8,128]{2,1,0:T(8,128)S(1)}, f32[2,8,128]{2,1,0:T(8,128)S(1)}, u32[]{:S(2)}, u32[]{:S(2)}) collective-permute-start(f32[2,8,128]{2,1,0:T(8,128)S(1)} %pad_maximum_fusion.1), channel_id=1, source_target_pairs={{0,24},{4,28},{8,16},{12,20},{16,8},{20,12},{24,0},{28,4},{32,56},... | collective-permute-start | bytes 24584 | tf_op jit(solution)/shard_map/ppermute | solution.py:886
  74.1 15.3 %collective-permute-start.21 = (f32[2,76,8,128]{3,2,1,0:T(8,128)S(1)}, f32[2,76,8,128]{3,2,1,0:T(8,128)S(1)}, u32[]{:S(2)}, u32[]{:S(2)}) collective-permute-start(f32[2,76,8,128]{3,2,1,0:T(8,128)S(1)} %shard_map.120), channel_id=1, source_target_pairs={{0,2},{1,3},{2,0},{3,1},{4,6},{5,7},{6,4},{7,5},{8,10},{9,11},{10,... | collective-permute-start | bytes 1867784 | tf_op jit(solution)/shard_map/ppermute | solution.py:847
  77.5 4.1 %collective-permute-start.20 = (f32[2,8,128]{2,1,0:T(8,128)S(1)}, f32[2,8,128]{2,1,0:T(8,128)S(1)}, u32[]{:S(2)}, u32[]{:S(2)}) collective-permute-start(f32[2,8,128]{2,1,0:T(8,128)S(1)} %pad_maximum_fusion.2), channel_id=1, source_target_pairs={{0,96},{4,100},{8,104},{12,108},{16,112},{20,116},{24,120},{28,124... | collective-permute-start | bytes 24584 | tf_op jit(solution)/shard_map/ppermute | solution.py:886
  78.6 3.0 %collective-permute-start.19 = (f32[2,8,128]{2,1,0:T(8,128)S(1)}, f32[2,8,128]{2,1,0:T(8,128)S(1)}, u32[]{:S(2)}, u32[]{:S(2)}) collective-permute-start(f32[2,8,128]{2,1,0:T(8,128)S(1)} %pad_maximum_fusion.2), channel_id=1, source_target_pairs={{0,32},{4,36},{8,40},{12,44},{16,48},{20,52},{24,56},{28,60},{32,0... | collective-permute-start | bytes 24584 | tf_op jit(solution)/shard_map/ppermute | solution.py:886
  79.3 4.3 %collective-permute-start.18 = (f32[2,8,128]{2,1,0:T(8,128)S(1)}, f32[2,8,128]{2,1,0:T(8,128)S(1)}, u32[]{:S(2)}, u32[]{:S(2)}) collective-permute-start(f32[2,8,128]{2,1,0:T(8,128)S(1)} %pad_maximum_fusion.2), channel_id=1, source_target_pairs={{0,64},{4,68},{8,72},{12,76},{16,80},{20,84},{24,88},{28,92},{32,9... | collective-permute-start | bytes 24584 | tf_op jit(solution)/shard_map/ppermute | solution.py:886
  90.3 16.3 %collective-permute-start.23 = (f32[6,16,8,128]{3,2,1,0:T(8,128)S(1)}, f32[6,16,8,128]{3,2,1,0:T(8,128)S(1)}, u32[]{:S(2)}, u32[]{:S(2)}) collective-permute-start(f32[6,16,8,128]{3,2,1,0:T(8,128)S(1)} %get-tuple-element.114.power), channel_id=1, source_target_pairs={{0,2},{1,3},{2,0},{3,1},{4,6},{5,7},{6,4},{7,5},{8,10},{9,11},{10,... | collective-permute-start | bytes 1179656 | tf_op jit(solution)/shard_map/ppermute | solution.py:847
  90.5 14.1 %collective-permute-start.24 = (f32[6,3,8,128]{3,2,1,0:T(8,128)S(1)}, f32[6,3,8,128]{3,2,1,0:T(8,128)S(1)}, u32[]{:S(2)}, u32[]{:S(2)}) collective-permute-start(f32[6,3,8,128]{3,2,1,0:T(8,128)S(1)} %get-tuple-element.115), channel_id=1, source_target_pairs={{0,1},{1,0},{2,3},{3,2},{4,5},{5,4},{6,7},{7,6},{8,9},{9,8},{10,11... | collective-permute-start | bytes 221192 | tf_op jit(solution)/shard_map/ppermute | solution.py:843
  94.2 11.1 %collective-permute-start.25 = (f32[6,3,8,128]{3,2,1,0:T(8,128)S(1)}, f32[6,3,8,128]{3,2,1,0:T(8,128)S(1)}, u32[]{:S(2)}, u32[]{:S(2)}) collective-permute-start(f32[6,3,8,128]{3,2,1,0:T(8,128)S(1)} %get-tuple-element.115), channel_id=1, source_target_pairs={{0,3},{1,2},{2,1},{3,0},{4,7},{5,6},{6,5},{7,4},{8,11},{9,10},{10,... | collective-permute-start | bytes 221192 | tf_op jit(solution)/shard_map/ppermute | solution.py:851
  96.1 10.4 %copy-start.1 = (f32[64,12]{0,1:T(8,128)S(1)}, f32[64,12]{0,1:T(8,128)}, u32[]{:S(2)}) copy-start(f32[64,12]{0,1:T(8,128)} %param.16) | copy-start | bytes 9220
  96.1 9.5 %collective-permute-start.26 = (f32[6,3,8,128]{3,2,1,0:T(8,128)S(1)}, f32[6,3,8,128]{3,2,1,0:T(8,128)S(1)}, u32[]{:S(2)}, u32[]{:S(2)}) collective-permute-start(f32[6,3,8,128]{3,2,1,0:T(8,128)S(1)} %get-tuple-element.116), channel_id=1, source_target_pairs={{1,4},{4,1},{3,6},{6,3},{5,8},{8,5},{7,10},{10,7},{9,12},{12,9},{1... | collective-permute-start | bytes 221192 | tf_op jit(solution)/shard_map/ppermute | solution.py:861
  98.9 7.6 %collective-permute-start.27 = (f32[6,3,8,128]{3,2,1,0:T(8,128)S(1)}, f32[6,3,8,128]{3,2,1,0:T(8,128)S(1)}, u32[]{:S(2)}, u32[]{:S(2)}) collective-permute-start(f32[6,3,8,128]{3,2,1,0:T(8,128)S(1)} %get-tuple-element.116), channel_id=1, source_target_pairs={{1,6},{6,1},{3,4},{4,3},{5,10},{10,5},{7,8},{8,7},{9,14},{14,9},{1... | collective-permute-start | bytes 221192 | tf_op jit(solution)/shard_map/ppermute | solution.py:861
  119.8 7.7 %collective-permute-start.28 = (f32[16,16,8,128]{3,2,1,0:T(8,128)S(1)}, f32[16,16,8,128]{3,2,1,0:T(8,128)S(1)}, u32[]{:S(2)}, u32[]{:S(2)}) collective-permute-start(f32[16,16,8,128]{3,2,1,0:T(8,128)S(1)} %get-tuple-element.130.s_out), channel_id=1, source_target_pairs={{0,1},{1,0},{2,3},{3,2},{4,5},{5,4},{6,7},{7,6},{8,9},{9,8},{10,11... | collective-permute-start | bytes 3145736 | tf_op jit(solution)/shard_map/ppermute | solution.py:843
  124.3 12.2 %collective-permute-start.29 = (f32[6,16,8,128]{3,2,1,0:T(8,128)S(1)}, f32[6,16,8,128]{3,2,1,0:T(8,128)S(1)}, u32[]{:S(2)}, u32[]{:S(2)}) collective-permute-start(f32[6,16,8,128]{3,2,1,0:T(8,128)S(1)} %get-tuple-element.131), channel_id=1, source_target_pairs={{0,2},{1,3},{2,0},{3,1},{4,6},{5,7},{6,4},{7,5},{8,10},{9,11},{10,... | collective-permute-start | bytes 1179656 | tf_op jit(solution)/shard_map/ppermute | solution.py:847
  125.5 12.1 %collective-permute-start.22 = (f32[3,16,8,128]{3,2,1,0:T(8,128)S(1)}, f32[3,16,8,128]{3,2,1,0:T(8,128)S(1)}, u32[]{:S(2)}, u32[]{:S(2)}) collective-permute-start(f32[3,16,8,128]{3,2,1,0:T(8,128)S(1)} %get-tuple-element.113), channel_id=1, source_target_pairs={{0,1},{1,0},{2,3},{3,2},{4,5},{5,4},{6,7},{7,6},{8,9},{9,8},{10,11... | collective-permute-start | bytes 589832 | tf_op jit(solution)/shard_map/ppermute | solution.py:843
  136.7 2.0 %collective-permute-start.30 = (f32[3,16,8,128]{3,2,1,0:T(8,128)S(1)}, f32[3,16,8,128]{3,2,1,0:T(8,128)S(1)}, u32[]{:S(2)}, u32[]{:S(2)}) collective-permute-start(f32[3,16,8,128]{3,2,1,0:T(8,128)S(1)} %get-tuple-element.134), channel_id=1, source_target_pairs={{0,1},{1,0},{2,3},{3,2},{4,5},{5,4},{6,7},{7,6},{8,9},{9,8},{10,11... | collective-permute-start | bytes 589832 | tf_op jit(solution)/shard_map/ppermute | solution.py:843
